TPU v7x, 32 devices: a whole 2x2x4 slice. The times are simulated.
32 devices in a mesh: row: 8 (over y, x, core), col: 4 (over z).
Axes of the slice: x: 2, y: 2, z: 4, core: 2. Of those that a mesh axis runs over, the one named last changes fastest.
Arguments:
- x_blocks: bfloat16 [128, 8, 2, 128, 128], P('row', 'col'), may hold values from -1.796875 to 1.796875
- x_columns: int32 [128, 8, 2], P('row', 'col'), may hold values from 0 to 95, as said below
- kept_columns: int32 [768, 8], P('row', 'col'), may hold values from 0 to 191, as said below
Outputs:
- result_blocks: float32 [768, 8, 128, 128], P('row', 'col')
Inputs may be any that keep to these rules, and one draw needn't show every extreme that they name: `x_columns`: the 2 entries of one block row and one group are distinct. `kept_columns`: the 2 entries of one result block row within one column panel are distinct.
All inputs are finite; a program needn't handle non-finite values.
Results may differ from a plain program's by a relative error of at most 0.0003.
Values may be sent and summed in bfloat16 or wider, within the bound.
No kernel may reach another device: no remote copies, remote signals or barrier semaphores. Data moves between devices by JAX's collectives and lax.ppermute only.
A program may use at most 320 MiB of HBM per device.

v0:
```python
import jax
import jax.numpy as jnp
from jax import lax
from jax.sharding import PartitionSpec as P


def block_products(a_values, a_cols, b_values, b_cols, kept_columns):
    row_count = a_values.shape[0]
    block_size = a_values.shape[-1]
    width_g = kept_columns.shape[0]
    slots_b = b_values.shape[1] * b_values.shape[2]
    panel_pos = (lax.broadcasted_iota(jnp.int32, b_cols.shape, 1) * width_g + b_cols).reshape(
        row_count, slots_b
    )
    b_flat = b_values.reshape(row_count, slots_b, block_size, block_size)
    onehot = a_cols[:, :, None] == lax.broadcasted_iota(jnp.int32, (1, 1, width_g), 2)
    kept_here = jnp.sum(jnp.where(onehot[:, :, :, None], kept_columns[None, None, :, :], 0), axis=2)
    selector = (kept_here[:, :, :, None] == panel_pos[:, None, None, :]).astype(jnp.bfloat16)
    chosen = jnp.einsum(
        "kesf,kftj->kestj", selector, b_flat, preferred_element_type=jnp.float32
    ).astype(jnp.bfloat16)
    return jnp.einsum("keti,kestj->kesij", a_values, chosen, preferred_element_type=jnp.float32)


def reduce_rows(products, a_cols, width_g):
    pair_count = a_cols.shape[0] * a_cols.shape[1]
    kept_count = products.shape[-3]
    block_size = products.shape[-1]
    targets = a_cols.reshape(pair_count)
    flat = products.reshape(pair_count, kept_count, block_size, block_size)
    zero_sums = jnp.zeros((width_g, kept_count, block_size, block_size), jnp.float32)
    return zero_sums.at[targets].add(flat)


def on_device(x_blocks, x_columns, kept_columns):
    rows_here = x_blocks.shape[0]
    slot_count = x_blocks.shape[2]
    block_size = x_blocks.shape[-1]
    width_g = kept_columns.shape[0]
    n_row = lax.axis_size("row")
    n_col = lax.axis_size("col")
    col_tags = x_columns.astype(jnp.bfloat16)
    relaid = (
        lax.all_to_all(x_blocks, "col", split_axis=0, concat_axis=1, tiled=True),
        lax.all_to_all(col_tags, "col", split_axis=0, concat_axis=1, tiled=True),
    )
    relaid = (
        lax.all_to_all(relaid[0], "row", split_axis=1, concat_axis=0, tiled=True),
        lax.all_to_all(relaid[1], "row", split_axis=1, concat_axis=0, tiled=True),
    )
    gathered = (
        lax.all_gather(relaid[0][:, 0], "col", axis=0, tiled=True),
        lax.all_gather(relaid[1][:, 0], "col", axis=0, tiled=True),
    )
    sub_rows = rows_here // n_col
    a_values = gathered[0].reshape(n_col, n_row, sub_rows, slot_count, block_size, block_size)
    a_values = a_values.transpose(1, 0, 2, 3, 4, 5).reshape(
        n_row * rows_here, slot_count, block_size, block_size
    )
    a_cols = gathered[1].reshape(n_col, n_row, sub_rows, slot_count).transpose(1, 0, 2, 3)
    a_cols = a_cols.reshape(n_row * rows_here, slot_count).astype(jnp.int32)
    b_values = lax.all_gather(x_blocks, "row", axis=0, tiled=True)
    b_tags = lax.all_gather(col_tags, "row", axis=0, tiled=True)
    fresh = block_products(a_values, a_cols, b_values, b_tags.astype(jnp.int32), kept_columns)
    summed = reduce_rows(fresh, a_cols, width_g)
    return summed


def solution(mesh):
    placed = (P("row", "col", None, None, None), P("row", "col", None), P("row", "col"))
    return jax.shard_map(
        on_device,
        mesh=mesh,
        in_specs=placed,
        out_specs=P("row", "col", None, None),
        check_vma=False,
    )
```

profile of v0, /device:TPU:0, one launch (start us, length us, event | category | flops | bytes accessed | tf_op | source)
XLA Modules:
  0.0 528.8 jit_solution(2229137912944791746)
XLA Ops:
  6.5 0.0 copy-start
  6.5 0.0 copy-start.1
  6.5 0.0 all-gather.6.cloned.1.call-start
  6.5 54.6 %all_to_all.66 = bf16[16,2,2,128,128]{4,3,2,1,0:T(8,128)(2,1)S(1)} all-to-all(bf16[16,2,2,128,128]{4,3,2,1,0:T(8,128)(2,1)} %param.3), channel_id=1, replica_groups=mesh['row'=8,'col'=4] {'col'}, dimensions={0} | all-to-all | bytes 4194304 | tf_op jit(solution)/shard_map/all_to_all | solution.py:44
  61.2 0.2 copy.98
  61.4 0.2 copy.99
  61.7 30.2 %all_to_all.67 = bf16[4,8,2,128,128]{4,3,2,0,1:T(8,128)(2,1)} all-to-all(bf16[4,8,2,128,128]{4,3,2,0,1:T(8,128)(2,1)S(1)} %copy.99), channel_id=1, replica_groups=mesh['row'=8,'col'=4] {'row'}, dimensions={1} | all-to-all | bytes 4194304 | tf_op jit(solution)/shard_map/all_to_all | solution.py:48
  91.9 0.0 all-gather.6.cloned.1.call-update
  91.9 0.0 all-gather.4.cloned.1.call-start
  92.0 0.7 all-gather.4.cloned.1.call-update
  92.7 0.0 copy-done
  92.7 0.1 copy.86
  92.8 0.6 convert_element_type.41
  93.4 3.3 all-to-all-start
  96.7 8.4 %all_gather.13 = bf16[128,2,2]{2,1,0:T(2,128)(2,1)S(1)} all-gather(bf16[16,2,2]{2,1,0:T(2,128)(2,1)} %convert_element_type.41), channel_id=1, replica_groups=mesh['row'=8,'col'=4] {'row'}, dimensions={0}, use_global_device_ids=true | all-gather | bytes 1152 | tf_op jit(solution)/shard_map/all_gather | solution.py:63
  105.1 0.1 copy.95
  105.2 0.1 convert_add_fusion
  105.2 0.0 all-to-all-done
  105.2 0.1 copy.106
  105.4 0.6 copy.89
  106.0 3.3 all-to-all-start.1
  109.3 0.1 copy.96
  109.4 4.4 all-to-all-done.1
  113.8 0.1 copy.90
  113.9 0.1 copy.91
  114.0 0.1 reshape.72
  114.1 12.3 %all-gather = bf16[4,32,2]{1,2,0:T(2,128)(2,1)S(1)} all-gather(bf16[1,32,2]{1,2,0:T(2,128)(2,1)S(1)} %reshape.72), channel_id=1, replica_groups=mesh['row'=8,'col'=4] {'col'}, dimensions={0}, use_global_device_ids=true | all-gather | bytes 640 | tf_op jit(solution)/shard_map/all_gather | solution.py:53
  126.4 0.1 reshape.62
  126.5 0.3 copy.92
  126.8 0.1 reshape.61
  126.9 0.1 reshape.60
  127.1 0.0 copy-done.1
  127.1 0.1 select_reduce_fusion
  127.2 0.2 copy.94
  127.4 111.7 %all-gather.6.cloned.1.call-done = bf16[128,2,128,128]{3,2,1,0:T(8,128)(2,1)} async-done(((bf16[32,2,128,128]{3,2,1,0:T(8,128)(2,1)}), bf16[128,2,128,128]{3,2,1,0:T(8,128)(2,1)}) %all-gather.6.cloned.1.call-update) | async-done | bytes 8388624 | tf_op jit(solution)/shard_map/all_gather | solution.py:52
  239.1 11.3 %copy.100 = bf16[8,4,4,2,128,128]{5,4,3,2,1,0:T(8,128)(2,1)} copy(bf16[8,4,4,2,128,128]{5,4,3,2,0,1:T(8,128)(2,1)} %bitcast.55) | data formatting | bytes 16777216 | tf_op jit(solution)/shard_map/transpose | solution.py:57
  250.4 78.7 %all-gather.4.cloned.1.call-done = bf16[128,2,2,128,128]{4,3,2,1,0:T(8,128)(2,1)} async-done(((bf16[16,2,2,128,128]{4,3,2,1,0:T(8,128)(2,1)}), bf16[128,2,2,128,128]{4,3,2,1,0:T(8,128)(2,1)}) %all-gather.4.cloned.1.call-update) | async-done | bytes 16777232 | tf_op jit(solution)/shard_map/all_gather | solution.py:62
  329.1 30.7 %copy.97 = bf16[128,2,2,128,128]{4,2,1,3,0:T(2,128)(2,1)} copy(bf16[128,2,2,128,128]{4,3,2,1,0:T(8,128)(2,1)} %all-gather.4.cloned.1.call-done) | data formatting | bytes 33554432 | tf_op jit(solution)/shard_map/all_gather | solution.py:62
  359.8 26.8 %convolution_convert_fusion = bf16[128,2,2,128,128]{4,2,3,1,0:T(2,128)(2,1)} fusion(bf16[128,4,128,128,1]{3,1,2,4,0:T(4,128)(2,1)} %bitcast.54, s32[128,4]{1,0:T(8,128)S(1)} %copy.96, s32[128,2,2]{2,1,0:T(2,128)S(1)} %copy.94), kind=kOutput, calls=%fused_computation.1 | convolution fusion | flops 75499520 | bytes 33558528 | tf_op jit(solution)/shard_map/kesf,kftj->kestj/dot_general | solution.py:19
  386.6 20.1 %fusion = f32[128,2,2,128,128]{4,3,2,1,0:T(8,128)} fusion(bf16[128,2,128,128,1]{3,2,4,1,0:T(8,128)(2,1)} %bitcast.53, bf16[128,2,2,128,128]{4,2,3,1,0:T(2,128)(2,1)} %convolution_convert_fusion), kind=kOutput, calls=%fused_computation.2 | convolution fusion | flops 2147483648 | bytes 58720256 | tf_op jit(solution)/shard_map/keti,kestj->kesij/dot_general | solution.py:22
  406.8 33.4 %copy.102 = f32[256,2,128,128]{3,2,1,0:T(8,128)} copy(f32[256,2,128,128]{2,3,1,0:T(8,128)} %bitcast.52) | data formatting | bytes 67108864 | tf_op jit(solution)/shard_map/reshape | solution.py:30
  440.2 6.4 %broadcast_in_dim.28 = f32[96,2,128,128]{3,2,1,0:T(8,128)} broadcast(f32[]{:T(128)} %constant.3.clone.1), dimensions={} | broadcast | bytes 12582916 | tf_op jit(solution)/shard_map/broadcast_in_dim | solution.py:31
  446.6 75.4 %scatter_fusion = f32[96,2,128,128]{3,2,1,0:T(8,128)} fusion(f32[96,2,128,128]{3,2,1,0:T(8,128)} %broadcast_in_dim.28, s32[256]{0:T(256)S(1)} %bitcast.66, f32[256,2,128,128]{3,2,1,0:T(8,128)} %copy.102), kind=kCustom, calls=%fused_computation | custom fusion | flops 8388608 | bytes 100664320 | tf_op jit(solution)/shard_map/scatter-add | solution.py:32
  (6 shorter events, 0.1 us)
Async XLA Ops:
  6.5 86.2 %copy-start = (s32[16,2,2]{0,2,1:T(2,128)S(1)}, s32[16,2,2]{0,2,1:T(2,128)}, u32[]{:S(2)}) copy-start(s32[16,2,2]{0,2,1:T(2,128)} %param.4) | copy-start | bytes 772
  6.5 120.6 %copy-start.1 = (s32[96,2]{0,1:T(2,128)S(1)}, s32[96,2]{0,1:T(2,128)}, u32[]{:S(2)}) copy-start(s32[96,2]{0,1:T(2,128)} %param.5) | copy-start | bytes 2308
  6.5 232.6 %all-gather.6.cloned.1.call-start = ((), (), s32[]{:S(2)}) async-start(), calls=%async_computation.5 | async-start | bytes 10485760 | tf_op jit(solution)/shard_map/all_gather | solution.py:52
  91.9 237.2 %all-gather.4.cloned.1.call-start = ((), (), s32[]{:S(2)}) async-start(), calls=%async_computation.4 | async-start | bytes 18874368 | tf_op jit(solution)/shard_map/all_gather | solution.py:62
  93.4 11.8 %all-to-all-start = ((bf16[16,2,2]{2,1,0:T(2,128)(2,1)}), bf16[16,2,2]{2,1,0:T(2,128)(2,1)S(1)}, u32[]{:S(2)}, u32[]{:S(2)}) async-start(bf16[16,2,2]{2,1,0:T(2,128)(2,1)} %convert_element_type.41), calls=%async_computation | async-start | bytes 16384 | tf_op jit(solution)/shard_map/all_to_all | solution.py:45
  106.0 7.8 %all-to-all-start.1 = ((bf16[4,8,2]{0,2,1:T(2,128)(2,1)}), bf16[4,8,2]{0,2,1:T(2,128)(2,1)S(1)}, u32[]{:S(2)}, u32[]{:S(2)}) async-start(bf16[4,8,2]{0,2,1:T(2,128)(2,1)} %copy.89), calls=%async_computation.1 | async-start | bytes 8192 | tf_op jit(solution)/shard_map/all_to_all | solution.py:49
Sparse Core Ops, SparseCore 0:
  92.1 146.9 all-gather.5
  241.0 88.0 all-gather.3
where the time goes:
time: 530 us; the launch traced here: 529 us
  waiting for transfers between devices  195 us (37%)
  blocking collectives  106 us (20%)
  local copies, waits for them, and re-layouts  84.5 us (16%)
  other arithmetic  76.3 us (14%)
  matrix products  47 us (9%)
  between operations  13.5 us (3%)
  starting transfers between devices  6.61 us (1%)
    all_gather x1, waiting for transfers between devices, on_device(): lax.all_gather(relaid[0][:, 0], 'col', axis=0, tiled=True)  112 us
    all_gather x1, waiting for transfers between devices, on_device(): b_values = lax.all_gather(x_blocks, 'row', axis=0, tiled=True)  78.7 us
    scatter-add x1, other arithmetic, reduce_rows(): return zero_sums.at[targets].add(flat)  75.4 us
    all_to_all x1, blocking collectives, on_device(): lax.all_to_all(x_blocks, 'col', split_axis=0, concat_axis=1, tiled=True)  54.6 us
    reshape x1, local copies, waits for them, and re-layouts, reduce_rows(): flat = products.reshape(pair_count, kept_count, block_size, block_size)  33.4 us
    all_gather x1, local copies, waits for them, and re-layouts, on_device(): b_values = lax.all_gather(x_blocks, 'row', axis=0, tiled=True)  30.7 us
    all_to_all x1, blocking collectives, on_device(): lax.all_to_all(relaid[0], 'row', split_axis=1, concat_axis=0, tiled=True)  30.2 us
    dot_general x1, matrix products, block_products(): jnp.einsum('kesf,kftj->kestj', selector, b_flat, preferred_element_type=j...  26.8 us
  transfers between devices with their start and end apart: 4, of which 3 were waited for; matrix products, arithmetic and copies ran while one was open for 3% of the time, Pallas kernels for 0%

commit v1 on v0

v1 whole, which is shorter than its diff:
```python
import functools

import jax
import jax.numpy as jnp
from jax import lax
from jax.experimental import pallas as pl
from jax.experimental.pallas import tpu as pltpu
from jax.sharding import PartitionSpec as P

SHIFT = 16
UNROLL = 8


def product_kernel(code_ref, place_ref, *refs, cuts, source_count, slot_count, group_count, first):
    chip_count, panel_slots = source_count // group_count, group_count * slot_count
    row0, row_count, pieces = cuts[0], cuts[-1] - cuts[0], list(zip(cuts, cuts[1:]))
    a_refs = []
    for _ in pieces:
        a_refs.append(refs[:source_count])
        refs = refs[source_count:]
    b_refs, refs = (refs[:source_count], refs[source_count : 2 * source_count]), refs[2 * source_count :]
    if not first:
        before_ref, refs = refs[0], refs[1:]
    out_ref, blocks, total, list_a, list_b, list_o, touched, seen, a_sem, b_sem, out_sem = refs
    own, group, panel = place_ref[0], place_ref[1], place_ref[2]
    a_size, b_size = row_count * slot_count, row_count * panel_slots
    b_base = source_count * a_size

    def a_part(source):
        return blocks.at[pl.ds(source * a_size, a_size)]

    def start_a(source):
        chip, side = source // group_count, source % group_count
        for piece, (i, j) in enumerate(pieces):
            at = source * a_size + (i - row0) * slot_count
            for row in range(j - i):
                held = a_refs[piece][side * chip_count + chip]
                held = held.at[panel] if len(held.shape) == 4 else held
                sent = held.at[pl.ds(row * panel_slots + group * slot_count, slot_count)]
                part = blocks.at[pl.ds(at + row * slot_count, slot_count)]
                pltpu.make_async_copy(sent, part, a_sem.at[source]).start()

    def wait_a(source):
        pltpu.make_async_copy(a_part(source), a_part(source), a_sem.at[source]).wait()

    half = b_refs[0][0].shape[0]
    b_start, b_end = row0 * panel_slots, (row0 + row_count) * panel_slots

    def b_copies(source):
        for at, (i, j) in enumerate(((b_start, min(b_end, half)), (max(b_start, half), b_end))):
            if i < j:
                sent = b_refs[at][source].at[pl.ds(i - at * half, j - i)]
                part = blocks.at[pl.ds(b_base + source * b_size + i - b_start, j - i)]
                yield pltpu.make_async_copy(sent, part, b_sem.at[at, source])

    def load(block):
        return pltpu.make_async_copy(before_ref.at[block], total.at[block], out_sem.at[block])

    def store(block):
        return pltpu.make_async_copy(total.at[block], out_ref.at[block], out_sem.at[block])

    for source in range(source_count):
        for copy in b_copies(source):
            copy.start()

    @pl.when(own == 0)
    def _():
        for source in range(source_count):
            start_a(source)

    block_total = out_ref.shape[0]
    keep_count = code_ref.shape[0] // (source_count * row_count * slot_count)
    if first:
        total[...] = jnp.zeros_like(total)
    else:

        def clear(block, carry):
            seen[block] = 0
            return carry

        lax.fori_loop(0, block_total, clear, 0)

    def note(at, counts):
        count, touched_count = counts
        row, slot = at // slot_count, at % slot_count
        kept_at = b_base + row * panel_slots + group * slot_count + slot
        a_at = jnp.where(own == 1, kept_at, at)
        for keep in range(keep_count):
            code = code_ref[at * keep_count + keep]
            block = lax.bitwise_and(code, (1 << SHIFT) - 1)
            list_a[count] = a_at
            list_b[count] = lax.shift_right_logical(code, SHIFT) + b_base
            list_o[count] = block
            count = count + (code >= 0).astype(jnp.int32)
            if not first:
                known = jnp.minimum(block, block_total - 1)
                fresh = jnp.logical_and(code >= 0, seen[known] == 0)
                touched[touched_count] = known

                @pl.when(fresh)
                def _():
                    seen[known] = 1
                    load(known).start()

                touched_count = touched_count + fresh.astype(jnp.int32)
        return count, touched_count

    count, touched_count = lax.fori_loop(
        0, source_count * row_count * slot_count, note, (jnp.int32(0), jnp.int32(0))
    )

    def each_touched(act):
        def step(at, carry):
            act(touched[at])
            return carry

        lax.fori_loop(0, touched_count, step, 0)

    for source in range(source_count):
        for copy in b_copies(source):
            copy.wait()

    @pl.when(own == 0)
    def _():
        for source in range(source_count):
            wait_a(source)

    if not first:
        each_touched(lambda block: load(block).wait())

    def product(at):
        a, b = blocks[list_a[at]], blocks[list_b[at]]
        return lax.dot_general(a, b, (((0,), (0,)), ((), ())), preferred_element_type=jnp.float32)

    def several(step, carry):
        at = step * UNROLL
        values = [product(at + k) for k in range(UNROLL)]
        for k in range(UNROLL):
            total[list_o[at + k]] += values[k]
        return carry

    for k in range(UNROLL):
        list_a[count + k] = b_base
        list_b[count + k] = b_base
        list_o[count + k] = block_total
    lax.fori_loop(0, (count + UNROLL - 1) // UNROLL, several, 0)
    if first:
        whole_store = pltpu.make_async_copy(total.at[pl.ds(0, block_total)], out_ref, out_sem.at[0])
        whole_store.start()
        whole_store.wait()
    else:
        each_touched(lambda block: store(block).start())
        each_touched(lambda block: store(block).wait())


def add_products(cuts, code, place, a_parts, b_parts, before, out_blocks, group_count, slot_count):
    source_count, block_size, row_count = len(b_parts) // 2, b_parts[0].shape[-1], cuts[-1] - cuts[0]
    pairs = code.shape[0]
    first = before is None
    anywhere = pl.BlockSpec(memory_space=pl.ANY)
    scalars = pl.BlockSpec(memory_space=pltpu.SMEM)
    operands = [code, place, *a_parts, *b_parts] + ([] if first else [before])
    block_count = source_count * row_count * (1 + group_count) * slot_count
    return pl.pallas_call(
        functools.partial(
            product_kernel,
            cuts=cuts,
            source_count=source_count,
            slot_count=slot_count,
            group_count=group_count,
            first=first,
        ),
        out_shape=jax.ShapeDtypeStruct((out_blocks, block_size, block_size), jnp.float32),
        in_specs=[scalars, scalars] + [anywhere] * (len(operands) - 2),
        out_specs=anywhere,
        scratch_shapes=[
            pltpu.VMEM((block_count, block_size, block_size), jnp.bfloat16),
            pltpu.VMEM((out_blocks + 1, block_size, block_size), jnp.float32),
            pltpu.SMEM((pairs + UNROLL,), jnp.int32),
            pltpu.SMEM((pairs + UNROLL,), jnp.int32),
            pltpu.SMEM((pairs + UNROLL,), jnp.int32),
            pltpu.SMEM((out_blocks + 1,), jnp.int32),
            pltpu.SMEM((out_blocks,), jnp.int32),
            pltpu.SemaphoreType.DMA((source_count,)),
            pltpu.SemaphoreType.DMA((2, source_count)),
            pltpu.SemaphoreType.DMA((out_blocks,)),
        ],
        input_output_aliases={} if first else {len(operands) - 1: 0},
        compiler_params=pltpu.CompilerParams(vmem_limit_bytes=52 << 20),
        cost_estimate=pl.CostEstimate(
            flops=2 * pairs * block_size**3,
            bytes_accessed=2 * block_count * block_size**2 + 8 * out_blocks * block_size**2,
            transcendentals=0,
        ),
    )(*operands)


def after(value, *others):
    return lax.optimization_barrier((value, *others))


def on_device(x_blocks, x_columns, kept_columns):
    rows_here, group_count, slot_count, block_size, _ = x_blocks.shape
    width_g, keep_count = kept_columns.shape
    n_row = lax.axis_size("row")
    n_col = lax.axis_size("col")
    row, col = lax.axis_index("row"), lax.axis_index("col")
    panel, group = row // group_count, row % group_count
    out_blocks = width_g * keep_count
    panel_slots = group_count * slot_count
    cuts = (0, rows_here * 8 // 16, rows_here * 13 // 16, rows_here)
    everyone = [(r, c) for r in range(n_row) for c in range(n_col)]

    def send(value, pairs):
        places = [(r * n_col + c, r2 * n_col + c2) for (r, c), (r2, c2) in pairs]
        return lax.ppermute(value, ("row", "col"), places)

    def to_row(value, offset, skip_panel=False):
        return send(
            value,
            [
                ((r, c), (r ^ offset, c))
                for r, c in everyone
                if not (skip_panel and (r ^ offset) // group_count == c)
            ],
        )

    x_flat = x_blocks.reshape(rows_here * panel_slots, block_size, block_size)
    first_part = x_flat[: cuts[1] * panel_slots]
    x_rest, first_part = after(x_flat, first_part)
    gathered = [lax.all_gather(first_part, "col")]
    for i, j in zip(cuts[1:], cuts[2:]):
        gathered.append(lax.all_gather(x_rest[i * panel_slots : j * panel_slots], "col"))
    tags = x_columns.reshape(rows_here, panel_slots).astype(jnp.bfloat16)
    tags = jnp.pad(tags, ((0, block_size - rows_here), (0, block_size - panel_slots)))
    half = rows_here * panel_slots // 2
    halves = [
        first_part if half == cuts[1] * panel_slots else x_flat[:half],
        jnp.concatenate([x_rest[half:], tags[None]]),
    ]

    chips = range(group_count, n_row, group_count)
    near = [offset for offset in chips if not (offset // group_count) & (offset // group_count - 1)]
    far = [offset for offset in chips if offset not in near]
    b_parts = [[part] + [None] * (n_row - 1) for part in halves]
    for at in range(2):
        for offset in near if at else near[::-1]:
            b_parts[at][offset] = to_row(halves[at], offset)
    for offset in sorted(far, key=lambda offset: bin(offset).count("1")):
        steps = [step for step in near if step & offset]
        for at, step in enumerate((steps[0], steps[-1])):
            b_parts[at][offset] = to_row(b_parts[at][offset ^ step], step)
    for at in range(2):
        for offset in (0, *near):
            for side in range(1, group_count):
                b_parts[at][offset + side] = to_row(b_parts[at][offset], side)
    there = [(at, offset) for at in range(2) for offset in range(n_row) if b_parts[at][offset] is not None]
    gathered[0], *arrived = after(gathered[0], *(b_parts[at][offset] for at, offset in there))
    for (at, offset), part in zip(there, arrived):
        b_parts[at][offset] = part
    for at in range(2):
        for offset in far:
            for side in range(1, group_count):
                b_parts[at][offset + side] = to_row(b_parts[at][offset], side)

    def pieces(q):
        return [
            lax.dynamic_index_in_dim(gathered[q], panel ^ (offset // group_count), 0, False) for offset in chips
        ]

    def in_plane(q, parts):
        return [gathered[q], *(to_row(part, offset, True) for offset, part in zip(chips, parts))]

    def own_swaps(q):
        own = lax.dynamic_index_in_dim(gathered[q], panel, 0, False)
        return [to_row(own, side) for side in range(1, group_count)]

    def cores(held, own_swapped):
        parts = list(held)
        for side in range(1, group_count):
            parts += [own_swapped[side - 1], *(to_row(h, side) for h in held[1:])]
        return parts

    held = in_plane(0, pieces(0))
    own_swapped = own_swaps(0)

    tag_parts = [part[-1, :rows_here, :panel_slots] for part in b_parts[1]]
    columns = jnp.stack(tag_parts).reshape(n_row, rows_here, group_count, slot_count)
    group_columns = lax.dynamic_index_in_dim(columns, group, 2, False)
    a_cols = group_columns
    for hop in range(1, n_col):
        pairs = [((r, r // group_count), (r, (r // group_count + hop) % n_col)) for r in range(n_row)]
        a_cols = jnp.where((col - panel) % n_col == hop, send(group_columns, pairs), a_cols)
    a_cols, *arrived = after(a_cols, *own_swapped, *held)
    own_swapped, held = arrived[: group_count - 1], arrived[group_count - 1 :]
    a_cols, b_cols = a_cols.astype(jnp.int32), columns.astype(jnp.int32)
    b_cols = b_cols + width_g * lax.broadcasted_iota(jnp.int32, columns.shape, 2)
    b_cols = b_cols.reshape(n_row, rows_here, panel_slots)
    onehot = a_cols[..., None] == jnp.arange(width_g, dtype=jnp.int32)
    wanted = jnp.sum(jnp.where(onehot[..., None], kept_columns, 0), axis=3)
    match = wanted[..., None] == b_cols[:, :, None, None, :]
    hit = jnp.max(jnp.where(match, jnp.arange(panel_slots, dtype=jnp.int32), -1), axis=-1)
    result = a_cols[..., None] * keep_count + jnp.arange(keep_count, dtype=jnp.int32)
    place = jnp.stack([(panel == col).astype(jnp.int32), group, panel]).astype(jnp.int32)
    codes = []
    for i, j in zip(cuts, cuts[1:]):
        rows_q = jnp.arange(n_row * (j - i), dtype=jnp.int32).reshape(n_row, j - i, 1, 1)
        code = (rows_q * panel_slots + hit[:, i:j]) * (1 << SHIFT) + result[:, i:j]
        codes.append(jnp.where(hit[:, i:j] >= 0, code, -1).reshape(-1))

    out, parts = None, pieces(1)
    for q in range(len(gathered)):
        a_parts = cores(held, own_swapped)
        if q + 1 < len(gathered):
            arrived = after(*parts, *held[1:])
            held[1:] = arrived[len(chips) :]
            coming = in_plane(q + 1, arrived[: len(chips)])
            own_swapped = own_swaps(q + 1)
        out = add_products(
            cuts[q : q + 2], codes[q], place, a_parts, [*b_parts[0], *b_parts[1]], out, out_blocks, group_count, slot_count
        )
        parts = []
        if q + 2 < len(gathered):
            out, gathered[q + 2] = after(out, gathered[q + 2])
            parts = pieces(q + 2)
        if q + 1 < len(gathered):
            out, *arrived = after(out, *own_swapped, *parts, *coming[1:])
            own_swapped, arrived = arrived[: group_count - 1], arrived[group_count - 1 :]
            parts, held = arrived[: len(parts)], [coming[0], *arrived[len(parts) :]]
    return out.reshape(width_g, keep_count, block_size, block_size)


def solution(mesh):
    placed = (P("row", "col", None, None, None), P("row", "col", None), P("row", "col"))
    return jax.shard_map(
        on_device,
        mesh=mesh,
        in_specs=placed,
        out_specs=P("row", "col", None, None),
        check_vma=False,
    )
```

time: 530 us -> 234 us (0.44)
  blocking collectives: 106 us -> 0 us
  waiting for transfers between devices: 195 us -> 111 us
  other arithmetic: 76.3 us -> 2.54 us
  local copies, waits for them, and re-layouts: 84.5 us -> 26.7 us
  matrix products: 47 us -> 0 us
  Pallas kernels: 0 us -> 37.6 us
  starting transfers between devices: 6.61 us -> 41.8 us
    all_gather x2 -> x3, waiting for transfers between devices: 190 us -> 11.6 us  [the longest x2 6.79 us: on_device(): lax.all_gather(x_rest[i * panel_slots:j * panel_slots], 'col')]
    ppermute x0 -> x38, waiting for transfers between devices: none -> 99.3 us  [send(): return lax.ppermute(value, ('row', 'col'), places)]
    all_to_all x2 -> x0, blocking collectives: 84.9 us -> none  [the longest x1 54.6 us: on_device(): lax.all_to_all(x_blocks, 'col', split_axis=0, concat_axis=1, tiled=True)]
    scatter-add x1 -> x0, other arithmetic: 75.4 us -> none  [reduce_rows(): return zero_sums.at[targets].add(flat)]
    dot_general x2 -> x0, matrix products: 47 us -> none  [the longest x1 26.8 us: block_products(): jnp.einsum('kesf,kftj->kestj', selector, b_flat, preferred_element_type=j...]
    ppermute x0 -> x38, starting transfers between devices: none -> 41.7 us  [send(): return lax.ppermute(value, ('row', 'col'), places)]
    pallas_call x0 -> x3, Pallas kernels: none -> 37.6 us  [add_products(): pl.pallas_call(functools.partial(product_kernel, cuts=cuts, source_count=...]
    reshape x1 -> x3, local copies, waits for them, and re-layouts: 33.4 us -> 0.43 us  [on_device(): codes.append(jnp.where(hit[:, i:j] >= 0, code, -1).reshape(-1))]
  transfers between devices with their start and end apart: 4 -> 41, of which waited for: 3 -> 18; matrix products, arithmetic and copies ran while one was open for 3% -> 10% of each run, Pallas kernels for 0% -> 12%
where the time goes in v1:
time: 234 us; the launch traced here: 233 us
  waiting for transfers between devices  111 us (47%)
  starting transfers between devices  41.8 us (18%)
  Pallas kernels  37.6 us (16%)
  local copies, waits for them, and re-layouts  26.7 us (11%)
  between operations  13.6 us (6%)
  other arithmetic  2.54 us (1%)
    ppermute x38, waiting for transfers between devices, send(): return lax.ppermute(value, ('row', 'col'), places)  99.3 us
    ppermute x38, starting transfers between devices, send(): return lax.ppermute(value, ('row', 'col'), places)  41.7 us
    pallas_call x3, Pallas kernels, add_products(): pl.pallas_call(functools.partial(product_kernel, cuts=cuts, source_count=...  37.6 us
    squeeze x2, local copies, waits for them, and re-layouts, pieces(): lax.dynamic_index_in_dim(gathered[q], panel ^ offset // group_count, 0, F...  7.61 us
    all_gather x2, waiting for transfers between devices, on_device(): lax.all_gather(x_rest[i * panel_slots:j * panel_slots], 'col')  6.79 us
    slice x16, local copies, waits for them, and re-layouts, on_device(): tag_parts = [part[-1, :rows_here, :panel_slots] for part in b_parts[1]]  4.9 us
    all_gather x1, waiting for transfers between devices, on_device(): gathered = [lax.all_gather(first_part, 'col')]  4.83 us
  transfers between devices with their start and end apart: 41, of which 18 were waited for; matrix products, arithmetic and copies ran while one was open for 10% of the time, Pallas kernels for 12%

profile of v1, /device:TPU:0, one launch (start us, length us, event | category | flops | bytes accessed | tf_op | source)
XLA Modules:
  0.0 233.2 jit_solution(9822189153651066781)
XLA Ops:
  6.5 2.5 %slice.60 = bf16[8,2,2,128,128]{4,3,2,1,0:T(8,128)(2,1)} slice(bf16[16,2,2,128,128]{4,3,2,1,0:T(8,128)(2,1)} %param.3), slice={[0:8], [0:2], [0:2], [0:128], [0:128]} | slice | bytes 2097152 | tf_op jit(solution)/shard_map/slice | solution.py:229
  9.1 3.0 %collective-permute-start.3 = (bf16[32,128,128]{2,1,0:T(8,128)(2,1)}, bf16[32,128,128]{2,1,0:T(8,128)(2,1)S(1)}, u32[]{:S(2)}, u32[]{:S(2)}) collective-permute-start(bf16[32,128,128]{2,1,0:T(8,128)(2,1)} %bitcast.42), channel_id=1, source_target_pairs={{0,16},{1,17},{2,18},{3,19},{4,20},{5,21},{6,22},{7,23},{8,24},{9,... | collective-permute-start | bytes 3145736 | tf_op jit(solution)/shard_map/ppermute | solution.py:216
  12.1 1.5 collective-permute-start.1
  13.6 0.9 slice.78
  14.6 1.0 slice.62
  15.8 1.4 pad_maximum_fusion.refs_16_
  17.2 0.6 collective-permute-start.9
  17.9 18.4 %collective-permute-done.3.refs_12_ = bf16[32,128,128]{2,1,0:T(8,128)(2,1)S(1)} collective-permute-done((bf16[32,128,128]{2,1,0:T(8,128)(2,1)}, bf16[32,128,128]{2,1,0:T(8,128)(2,1)S(1)}, u32[]{:S(2)}, u32[]{:S(2)}) %collective-permute-start.3) | collective-permute-done | bytes 1048608 | tf_op jit(solution)/shard_map/ppermute | solution.py:216
  36.3 2.2 collective-permute-done.1.refs_10_
  38.5 1.5 collective-permute-start.5
  40.0 18.6 %collective-permute-done.9.refs_20_ = bf16[33,128,128]{2,1,0:T(8,128)(2,1)S(1)} collective-permute-done((bf16[33,128,128]{2,1,0:T(8,128)(2,1)S(1)}, bf16[33,128,128]{2,1,0:T(8,128)(2,1)S(1)}, u32[]{:S(2)}, u32[]{:S(2)}) %collective-permute-start.9) | collective-permute-done | bytes 1081376 | tf_op jit(solution)/shard_map/ppermute | solution.py:216
  58.7 2.9 %collective-permute-done.7.refs_18_ = bf16[33,128,128]{2,1,0:T(8,128)(2,1)S(1)} collective-permute-done((bf16[33,128,128]{2,1,0:T(8,128)(2,1)S(1)}, bf16[33,128,128]{2,1,0:T(8,128)(2,1)S(1)}, u32[]{:S(2)}, u32[]{:S(2)}) %collective-permute-start.7) | collective-permute-done | bytes 1081376 | tf_op jit(solution)/shard_map/ppermute | solution.py:216
  61.7 0.5 collective-permute-start.4
  62.2 20.4 %collective-permute-done.5.refs_14_ = bf16[32,128,128]{2,1,0:T(8,128)(2,1)S(1)} collective-permute-done((bf16[32,128,128]{2,1,0:T(8,128)(2,1)S(1)}, bf16[32,128,128]{2,1,0:T(8,128)(2,1)S(1)}, u32[]{:S(2)}, u32[]{:S(2)}) %collective-permute-start.5) | collective-permute-done | bytes 1048608 | tf_op jit(solution)/shard_map/ppermute | solution.py:216
  82.6 2.9 %collective-permute-done.2.refs_11_ = bf16[32,128,128]{2,1,0:T(8,128)(2,1)S(1)} collective-permute-done((bf16[32,128,128]{2,1,0:T(8,128)(2,1)}, bf16[32,128,128]{2,1,0:T(8,128)(2,1)S(1)}, u32[]{:S(2)}, u32[]{:S(2)}) %collective-permute-start.2) | collective-permute-done | bytes 1048608 | tf_op jit(solution)/shard_map/ppermute | solution.py:216
  85.5 0.9 copy-done.11
  86.4 0.4 copy-done.5
  86.8 1.0 copy-done.6
  87.8 4.8 %all-gather.7.cloned.1.call-done = bf16[128,128,128]{2,1,0:T(8,128)(2,1)} async-done(((bf16[32,128,128]{2,1,0:T(8,128)(2,1)}), bf16[128,128,128]{2,1,0:T(8,128)(2,1)}) %all-gather.7.cloned.1.call-update) | async-done | bytes 4194320 | tf_op jit(solution)/shard_map/all_gather | solution.py:231
  92.7 4.4 %dynamic-slice_bitcast_fusion = (bf16[32,128,128]{2,1,0:T(8,128)(2,1)}, bf16[32,128,128]{2,1,0:T(8,128)(2,1)}, bf16[32,128,128]{2,1,0:T(8,128)(2,1)}, bf16[32,128,128]{2,1,0:T(8,128)(2,1)}) fusion(bf16[4,32,128,128]{3,2,1,0:T(8,128)(2,1)} %bitcast.48, s32[]{:T(128)S(6)} %select_n.99, s32[]{:T(128)S(6)} %select_n.98, s32[]{:T(128)S(6)} %select_n.97, ...), kind=kLoop, calls=%fused_computation.1 | loop fusion | bytes 8388624 | tf_op jit(solution)/shard_map/jit(dynamic_index_in_dim)/squeeze | solution.py:268
  97.0 5.3 %collective-permute-start.19 = (bf16[32,128,128]{2,1,0:T(8,128)(2,1)}, bf16[32,128,128]{2,1,0:T(8,128)(2,1)}, u32[]{:S(2)}, u32[]{:S(2)}) collective-permute-start(bf16[32,128,128]{2,1,0:T(8,128)(2,1)} %get-tuple-element.93), channel_id=1, source_target_pairs={{0,24},{1,25},{2,26},{4,28},{5,29},{6,30},{8,16},{9,17},{11,19},{1... | collective-permute-start | bytes 3145736 | tf_op jit(solution)/shard_map/ppermute | solution.py:216
  102.3 2.5 %collective-permute-start.18 = (bf16[32,128,128]{2,1,0:T(8,128)(2,1)}, bf16[32,128,128]{2,1,0:T(8,128)(2,1)}, u32[]{:S(2)}, u32[]{:S(2)}) collective-permute-start(bf16[32,128,128]{2,1,0:T(8,128)(2,1)} %get-tuple-element.94), channel_id=1, source_target_pairs={{0,16},{1,17},{3,19},{4,20},{5,21},{7,23},{8,24},{9,25},{10,26},{1... | collective-permute-start | bytes 3145736 | tf_op jit(solution)/shard_map/ppermute | solution.py:216
  104.8 1.3 collective-permute-start.17
  106.2 1.8 slice.75
  108.1 0.7 slice.69
  108.9 0.7 slice.64
  109.7 0.7 slice.65
  110.4 0.7 slice.66
  111.3 0.7 slice.68
  112.2 0.7 slice.79
  113.1 1.3 collective-permute-start.15
  114.4 1.3 collective-permute-done.15
  115.7 1.3 collective-permute-start.14
  117.0 1.2 collective-permute-done.14
  118.3 1.3 collective-permute-start.13
  119.7 1.1 collective-permute-done.13
  120.9 4.3 %collective-permute-done.19.refs_3_ = bf16[32,128,128]{2,1,0:T(8,128)(2,1)} collective-permute-done((bf16[32,128,128]{2,1,0:T(8,128)(2,1)}, bf16[32,128,128]{2,1,0:T(8,128)(2,1)}, u32[]{:S(2)}, u32[]{:S(2)}) %collective-permute-start.19) | collective-permute-done | bytes 1048608 | tf_op jit(solution)/shard_map/ppermute | solution.py:216
  125.2 22.0 %collective-permute-done.18.refs_2_ = bf16[32,128,128]{2,1,0:T(8,128)(2,1)} collective-permute-done((bf16[32,128,128]{2,1,0:T(8,128)(2,1)}, bf16[32,128,128]{2,1,0:T(8,128)(2,1)}, u32[]{:S(2)}, u32[]{:S(2)}) %collective-permute-start.18) | collective-permute-done | bytes 1048608 | tf_op jit(solution)/shard_map/ppermute | solution.py:216
  147.3 0.5 collective-permute-start.21
  147.8 3.2 %dynamic-slice_bitcast_fusion.4 = (bf16[20,128,128]{2,1,0:T(8,128)(2,1)}, bf16[20,128,128]{2,1,0:T(8,128)(2,1)}, bf16[20,128,128]{2,1,0:T(8,128)(2,1)}, bf16[20,128,128]{2,1,0:T(8,128)(2,1)}) fusion(bf16[4,20,128,128]{3,2,1,0:T(8,128)(2,1)} %bitcast.50, s32[]{:T(128)S(6)} %select_n.99, s32[]{:T(128)S(6)} %select_n.98, s32[]{:T(128)S(6)} %select_n.97, ...), kind=kLoop, calls=%fused_computation.5 | loop fusion | bytes 5242896 | tf_op jit(solution)/shard_map/jit(dynamic_index_in_dim)/squeeze | solution.py:268
  151.1 0.5 collective-permute-start.22
  151.7 0.7 select_reduce_fusion
  152.4 4.4 %collective-permute-start.25 = (bf16[20,128,128]{2,1,0:T(8,128)(2,1)}, bf16[20,128,128]{2,1,0:T(8,128)(2,1)S(1)}, u32[]{:S(2)}, u32[]{:S(2)}) collective-permute-start(bf16[20,128,128]{2,1,0:T(8,128)(2,1)} %get-tuple-element.74), channel_id=1, source_target_pairs={{0,8},{2,10},{3,11},{4,12},{6,14},{7,15},{9,1},{10,2},{11,3},{13,5... | collective-permute-start | bytes 1966088 | tf_op jit(solution)/shard_map/ppermute | solution.py:216
  156.8 3.4 %collective-permute-start.26 = (bf16[20,128,128]{2,1,0:T(8,128)(2,1)}, bf16[20,128,128]{2,1,0:T(8,128)(2,1)S(1)}, u32[]{:S(2)}, u32[]{:S(2)}) collective-permute-start(bf16[20,128,128]{2,1,0:T(8,128)(2,1)} %get-tuple-element.75), channel_id=1, source_target_pairs={{0,16},{1,17},{3,19},{4,20},{5,21},{7,23},{8,24},{9,25},{10,26},{1... | collective-permute-start | bytes 1966088 | tf_op jit(solution)/shard_map/ppermute | solution.py:216
  160.2 1.9 collective-permute-start.27
  162.5 15.9 %shard_map.37.refs_24_ = f32[192,128,128]{2,1,0:T(8,128)} custom-call(s32[256]{0:T(256)S(1)} %reshape.122.code_ref, s32[3]{0:T(128)S(1)} %pad_add_fusion.place_ref, bf16[4,32,128,128]{3,2,1,0:T(8,128)(2,1)} %bitcast.49, bf16[32,128,128]{2,1,0:T(8,128)(2,1)S(1)} %collective-permute-done.17.refs_1_, bf16[32,128,128]{2,1,0:T(8,128)(2,1)} %collective-permute-done.18.refs_2_, ...), custom_call_target="tpu_custom_call" | custom-call | flops 1073741824 | bytes 37748736 | tf_op jit(solution)/shard_map/pallas_call | solution.py:164
  178.5 6.8 %all-gather.9.cloned.1.call-done = bf16[48,128,128]{2,1,0:T(8,128)(2,1)} async-done(((bf16[12,128,128]{2,1,0:T(8,128)(2,1)}), bf16[48,128,128]{2,1,0:T(8,128)(2,1)}) %all-gather.9.cloned.1.call-update) | async-done | bytes 1572880 | tf_op jit(solution)/shard_map/all_gather | solution.py:233
  185.2 2.5 %dynamic-slice_bitcast_fusion.8 = (bf16[12,128,128]{2,1,0:T(8,128)(2,1)}, bf16[12,128,128]{2,1,0:T(8,128)(2,1)}, bf16[12,128,128]{2,1,0:T(8,128)(2,1)}, bf16[12,128,128]{2,1,0:T(8,128)(2,1)}) fusion(bf16[4,12,128,128]{3,2,1,0:T(8,128)(2,1)} %bitcast.52, s32[]{:T(128)S(6)} %select_n.96, s32[]{:T(128)S(6)} %select_n.99, s32[]{:T(128)S(6)} %select_n.98, ...), kind=kLoop, calls=%fused_computation.9 | loop fusion | bytes 3145744 | tf_op jit(solution)/shard_map/jit(dynamic_index_in_dim)/squeeze | solution.py:275
  187.8 0.7 collective-permute-done.26.refs_2_
  188.5 0.5 collective-permute-start.29
  189.0 3.1 %collective-permute-start.32 = (bf16[12,128,128]{2,1,0:T(8,128)(2,1)}, bf16[12,128,128]{2,1,0:T(8,128)(2,1)S(1)}, u32[]{:S(2)}, u32[]{:S(2)}) collective-permute-start(bf16[12,128,128]{2,1,0:T(8,128)(2,1)} %get-tuple-element.85), channel_id=1, source_target_pairs={{0,8},{2,10},{3,11},{4,12},{6,14},{7,15},{9,1},{10,2},{11,3},{13,5... | collective-permute-start | bytes 1179656 | tf_op jit(solution)/shard_map/ppermute | solution.py:216
  192.1 3.6 %collective-permute-start.33 = (bf16[12,128,128]{2,1,0:T(8,128)(2,1)}, bf16[12,128,128]{2,1,0:T(8,128)(2,1)S(1)}, u32[]{:S(2)}, u32[]{:S(2)}) collective-permute-start(bf16[12,128,128]{2,1,0:T(8,128)(2,1)} %get-tuple-element.86), channel_id=1, source_target_pairs={{0,16},{1,17},{3,19},{4,20},{5,21},{7,23},{8,24},{9,25},{10,26},{1... | collective-permute-start | bytes 1179656 | tf_op jit(solution)/shard_map/ppermute | solution.py:216
  195.8 2.8 %collective-permute-start.34 = (bf16[12,128,128]{2,1,0:T(8,128)(2,1)}, bf16[12,128,128]{2,1,0:T(8,128)(2,1)S(1)}, u32[]{:S(2)}, u32[]{:S(2)}) collective-permute-start(bf16[12,128,128]{2,1,0:T(8,128)(2,1)} %get-tuple-element.87), channel_id=1, source_target_pairs={{0,24},{1,25},{2,26},{4,28},{5,29},{6,30},{8,16},{9,17},{11,19},{1... | collective-permute-start | bytes 1179656 | tf_op jit(solution)/shard_map/ppermute | solution.py:216
  198.7 0.8 copy-done.14
  199.6 0.2 copy.39
  200.0 12.1 %shard_map.38.refs_24_ = f32[192,128,128]{2,1,0:T(8,128)} custom-call(s32[160]{0:T(256)S(1)} %reshape.126.code_ref, s32[3]{0:T(128)S(1)} %pad_add_fusion.place_ref, bf16[4,20,128,128]{3,2,1,0:T(8,128)(2,1)} %bitcast.51, bf16[20,128,128]{2,1,0:T(8,128)(2,1)S(1)} %collective-permute-done.25.refs_1_, ...), custom_call_target="tpu_custom_call", output_to_operand_aliasing={{}: (26, {})} | custom-call | flops 671088640 | bytes 33030144 | tf_op jit(solution)/shard_map/pallas_call | solution.py:164
  212.1 1.2 collective-permute-done.33.refs_2_
  213.2 0.5 collective-permute-start.36
  213.9 0.2 copy.37
  214.3 0.7 collective-permute-done.35.refs_5_
  215.0 0.6 collective-permute-done.36.refs_6_
  215.5 0.6 collective-permute-done.37.refs_7_
  216.3 0.8 copy-done.16
  217.0 9.6 %shard_map.39 = f32[192,128,128]{2,1,0:T(8,128)} custom-call(s32[96]{0:T(128)S(1)} %reshape.118.code_ref, s32[3]{0:T(128)S(1)} %pad_add_fusion.place_ref, bf16[4,12,128,128]{3,2,1,0:T(8,128)(2,1)} %bitcast.53, bf16[12,128,128]{2,1,0:T(8,128)(2,1)S(1)} %collective-permute-done.32.refs_1_, ...), custom_call_target="tpu_custom_call", output_to_operand_aliasing={{}: (26, {})} | custom-call | flops 402653184 | bytes 29884416 | tf_op jit(solution)/shard_map/pallas_call | solution.py:164
  (117 shorter events, 3.1 us)
Async XLA Ops:
  6.5 7.1 %copy-start.12 = (bf16[16,2,2,128,128]{4,3,2,1,0:T(8,128)(2,1)S(1)}, bf16[16,2,2,128,128]{4,3,2,1,0:T(8,128)(2,1)}, u32[]{:S(2)}) copy-start(bf16[16,2,2,128,128]{4,3,2,1,0:T(8,128)(2,1)} %param.3) | copy-start | bytes 6291460
  6.5 86.1 %all-gather.7.cloned.1.call-start = ((), (), s32[]{:S(2)}) async-start(), calls=%async_computation | async-start | bytes 5242880 | tf_op jit(solution)/shard_map/all_gather | solution.py:231
  9.0 138.7 %all-gather.11.cloned.1.call-start = ((), (), s32[]{:S(2)}) async-start(), calls=%async_computation.2 | async-start | bytes 3276800 | tf_op jit(solution)/shard_map/all_gather | solution.py:233
  9.1 27.2 %collective-permute-start.3 = (bf16[32,128,128]{2,1,0:T(8,128)(2,1)}, bf16[32,128,128]{2,1,0:T(8,128)(2,1)S(1)}, u32[]{:S(2)}, u32[]{:S(2)}) collective-permute-start(bf16[32,128,128]{2,1,0:T(8,128)(2,1)} %bitcast.42), channel_id=1, source_target_pairs={{0,16},{1,17},{2,18},{3,19},{4,20},{5,21},{6,22},{7,23},{8,24},{9,... | collective-permute-start | bytes 3145736 | tf_op jit(solution)/shard_map/ppermute | solution.py:216
  12.1 26.4 %collective-permute-start.1 = (bf16[32,128,128]{2,1,0:T(8,128)(2,1)}, bf16[32,128,128]{2,1,0:T(8,128)(2,1)}, u32[]{:S(2)}, u32[]{:S(2)}) collective-permute-start(bf16[32,128,128]{2,1,0:T(8,128)(2,1)} %bitcast.43), channel_id=1, source_target_pairs={{0,8},{1,9},{2,10},{3,11},{4,12},{5,13},{6,14},{7,15},{8,0},{9,1},... | collective-permute-start | bytes 3145736 | tf_op jit(solution)/shard_map/ppermute | solution.py:216
  14.6 1.1 copy-start.17
  14.6 170.7 %all-gather.9.cloned.1.call-start = ((), (), s32[]{:S(2)}) async-start(), calls=%async_computation.1 | async-start | bytes 1966080 | tf_op jit(solution)/shard_map/all_gather | solution.py:233
  15.8 20.6 %copy-start = (bf16[8,2,2,128,128]{4,3,2,1,0:T(8,128)(2,1)S(1)}, bf16[8,2,2,128,128]{4,3,2,1,0:T(8,128)(2,1)}, u32[]{:S(2)}) copy-start(bf16[8,2,2,128,128]{4,3,2,1,0:T(8,128)(2,1)} %slice.60) | copy-start | bytes 3145732
  17.2 91.6 %copy-start.1 = (bf16[33,128,128]{2,1,0:T(8,128)(2,1)}, bf16[33,128,128]{2,1,0:T(8,128)(2,1)S(1)}, u32[]{:S(2)}) copy-start(bf16[33,128,128]{2,1,0:T(8,128)(2,1)S(1)} %pad_maximum_fusion.refs_16_) | copy-start | bytes 3244036
  17.2 41.5 %collective-permute-start.9 = (bf16[33,128,128]{2,1,0:T(8,128)(2,1)S(1)}, bf16[33,128,128]{2,1,0:T(8,128)(2,1)S(1)}, u32[]{:S(2)}, u32[]{:S(2)}) collective-permute-start(bf16[33,128,128]{2,1,0:T(8,128)(2,1)S(1)} %pad_maximum_fusion.refs_16_), channel_id=1, source_target_pairs={{0,16},{1,17},{2,18},{3,19},{4,20},{5,21},{6,22},{7,23},{8,24},{9,... | collective-permute-start | bytes 3244040 | tf_op jit(solution)/shard_map/ppermute | solution.py:216
  17.8 43.8 %collective-permute-start.7 = (bf16[33,128,128]{2,1,0:T(8,128)(2,1)S(1)}, bf16[33,128,128]{2,1,0:T(8,128)(2,1)S(1)}, u32[]{:S(2)}, u32[]{:S(2)}) collective-permute-start(bf16[33,128,128]{2,1,0:T(8,128)(2,1)S(1)} %pad_maximum_fusion.refs_16_), channel_id=1, source_target_pairs={{0,8},{1,9},{2,10},{3,11},{4,12},{5,13},{6,14},{7,15},{8,0},{9,1},... | collective-permute-start | bytes 3244040 | tf_op jit(solution)/shard_map/ppermute | solution.py:216
  17.9 43.8 %collective-permute-start.6 = (bf16[33,128,128]{2,1,0:T(8,128)(2,1)S(1)}, bf16[33,128,128]{2,1,0:T(8,128)(2,1)S(1)}, u32[]{:S(2)}, u32[]{:S(2)}) collective-permute-start(bf16[33,128,128]{2,1,0:T(8,128)(2,1)S(1)} %pad_maximum_fusion.refs_16_), channel_id=1, source_target_pairs={{0,4},{1,5},{2,6},{3,7},{4,0},{5,1},{6,2},{7,3},{8,12},{9,13},{10,... | collective-permute-start | bytes 3244040 | tf_op jit(solution)/shard_map/ppermute | solution.py:216
  36.3 60.7 %copy-start.7 = (bf16[32,128,128]{2,1,0:T(8,128)(2,1)}, bf16[32,128,128]{2,1,0:T(8,128)(2,1)S(1)}, u32[]{:S(2)}) copy-start(bf16[32,128,128]{2,1,0:T(8,128)(2,1)S(1)} %collective-permute-done.3.refs_12_) | copy-start | bytes 3145732
  36.3 25.3 %collective-permute-start = (bf16[32,128,128]{2,1,0:T(8,128)(2,1)S(1)}, bf16[32,128,128]{2,1,0:T(8,128)(2,1)S(1)}, u32[]{:S(2)}, u32[]{:S(2)}) collective-permute-start(bf16[32,128,128]{2,1,0:T(8,128)(2,1)S(1)} %bitcast.47), channel_id=1, source_target_pairs={{0,4},{1,5},{2,6},{3,7},{4,0},{5,1},{6,2},{7,3},{8,12},{9,13},{10,... | collective-permute-start | bytes 3145736 | tf_op jit(solution)/shard_map/ppermute | solution.py:216
  38.5 44.1 %collective-permute-start.5 = (bf16[32,128,128]{2,1,0:T(8,128)(2,1)S(1)}, bf16[32,128,128]{2,1,0:T(8,128)(2,1)S(1)}, u32[]{:S(2)}, u32[]{:S(2)}) collective-permute-start(bf16[32,128,128]{2,1,0:T(8,128)(2,1)S(1)} %collective-permute-done.3.refs_12_), channel_id=1, source_target_pairs={{0,8},{1,9},{2,10},{3,11},{4,12},{5,13},{6,14},{7,15},{8,0},{9,1},... | collective-permute-start | bytes 3145736 | tf_op jit(solution)/shard_map/ppermute | solution.py:216
  58.7 52.5 %copy-start.2 = (bf16[33,128,128]{2,1,0:T(8,128)(2,1)}, bf16[33,128,128]{2,1,0:T(8,128)(2,1)S(1)}, u32[]{:S(2)}) copy-start(bf16[33,128,128]{2,1,0:T(8,128)(2,1)S(1)} %collective-permute-done.9.refs_20_) | copy-start | bytes 3244036
  58.7 26.8 %collective-permute-start.10 = (bf16[33,128,128]{2,1,0:T(8,128)(2,1)S(1)}, bf16[33,128,128]{2,1,0:T(8,128)(2,1)S(1)}, u32[]{:S(2)}, u32[]{:S(2)}) collective-permute-start(bf16[33,128,128]{2,1,0:T(8,128)(2,1)S(1)} %collective-permute-done.9.refs_20_), channel_id=1, source_target_pairs={{0,4},{1,5},{2,6},{3,7},{4,0},{5,1},{6,2},{7,3},{8,12},{9,13},{10,... | collective-permute-start | bytes 3244040 | tf_op jit(solution)/shard_map/ppermute | solution.py:216
  61.6 23.9 %copy-start.3 = (bf16[33,128,128]{2,1,0:T(8,128)(2,1)}, bf16[33,128,128]{2,1,0:T(8,128)(2,1)S(1)}, u32[]{:S(2)}) copy-start(bf16[33,128,128]{2,1,0:T(8,128)(2,1)S(1)} %collective-permute-done.7.refs_18_) | copy-start | bytes 3244036
  61.6 23.9 %collective-permute-start.11 = (bf16[33,128,128]{2,1,0:T(8,128)(2,1)S(1)}, bf16[33,128,128]{2,1,0:T(8,128)(2,1)S(1)}, u32[]{:S(2)}, u32[]{:S(2)}) collective-permute-start(bf16[33,128,128]{2,1,0:T(8,128)(2,1)S(1)} %collective-permute-done.7.refs_18_), channel_id=1, source_target_pairs={{0,16},{1,17},{2,18},{3,19},{4,20},{5,21},{6,22},{7,23},{8,24},{9,... | collective-permute-start | bytes 3244040 | tf_op jit(solution)/shard_map/ppermute | solution.py:216
  61.6 23.9 %copy-start.8 = (bf16[32,128,128]{2,1,0:T(8,128)(2,1)}, bf16[32,128,128]{2,1,0:T(8,128)(2,1)S(1)}, u32[]{:S(2)}) copy-start(bf16[32,128,128]{2,1,0:T(8,128)(2,1)S(1)} %collective-permute-done.refs_9_) | copy-start | bytes 3145732
  61.6 26.2 %collective-permute-start.8 = (bf16[33,128,128]{2,1,0:T(8,128)(2,1)S(1)}, bf16[33,128,128]{2,1,0:T(8,128)(2,1)}, u32[]{:S(2)}, u32[]{:S(2)}) collective-permute-start(bf16[33,128,128]{2,1,0:T(8,128)(2,1)S(1)} %collective-permute-done.7.refs_18_), channel_id=1, source_target_pairs={{0,4},{1,5},{2,6},{3,7},{4,0},{5,1},{6,2},{7,3},{8,12},{9,13},{10,... | collective-permute-start | bytes 3244040 | tf_op jit(solution)/shard_map/ppermute | solution.py:216
  61.7 23.8 %copy-start.4 = (bf16[33,128,128]{2,1,0:T(8,128)(2,1)}, bf16[33,128,128]{2,1,0:T(8,128)(2,1)S(1)}, u32[]{:S(2)}) copy-start(bf16[33,128,128]{2,1,0:T(8,128)(2,1)S(1)} %collective-permute-done.6.refs_17_) | copy-start | bytes 3244036
  61.7 20.9 %collective-permute-start.4 = (bf16[32,128,128]{2,1,0:T(8,128)(2,1)S(1)}, bf16[32,128,128]{2,1,0:T(8,128)(2,1)S(1)}, u32[]{:S(2)}, u32[]{:S(2)}) collective-permute-start(bf16[32,128,128]{2,1,0:T(8,128)(2,1)S(1)} %collective-permute-done.3.refs_12_), channel_id=1, source_target_pairs={{0,4},{1,5},{2,6},{3,7},{4,0},{5,1},{6,2},{7,3},{8,12},{9,13},{10,... | collective-permute-start | bytes 3145736 | tf_op jit(solution)/shard_map/ppermute | solution.py:216
  82.6 2.9 %copy-start.9 = (bf16[32,128,128]{2,1,0:T(8,128)(2,1)}, bf16[32,128,128]{2,1,0:T(8,128)(2,1)S(1)}, u32[]{:S(2)}) copy-start(bf16[32,128,128]{2,1,0:T(8,128)(2,1)S(1)} %collective-permute-done.5.refs_14_) | copy-start | bytes 3145732
  82.6 2.9 %collective-permute-start.2 = (bf16[32,128,128]{2,1,0:T(8,128)(2,1)}, bf16[32,128,128]{2,1,0:T(8,128)(2,1)S(1)}, u32[]{:S(2)}, u32[]{:S(2)}) collective-permute-start(bf16[32,128,128]{2,1,0:T(8,128)(2,1)} %collective-permute-done.1.refs_10_), channel_id=1, source_target_pairs={{0,4},{1,5},{2,6},{3,7},{4,0},{5,1},{6,2},{7,3},{8,12},{9,13},{10,... | collective-permute-start | bytes 3145736 | tf_op jit(solution)/shard_map/ppermute | solution.py:216
  82.6 2.9 %copy-start.10 = (bf16[32,128,128]{2,1,0:T(8,128)(2,1)}, bf16[32,128,128]{2,1,0:T(8,128)(2,1)S(1)}, u32[]{:S(2)}) copy-start(bf16[32,128,128]{2,1,0:T(8,128)(2,1)S(1)} %collective-permute-done.4.refs_13_) | copy-start | bytes 3145732
  85.5 1.0 copy-start.11
  85.5 1.3 copy-start.5
  86.8 1.0 copy-start.6
  92.7 19.6 %collective-permute-start.12 = (bf16[33,128,128]{2,1,0:T(8,128)(2,1)}, bf16[33,128,128]{2,1,0:T(8,128)(2,1)}, u32[]{:S(2)}, u32[]{:S(2)}) collective-permute-start(bf16[33,128,128]{2,1,0:T(8,128)(2,1)} %copy-done.6), channel_id=1, source_target_pairs={{0,4},{1,5},{2,6},{3,7},{4,0},{5,1},{6,2},{7,3},{8,12},{9,13},{10,... | collective-permute-start | bytes 3244040 | tf_op jit(solution)/shard_map/ppermute | solution.py:216
  97.0 28.1 %collective-permute-start.19 = (bf16[32,128,128]{2,1,0:T(8,128)(2,1)}, bf16[32,128,128]{2,1,0:T(8,128)(2,1)}, u32[]{:S(2)}, u32[]{:S(2)}) collective-permute-start(bf16[32,128,128]{2,1,0:T(8,128)(2,1)} %get-tuple-element.93), channel_id=1, source_target_pairs={{0,24},{1,25},{2,26},{4,28},{5,29},{6,30},{8,16},{9,17},{11,19},{1... | collective-permute-start | bytes 3145736 | tf_op jit(solution)/shard_map/ppermute | solution.py:216
  102.3 44.9 %collective-permute-start.18 = (bf16[32,128,128]{2,1,0:T(8,128)(2,1)}, bf16[32,128,128]{2,1,0:T(8,128)(2,1)}, u32[]{:S(2)}, u32[]{:S(2)}) collective-permute-start(bf16[32,128,128]{2,1,0:T(8,128)(2,1)} %get-tuple-element.94), channel_id=1, source_target_pairs={{0,16},{1,17},{3,19},{4,20},{5,21},{7,23},{8,24},{9,25},{10,26},{1... | collective-permute-start | bytes 3145736 | tf_op jit(solution)/shard_map/ppermute | solution.py:216
  104.8 42.5 %collective-permute-start.17 = (bf16[32,128,128]{2,1,0:T(8,128)(2,1)}, bf16[32,128,128]{2,1,0:T(8,128)(2,1)S(1)}, u32[]{:S(2)}, u32[]{:S(2)}) collective-permute-start(bf16[32,128,128]{2,1,0:T(8,128)(2,1)} %get-tuple-element.95), channel_id=1, source_target_pairs={{0,8},{2,10},{3,11},{4,12},{6,14},{7,15},{9,1},{10,2},{11,3},{13,5... | collective-permute-start | bytes 3145736 | tf_op jit(solution)/shard_map/ppermute | solution.py:216
  106.1 41.1 %collective-permute-start.16 = (bf16[32,128,128]{2,1,0:T(8,128)(2,1)}, bf16[32,128,128]{2,1,0:T(8,128)(2,1)}, u32[]{:S(2)}, u32[]{:S(2)}) collective-permute-start(bf16[32,128,128]{2,1,0:T(8,128)(2,1)} %get-tuple-element.96), channel_id=1, source_target_pairs={{0,4},{1,5},{2,6},{3,7},{4,0},{5,1},{6,2},{7,3},{8,12},{9,13},{10,... | collective-permute-start | bytes 3145736 | tf_op jit(solution)/shard_map/ppermute | solution.py:216
  113.1 2.6 %collective-permute-start.15 = (bf16[8,16,2]{1,0,2:T(8,128)(2,1)S(1)}, bf16[8,16,2]{1,0,2:T(8,128)(2,1)S(1)}, u32[]{:S(2)}, u32[]{:S(2)}) collective-permute-start(bf16[8,16,2]{1,0,2:T(8,128)(2,1)S(1)} %dynamic-slice_bitcast_fusion.12), channel_id=1, source_target_pairs={{0,1},{4,5},{9,10},{13,14},{18,19},{22,23},{27,24},{31,28}} | collective-permute-start | bytes 1544 | tf_op jit(solution)/shard_map/ppermute | solution.py:216
  115.7 2.6 %collective-permute-start.14 = (bf16[8,16,2]{1,0,2:T(8,128)(2,1)S(1)}, bf16[8,16,2]{1,0,2:T(8,128)(2,1)S(1)}, u32[]{:S(2)}, u32[]{:S(2)}) collective-permute-start(bf16[8,16,2]{1,0,2:T(8,128)(2,1)S(1)} %dynamic-slice_bitcast_fusion.12), channel_id=1, source_target_pairs={{0,2},{4,6},{9,11},{13,15},{18,16},{22,20},{27,25},{31,29}} | collective-permute-start | bytes 1544 | tf_op jit(solution)/shard_map/ppermute | solution.py:216
  118.3 2.6 %collective-permute-start.13 = (bf16[8,16,2]{1,0,2:T(8,128)(2,1)S(1)}, bf16[8,16,2]{1,0,2:T(8,128)(2,1)S(1)}, u32[]{:S(2)}, u32[]{:S(2)}) collective-permute-start(bf16[8,16,2]{1,0,2:T(8,128)(2,1)S(1)} %dynamic-slice_bitcast_fusion.12), channel_id=1, source_target_pairs={{0,3},{4,7},{9,8},{13,12},{18,17},{22,21},{27,26},{31,30}} | collective-permute-start | bytes 1544 | tf_op jit(solution)/shard_map/ppermute | solution.py:216
  120.9 31.6 %collective-permute-start.23 = (bf16[32,128,128]{2,1,0:T(8,128)(2,1)}, bf16[32,128,128]{2,1,0:T(8,128)(2,1)}, u32[]{:S(2)}, u32[]{:S(2)}) collective-permute-start(bf16[32,128,128]{2,1,0:T(8,128)(2,1)} %copy-done.9), channel_id=1, source_target_pairs={{0,4},{1,5},{2,6},{3,7},{4,0},{5,1},{6,2},{7,3},{8,12},{9,13},{10,... | collective-permute-start | bytes 3145736 | tf_op jit(solution)/shard_map/ppermute | solution.py:216
  147.3 9.6 %collective-permute-start.20 = (bf16[32,128,128]{2,1,0:T(8,128)(2,1)S(1)}, bf16[32,128,128]{2,1,0:T(8,128)(2,1)}, u32[]{:S(2)}, u32[]{:S(2)}) collective-permute-start(bf16[32,128,128]{2,1,0:T(8,128)(2,1)S(1)} %collective-permute-done.17.refs_1_), channel_id=1, source_target_pairs={{0,4},{1,5},{2,6},{3,7},{4,0},{5,1},{6,2},{7,3},{8,12},{9,13},{10,... | collective-permute-start | bytes 3145736 | tf_op jit(solution)/shard_map/ppermute | solution.py:216
  147.3 13.0 %collective-permute-start.21 = (bf16[32,128,128]{2,1,0:T(8,128)(2,1)}, bf16[32,128,128]{2,1,0:T(8,128)(2,1)}, u32[]{:S(2)}, u32[]{:S(2)}) collective-permute-start(bf16[32,128,128]{2,1,0:T(8,128)(2,1)} %collective-permute-done.18.refs_2_), channel_id=1, source_target_pairs={{0,4},{1,5},{2,6},{3,7},{4,0},{5,1},{6,2},{7,3},{8,12},{9,13},{10,... | collective-permute-start | bytes 3145736 | tf_op jit(solution)/shard_map/ppermute | solution.py:216
  147.8 4.0 %copy-start.18 = (s32[96,2]{0,1:T(2,128)S(1)}, s32[96,2]{0,1:T(2,128)}, u32[]{:S(2)}) copy-start(s32[96,2]{0,1:T(2,128)} %param.5) | copy-start | bytes 2308
  151.0 36.7 %collective-permute-start.24 = (bf16[20,128,128]{2,1,0:T(8,128)(2,1)}, bf16[20,128,128]{2,1,0:T(8,128)(2,1)}, u32[]{:S(2)}, u32[]{:S(2)}) collective-permute-start(bf16[20,128,128]{2,1,0:T(8,128)(2,1)} %get-tuple-element.100), channel_id=1, source_target_pairs={{0,4},{1,5},{2,6},{3,7},{4,0},{5,1},{6,2},{7,3},{8,12},{9,13},{10,... | collective-permute-start | bytes 1966088 | tf_op jit(solution)/shard_map/ppermute | solution.py:216
  151.1 11.4 %collective-permute-start.22 = (bf16[32,128,128]{2,1,0:T(8,128)(2,1)}, bf16[32,128,128]{2,1,0:T(8,128)(2,1)}, u32[]{:S(2)}, u32[]{:S(2)}) collective-permute-start(bf16[32,128,128]{2,1,0:T(8,128)(2,1)} %collective-permute-done.19.refs_3_), channel_id=1, source_target_pairs={{0,4},{1,5},{2,6},{3,7},{4,0},{5,1},{6,2},{7,3},{8,12},{9,13},{10,... | collective-permute-start | bytes 3145736 | tf_op jit(solution)/shard_map/ppermute | solution.py:216
  152.4 35.3 %collective-permute-start.25 = (bf16[20,128,128]{2,1,0:T(8,128)(2,1)}, bf16[20,128,128]{2,1,0:T(8,128)(2,1)S(1)}, u32[]{:S(2)}, u32[]{:S(2)}) collective-permute-start(bf16[20,128,128]{2,1,0:T(8,128)(2,1)} %get-tuple-element.74), channel_id=1, source_target_pairs={{0,8},{2,10},{3,11},{4,12},{6,14},{7,15},{9,1},{10,2},{11,3},{13,5... | collective-permute-start | bytes 1966088 | tf_op jit(solution)/shard_map/ppermute | solution.py:216
  156.8 31.6 %collective-permute-start.26 = (bf16[20,128,128]{2,1,0:T(8,128)(2,1)}, bf16[20,128,128]{2,1,0:T(8,128)(2,1)S(1)}, u32[]{:S(2)}, u32[]{:S(2)}) collective-permute-start(bf16[20,128,128]{2,1,0:T(8,128)(2,1)} %get-tuple-element.75), channel_id=1, source_target_pairs={{0,16},{1,17},{3,19},{4,20},{5,21},{7,23},{8,24},{9,25},{10,26},{1... | collective-permute-start | bytes 1966088 | tf_op jit(solution)/shard_map/ppermute | solution.py:216
  160.2 28.2 %collective-permute-start.27 = (bf16[20,128,128]{2,1,0:T(8,128)(2,1)}, bf16[20,128,128]{2,1,0:T(8,128)(2,1)S(1)}, u32[]{:S(2)}, u32[]{:S(2)}) collective-permute-start(bf16[20,128,128]{2,1,0:T(8,128)(2,1)} %get-tuple-element.76), channel_id=1, source_target_pairs={{0,24},{1,25},{2,26},{4,28},{5,29},{6,30},{8,16},{9,17},{11,19},{1... | collective-permute-start | bytes 1966088 | tf_op jit(solution)/shard_map/ppermute | solution.py:216
  188.5 7.3 %collective-permute-start.28 = (bf16[20,128,128]{2,1,0:T(8,128)(2,1)S(1)}, bf16[20,128,128]{2,1,0:T(8,128)(2,1)S(1)}, u32[]{:S(2)}, u32[]{:S(2)}) collective-permute-start(bf16[20,128,128]{2,1,0:T(8,128)(2,1)S(1)} %collective-permute-done.25.refs_1_), channel_id=1, source_target_pairs={{0,4},{1,5},{2,6},{3,7},{4,0},{5,1},{6,2},{7,3},{8,12},{9,13},{10,... | collective-permute-start | bytes 1966088 | tf_op jit(solution)/shard_map/ppermute | solution.py:216
  188.5 10.1 %collective-permute-start.29 = (bf16[20,128,128]{2,1,0:T(8,128)(2,1)S(1)}, bf16[20,128,128]{2,1,0:T(8,128)(2,1)S(1)}, u32[]{:S(2)}, u32[]{:S(2)}) collective-permute-start(bf16[20,128,128]{2,1,0:T(8,128)(2,1)S(1)} %collective-permute-done.26.refs_2_), channel_id=1, source_target_pairs={{0,4},{1,5},{2,6},{3,7},{4,0},{5,1},{6,2},{7,3},{8,12},{9,13},{10,... | collective-permute-start | bytes 1966088 | tf_op jit(solution)/shard_map/ppermute | solution.py:216
  189.0 11.0 %collective-permute-start.30 = (bf16[20,128,128]{2,1,0:T(8,128)(2,1)S(1)}, bf16[20,128,128]{2,1,0:T(8,128)(2,1)}, u32[]{:S(2)}, u32[]{:S(2)}) collective-permute-start(bf16[20,128,128]{2,1,0:T(8,128)(2,1)S(1)} %collective-permute-done.27.refs_3_), channel_id=1, source_target_pairs={{0,4},{1,5},{2,6},{3,7},{4,0},{5,1},{6,2},{7,3},{8,12},{9,13},{10,... | collective-permute-start | bytes 1966088 | tf_op jit(solution)/shard_map/ppermute | solution.py:216
  189.0 23.0 %collective-permute-start.32 = (bf16[12,128,128]{2,1,0:T(8,128)(2,1)}, bf16[12,128,128]{2,1,0:T(8,128)(2,1)S(1)}, u32[]{:S(2)}, u32[]{:S(2)}) collective-permute-start(bf16[12,128,128]{2,1,0:T(8,128)(2,1)} %get-tuple-element.85), channel_id=1, source_target_pairs={{0,8},{2,10},{3,11},{4,12},{6,14},{7,15},{9,1},{10,2},{11,3},{13,5... | collective-permute-start | bytes 1179656 | tf_op jit(solution)/shard_map/ppermute | solution.py:216
  192.1 21.1 %collective-permute-start.33 = (bf16[12,128,128]{2,1,0:T(8,128)(2,1)}, bf16[12,128,128]{2,1,0:T(8,128)(2,1)S(1)}, u32[]{:S(2)}, u32[]{:S(2)}) collective-permute-start(bf16[12,128,128]{2,1,0:T(8,128)(2,1)} %get-tuple-element.86), channel_id=1, source_target_pairs={{0,16},{1,17},{3,19},{4,20},{5,21},{7,23},{8,24},{9,25},{10,26},{1... | collective-permute-start | bytes 1179656 | tf_op jit(solution)/shard_map/ppermute | solution.py:216
  195.8 2.9 %copy-start.13 = (bf16[20,128,128]{2,1,0:T(8,128)(2,1)}, bf16[20,128,128]{2,1,0:T(8,128)(2,1)S(1)}, u32[]{:S(2)}) copy-start(bf16[20,128,128]{2,1,0:T(8,128)(2,1)S(1)} %collective-permute-done.28.refs_5_) | copy-start | bytes 1966084
  195.8 17.4 %collective-permute-start.34 = (bf16[12,128,128]{2,1,0:T(8,128)(2,1)}, bf16[12,128,128]{2,1,0:T(8,128)(2,1)S(1)}, u32[]{:S(2)}, u32[]{:S(2)}) collective-permute-start(bf16[12,128,128]{2,1,0:T(8,128)(2,1)} %get-tuple-element.87), channel_id=1, source_target_pairs={{0,24},{1,25},{2,26},{4,28},{5,29},{6,30},{8,16},{9,17},{11,19},{1... | collective-permute-start | bytes 1179656 | tf_op jit(solution)/shard_map/ppermute | solution.py:216
  198.6 0.9 copy-start.14
  199.5 13.7 %collective-permute-start.31 = (bf16[12,128,128]{2,1,0:T(8,128)(2,1)}, bf16[12,128,128]{2,1,0:T(8,128)(2,1)}, u32[]{:S(2)}, u32[]{:S(2)}) collective-permute-start(bf16[12,128,128]{2,1,0:T(8,128)(2,1)} %get-tuple-element.101), channel_id=1, source_target_pairs={{0,4},{1,5},{2,6},{3,7},{4,0},{5,1},{6,2},{7,3},{8,12},{9,13},{10,... | collective-permute-start | bytes 1179656 | tf_op jit(solution)/shard_map/ppermute | solution.py:216
  213.2 1.7 collective-permute-start.35
  213.2 2.3 collective-permute-start.36
  213.8 2.3 %collective-permute-start.37 = (bf16[12,128,128]{2,1,0:T(8,128)(2,1)S(1)}, bf16[12,128,128]{2,1,0:T(8,128)(2,1)S(1)}, u32[]{:S(2)}, u32[]{:S(2)}) collective-permute-start(bf16[12,128,128]{2,1,0:T(8,128)(2,1)S(1)} %collective-permute-done.34.refs_3_), channel_id=1, source_target_pairs={{0,4},{1,5},{2,6},{3,7},{4,0},{5,1},{6,2},{7,3},{8,12},{9,13},{10,... | collective-permute-start | bytes 1179656 | tf_op jit(solution)/shard_map/ppermute | solution.py:216
  215.5 0.7 copy-start.15
  216.3 0.8 copy-start.16
Sparse Core Ops, SparseCore 0:
  9.2 83.4 all-gather.6
  94.2 53.3 all-gather.10
  149.2 36.0 all-gather.8

commit v2 on v1

--- a/solution.py
+++ b/solution.py
@@ -11,7 +11,74 @@
 UNROLL = 8
 
 
-def product_kernel(code_ref, place_ref, *refs, cuts, source_count, slot_count, group_count, first):
+def fill_plan(code_ref, plan_ref, seen, own, group, slot_count, group_count, keep_count, block_total):
+    panel_slots = group_count * slot_count
+    pairs = code_ref.shape[0]
+    size = pairs + UNROLL
+    b_base = pairs // keep_count
+
+    def clear(block, carry):
+        seen[block] = 0
+        return carry
+
+    lax.fori_loop(0, block_total, clear, 0)
+
+    def note(at, counts):
+        count, touched_count = counts
+        row, slot = at // slot_count, at % slot_count
+        a_at = jnp.where(own == 1, b_base + row * panel_slots + group * slot_count + slot, at)
+        for keep in range(keep_count):
+            code = code_ref[at * keep_count + keep]
+            block = lax.bitwise_and(code, (1 << SHIFT) - 1)
+            known = jnp.minimum(block, block_total - 1)
+            plan_ref[2 + count] = a_at
+            plan_ref[2 + size + count] = lax.shift_right_logical(code, SHIFT) + b_base
+            plan_ref[2 + 2 * size + count] = block
+            count = count + (code >= 0).astype(jnp.int32)
+            fresh = jnp.logical_and(code >= 0, seen[known] == 0)
+            plan_ref[2 + 3 * size + touched_count] = known
+            seen[known] = jnp.where(code >= 0, 1, seen[known])
+            touched_count = touched_count + fresh.astype(jnp.int32)
+        return count, touched_count
+
+    count, touched_count = lax.fori_loop(0, b_base, note, (jnp.int32(0), jnp.int32(0)))
+    for k in range(UNROLL):
+        plan_ref[2 + count + k] = b_base
+        plan_ref[2 + size + count + k] = b_base
+        plan_ref[2 + 2 * size + count + k] = block_total
+    plan_ref[0] = (count + UNROLL - 1) // UNROLL
+    plan_ref[1] = touched_count
+
+
+def plan_kernel(place_ref, *refs, **sizes):
+    chunk_count = len(refs) // 2
+    for chunk in range(chunk_count):
+        fill_plan(refs[chunk], refs[chunk_count + chunk], refs[-1], place_ref[0], place_ref[1], **sizes)
+
+
+def plan_size(pairs, out_blocks):
+    return 3 * (pairs + UNROLL) + out_blocks + 4
+
+
+def make_plans(codes, place, out_blocks, group_count, slot_count, keep_count):
+    scalars = pl.BlockSpec(memory_space=pltpu.SMEM)
+    return pl.pallas_call(
+        functools.partial(
+            plan_kernel,
+            slot_count=slot_count,
+            group_count=group_count,
+            keep_count=keep_count,
+            block_total=out_blocks,
+        ),
+        out_shape=[jax.ShapeDtypeStruct((plan_size(code.shape[0], out_blocks),), jnp.int32) for code in codes],
+        in_specs=[scalars] * (1 + len(codes)),
+        out_specs=[scalars] * len(codes),
+        scratch_shapes=[pltpu.SMEM((out_blocks,), jnp.int32)],
+        cost_estimate=pl.CostEstimate(flops=0, bytes_accessed=1 << 10, transcendentals=0),
+    )(place, *codes)
+
+
+def product_kernel(plan_ref, place_ref, *refs, cuts, pairs, source_count, slot_count, group_count, first):
     chip_count, panel_slots = source_count // group_count, group_count * slot_count
     row0, row_count, pieces = cuts[0], cuts[-1] - cuts[0], list(zip(cuts, cuts[1:]))
     a_refs = []
@@ -21,8 +88,11 @@
     b_refs, refs = (refs[:source_count], refs[source_count : 2 * source_count]), refs[2 * source_count :]
     if not first:
         before_ref, refs = refs[0], refs[1:]
-    out_ref, blocks, total, list_a, list_b, list_o, touched, seen, a_sem, b_sem, out_sem = refs
     own, group, panel = place_ref[0], place_ref[1], place_ref[2]
+    size = pairs + UNROLL
+    if first:
+        code_ref, plan_ref, seen, refs = plan_ref, refs[-2], refs[-1], refs[:-2]
+    out_ref, blocks, total, a_sem, b_sem, out_sem = refs
     a_size, b_size = row_count * slot_count, row_count * panel_slots
     b_base = source_count * a_size
 
@@ -68,53 +138,19 @@
         for source in range(source_count):
             start_a(source)
 
-    block_total = out_ref.shape[0]
-    keep_count = code_ref.shape[0] // (source_count * row_count * slot_count)
+    def each_touched(act):
+        def step(at, carry):
+            act(plan_ref[2 + 3 * size + at])
+            return carry
+
+        lax.fori_loop(0, plan_ref[1], step, 0)
+
     if first:
         total[...] = jnp.zeros_like(total)
+        keep_count = pairs // (source_count * row_count * slot_count)
+        fill_plan(code_ref, plan_ref, seen, own, group, slot_count, group_count, keep_count, out_ref.shape[0])
     else:
-
-        def clear(block, carry):
-            seen[block] = 0
-            return carry
-
-        lax.fori_loop(0, block_total, clear, 0)
-
-    def note(at, counts):
-        count, touched_count = counts
-        row, slot = at // slot_count, at % slot_count
-        kept_at = b_base + row * panel_slots + group * slot_count + slot
-        a_at = jnp.where(own == 1, kept_at, at)
-        for keep in range(keep_count):
-            code = code_ref[at * keep_count + keep]
-            block = lax.bitwise_and(code, (1 << SHIFT) - 1)
-            list_a[count] = a_at
-            list_b[count] = lax.shift_right_logical(code, SHIFT) + b_base
-            list_o[count] = block
-            count = count + (code >= 0).astype(jnp.int32)
-            if not first:
-                known = jnp.minimum(block, block_total - 1)
-                fresh = jnp.logical_and(code >= 0, seen[known] == 0)
-                touched[touched_count] = known
-
-                @pl.when(fresh)
-                def _():
-                    seen[known] = 1
-                    load(known).start()
-
-                touched_count = touched_count + fresh.astype(jnp.int32)
-        return count, touched_count
-
-    count, touched_count = lax.fori_loop(
-        0, source_count * row_count * slot_count, note, (jnp.int32(0), jnp.int32(0))
-    )
-
-    def each_touched(act):
-        def step(at, carry):
-            act(touched[at])
-            return carry
-
-        lax.fori_loop(0, touched_count, step, 0)
+        each_touched(lambda block: load(block).start())
 
     for source in range(source_count):
         for copy in b_copies(source):
@@ -129,23 +165,19 @@
         each_touched(lambda block: load(block).wait())
 
     def product(at):
-        a, b = blocks[list_a[at]], blocks[list_b[at]]
+        a, b = blocks[plan_ref[2 + at]], blocks[plan_ref[2 + size + at]]
         return lax.dot_general(a, b, (((0,), (0,)), ((), ())), preferred_element_type=jnp.float32)
 
     def several(step, carry):
         at = step * UNROLL
         values = [product(at + k) for k in range(UNROLL)]
         for k in range(UNROLL):
-            total[list_o[at + k]] += values[k]
+            total[plan_ref[2 + 2 * size + at + k]] += values[k]
         return carry
 
-    for k in range(UNROLL):
-        list_a[count + k] = b_base
-        list_b[count + k] = b_base
-        list_o[count + k] = block_total
-    lax.fori_loop(0, (count + UNROLL - 1) // UNROLL, several, 0)
+    lax.fori_loop(0, plan_ref[0], several, 0)
     if first:
-        whole_store = pltpu.make_async_copy(total.at[pl.ds(0, block_total)], out_ref, out_sem.at[0])
+        whole_store = pltpu.make_async_copy(total.at[pl.ds(0, out_ref.shape[0])], out_ref, out_sem.at[0])
         whole_store.start()
         whole_store.wait()
     else:
@@ -153,18 +185,18 @@
         each_touched(lambda block: store(block).wait())
 
 
-def add_products(cuts, code, place, a_parts, b_parts, before, out_blocks, group_count, slot_count):
+def add_products(cuts, pairs, plan, place, a_parts, b_parts, before, out_blocks, group_count, slot_count):
     source_count, block_size, row_count = len(b_parts) // 2, b_parts[0].shape[-1], cuts[-1] - cuts[0]
-    pairs = code.shape[0]
     first = before is None
     anywhere = pl.BlockSpec(memory_space=pl.ANY)
     scalars = pl.BlockSpec(memory_space=pltpu.SMEM)
-    operands = [code, place, *a_parts, *b_parts] + ([] if first else [before])
+    operands = [plan, place, *a_parts, *b_parts] + ([] if first else [before])
     block_count = source_count * row_count * (1 + group_count) * slot_count
     return pl.pallas_call(
         functools.partial(
             product_kernel,
             cuts=cuts,
+            pairs=pairs,
             source_count=source_count,
             slot_count=slot_count,
             group_count=group_count,
@@ -176,15 +208,12 @@
         scratch_shapes=[
             pltpu.VMEM((block_count, block_size, block_size), jnp.bfloat16),
             pltpu.VMEM((out_blocks + 1, block_size, block_size), jnp.float32),
-            pltpu.SMEM((pairs + UNROLL,), jnp.int32),
-            pltpu.SMEM((pairs + UNROLL,), jnp.int32),
-            pltpu.SMEM((pairs + UNROLL,), jnp.int32),
-            pltpu.SMEM((out_blocks + 1,), jnp.int32),
-            pltpu.SMEM((out_blocks,), jnp.int32),
             pltpu.SemaphoreType.DMA((source_count,)),
             pltpu.SemaphoreType.DMA((2, source_count)),
             pltpu.SemaphoreType.DMA((out_blocks,)),
-        ],
+        ]
+        + first
+        * [pltpu.SMEM((plan_size(pairs, out_blocks),), jnp.int32), pltpu.SMEM((out_blocks,), jnp.int32)],
         input_output_aliases={} if first else {len(operands) - 1: 0},
         compiler_params=pltpu.CompilerParams(vmem_limit_bytes=52 << 20),
         cost_estimate=pl.CostEstimate(
@@ -308,7 +337,7 @@
         code = (rows_q * panel_slots + hit[:, i:j]) * (1 << SHIFT) + result[:, i:j]
         codes.append(jnp.where(hit[:, i:j] >= 0, code, -1).reshape(-1))
 
-    out, parts = None, pieces(1)
+    out, parts, plans = None, pieces(1), codes[:1]
     for q in range(len(gathered)):
         a_parts = cores(held, own_swapped)
         if q + 1 < len(gathered):
@@ -317,11 +346,14 @@
             coming = in_plane(q + 1, arrived[: len(chips)])
             own_swapped = own_swaps(q + 1)
         out = add_products(
-            cuts[q : q + 2], codes[q], place, a_parts, [*b_parts[0], *b_parts[1]], out, out_blocks, group_count, slot_count
+            cuts[q : q + 2], codes[q].shape[0], plans[q], place, a_parts, [*b_parts[0], *b_parts[1]], out, out_blocks, group_count, slot_count
         )
         parts = []
         if q + 2 < len(gathered):
-            out, gathered[q + 2] = after(out, gathered[q + 2])
+            if q == 0:
+                out, *later = after(out, *codes[1:])
+                plans += make_plans(later, place, out_blocks, group_count, slot_count, keep_count)
+            out, gathered[q + 2], *plans = after(out, gathered[q + 2], *plans)
             parts = pieces(q + 2)
         if q + 1 < len(gathered):
             out, *arrived = after(out, *own_swapped, *parts, *coming[1:])

time: 234 us -> 241 us (1.030)
  Pallas kernels: 37.6 us -> 44.4 us
    ppermute x38, waiting for transfers between devices: 99.3 us -> 75.2 us  [send(): return lax.ppermute(value, ('row', 'col'), places)]
    all_gather x2, waiting for transfers between devices: 6.79 us -> 30.5 us  [on_device(): lax.all_gather(x_rest[i * panel_slots:j * panel_slots], 'col')]
    pallas_call x3 -> x4, Pallas kernels: 37.6 us -> 44.4 us  [the longest x3 37 us: add_products(): pl.pallas_call(functools.partial(product_kernel, cuts=cuts, pairs=pairs,...]
    unnamed x38 -> x50, local copies, waits for them, and re-layouts: 4.12 us -> 5.31 us
  transfers between devices with their start and end apart: 41 -> 41, of which waited for: 18 -> 15; matrix products, arithmetic and copies ran while one was open for 10% -> 9% of each run, Pallas kernels for 12% -> 15%
where the time goes in v2:
time: 241 us; the launch traced here: 239 us
  waiting for transfers between devices  109 us (45%)
  Pallas kernels  44.4 us (18%)
  starting transfers between devices  41 us (17%)
  local copies, waits for them, and re-layouts  28 us (12%)
  between operations  13.8 us (6%)
  other arithmetic  2.44 us (1%)
    ppermute x38, waiting for transfers between devices, send(): return lax.ppermute(value, ('row', 'col'), places)  75.2 us
    ppermute x38, starting transfers between devices, send(): return lax.ppermute(value, ('row', 'col'), places)  40.9 us
    pallas_call x3, Pallas kernels, add_products(): pl.pallas_call(functools.partial(product_kernel, cuts=cuts, pairs=pairs,...  37 us
    all_gather x2, waiting for transfers between devices, on_device(): lax.all_gather(x_rest[i * panel_slots:j * panel_slots], 'col')  30.5 us
    squeeze x2, local copies, waits for them, and re-layouts, pieces(): lax.dynamic_index_in_dim(gathered[q], panel ^ offset // group_count, 0, F...  7.76 us
    pallas_call x1, Pallas kernels, make_plans(): pl.pallas_call(functools.partial(plan_kernel, slot_count=slot_count, grou...  7.33 us
    unnamed x50, local copies, waits for them, and re-layouts  5.31 us
    slice x16, local copies, waits for them, and re-layouts, on_device(): tag_parts = [part[-1, :rows_here, :panel_slots] for part in b_parts[1]]  4.91 us
  transfers between devices with their start and end apart: 41, of which 15 were waited for; matrix products, arithmetic and copies ran while one was open for 9% of the time, Pallas kernels for 15%

profile of v2, /device:TPU:0, one launch (start us, length us, event | category | flops | bytes accessed | tf_op | source)
XLA Modules:
  0.0 239.1 jit_solution(12208793415151123105)
XLA Ops:
  6.5 2.4 %slice.60 = bf16[8,2,2,128,128]{4,3,2,1,0:T(8,128)(2,1)} slice(bf16[16,2,2,128,128]{4,3,2,1,0:T(8,128)(2,1)} %param.3), slice={[0:8], [0:2], [0:2], [0:128], [0:128]} | slice | bytes 2097152 | tf_op jit(solution)/shard_map/slice | solution.py:258
  9.1 0.9 slice.78
  10.1 0.4 copy-done.4
  10.5 3.0 %collective-permute-start.3 = (bf16[32,128,128]{2,1,0:T(8,128)(2,1)S(1)}, bf16[32,128,128]{2,1,0:T(8,128)(2,1)}, u32[]{:S(2)}, u32[]{:S(2)}) collective-permute-start(bf16[32,128,128]{2,1,0:T(8,128)(2,1)S(1)} %bitcast.45), channel_id=1, source_target_pairs={{0,16},{1,17},{2,18},{3,19},{4,20},{5,21},{6,22},{7,23},{8,24},{9,... | collective-permute-start | bytes 3145736 | tf_op jit(solution)/shard_map/ppermute | solution.py:245
  13.4 1.5 collective-permute-start.1
  14.9 1.0 slice.62
  16.1 1.3 pad_maximum_fusion.refs_16_
  17.4 0.6 collective-permute-start.9
  18.1 19.4 %collective-permute-done.3.refs_12_ = bf16[32,128,128]{2,1,0:T(8,128)(2,1)} collective-permute-done((bf16[32,128,128]{2,1,0:T(8,128)(2,1)S(1)}, bf16[32,128,128]{2,1,0:T(8,128)(2,1)}, u32[]{:S(2)}, u32[]{:S(2)}) %collective-permute-start.3) | collective-permute-done | bytes 1048608 | tf_op jit(solution)/shard_map/ppermute | solution.py:245
  37.5 2.1 collective-permute-done.1.refs_10_
  39.6 1.5 collective-permute-start.5
  41.1 18.6 %collective-permute-done.9.refs_20_ = bf16[33,128,128]{2,1,0:T(8,128)(2,1)S(1)} collective-permute-done((bf16[33,128,128]{2,1,0:T(8,128)(2,1)S(1)}, bf16[33,128,128]{2,1,0:T(8,128)(2,1)S(1)}, u32[]{:S(2)}, u32[]{:S(2)}) %collective-permute-start.9) | collective-permute-done | bytes 1081376 | tf_op jit(solution)/shard_map/ppermute | solution.py:245
  59.8 2.9 %collective-permute-done.7.refs_18_ = bf16[33,128,128]{2,1,0:T(8,128)(2,1)S(1)} collective-permute-done((bf16[33,128,128]{2,1,0:T(8,128)(2,1)S(1)}, bf16[33,128,128]{2,1,0:T(8,128)(2,1)S(1)}, u32[]{:S(2)}, u32[]{:S(2)}) %collective-permute-start.7) | collective-permute-done | bytes 1081376 | tf_op jit(solution)/shard_map/ppermute | solution.py:245
  62.8 0.5 collective-permute-start.4
  63.3 20.4 %collective-permute-done.5.refs_14_ = bf16[32,128,128]{2,1,0:T(8,128)(2,1)S(1)} collective-permute-done((bf16[32,128,128]{2,1,0:T(8,128)(2,1)}, bf16[32,128,128]{2,1,0:T(8,128)(2,1)S(1)}, u32[]{:S(2)}, u32[]{:S(2)}) %collective-permute-start.5) | collective-permute-done | bytes 1048608 | tf_op jit(solution)/shard_map/ppermute | solution.py:245
  83.7 2.9 %collective-permute-done.2.refs_11_ = bf16[32,128,128]{2,1,0:T(8,128)(2,1)S(1)} collective-permute-done((bf16[32,128,128]{2,1,0:T(8,128)(2,1)}, bf16[32,128,128]{2,1,0:T(8,128)(2,1)S(1)}, u32[]{:S(2)}, u32[]{:S(2)}) %collective-permute-start.2) | collective-permute-done | bytes 1048608 | tf_op jit(solution)/shard_map/ppermute | solution.py:245
  86.6 0.9 copy-done.15
  87.6 0.4 copy-done.9
  88.0 1.0 copy-done.10
  88.9 3.7 %all-gather.7.cloned.1.call-done = bf16[128,128,128]{2,1,0:T(8,128)(2,1)} async-done(((bf16[32,128,128]{2,1,0:T(8,128)(2,1)}), bf16[128,128,128]{2,1,0:T(8,128)(2,1)}) %all-gather.7.cloned.1.call-update) | async-done | bytes 4194320 | tf_op jit(solution)/shard_map/all_gather | solution.py:260
  92.6 1.8 slice.77
  94.5 4.4 %dynamic-slice_bitcast_fusion = (bf16[32,128,128]{2,1,0:T(8,128)(2,1)}, bf16[32,128,128]{2,1,0:T(8,128)(2,1)}, bf16[32,128,128]{2,1,0:T(8,128)(2,1)}, bf16[32,128,128]{2,1,0:T(8,128)(2,1)}) fusion(bf16[4,32,128,128]{3,2,1,0:T(8,128)(2,1)} %bitcast.48, s32[]{:T(128)S(6)} %select_n.99, s32[]{:T(128)S(6)} %select_n.98, s32[]{:T(128)S(6)} %select_n.97, ...), kind=kLoop, calls=%fused_computation.1 | loop fusion | bytes 8388624 | tf_op jit(solution)/shard_map/jit(dynamic_index_in_dim)/squeeze | solution.py:297
  98.9 5.3 %collective-permute-start.19 = (bf16[32,128,128]{2,1,0:T(8,128)(2,1)}, bf16[32,128,128]{2,1,0:T(8,128)(2,1)}, u32[]{:S(2)}, u32[]{:S(2)}) collective-permute-start(bf16[32,128,128]{2,1,0:T(8,128)(2,1)} %get-tuple-element.107), channel_id=1, source_target_pairs={{0,24},{1,25},{2,26},{4,28},{5,29},{6,30},{8,16},{9,17},{11,19},{1... | collective-permute-start | bytes 3145736 | tf_op jit(solution)/shard_map/ppermute | solution.py:245
  104.2 2.5 %collective-permute-start.18 = (bf16[32,128,128]{2,1,0:T(8,128)(2,1)}, bf16[32,128,128]{2,1,0:T(8,128)(2,1)}, u32[]{:S(2)}, u32[]{:S(2)}) collective-permute-start(bf16[32,128,128]{2,1,0:T(8,128)(2,1)} %get-tuple-element.108), channel_id=1, source_target_pairs={{0,16},{1,17},{3,19},{4,20},{5,21},{7,23},{8,24},{9,25},{10,26},{1... | collective-permute-start | bytes 3145736 | tf_op jit(solution)/shard_map/ppermute | solution.py:245
  106.7 1.3 collective-permute-start.17
  108.2 0.7 slice.69
  109.0 0.7 slice.64
  109.8 0.7 slice.65
  110.6 0.7 slice.66
  111.5 0.7 slice.68
  112.4 0.7 slice.79
  113.2 1.3 collective-permute-start.15
  114.7 1.1 collective-permute-done.15
  115.8 1.3 collective-permute-start.14
  117.1 30.5 %all-gather.11.cloned.1.call-done = bf16[80,128,128]{2,1,0:T(8,128)(2,1)} async-done(((bf16[20,128,128]{2,1,0:T(8,128)(2,1)}), bf16[80,128,128]{2,1,0:T(8,128)(2,1)}) %all-gather.11.cloned.1.call-update) | async-done | bytes 2621456 | tf_op jit(solution)/shard_map/all_gather | solution.py:262
  147.6 3.4 %dynamic-slice_bitcast_fusion.4 = (bf16[20,128,128]{2,1,0:T(8,128)(2,1)}, bf16[20,128,128]{2,1,0:T(8,128)(2,1)}, bf16[20,128,128]{2,1,0:T(8,128)(2,1)}, bf16[20,128,128]{2,1,0:T(8,128)(2,1)}) fusion(bf16[4,20,128,128]{3,2,1,0:T(8,128)(2,1)} %bitcast.50, s32[]{:T(128)S(6)} %select_n.99, s32[]{:T(128)S(6)} %select_n.98, s32[]{:T(128)S(6)} %select_n.97, ...), kind=kLoop, calls=%fused_computation.5 | loop fusion | bytes 5242896 | tf_op jit(solution)/shard_map/jit(dynamic_index_in_dim)/squeeze | solution.py:297
  150.9 2.8 %collective-permute-start.13 = (bf16[8,16,2]{1,0,2:T(8,128)(2,1)S(1)}, bf16[8,16,2]{1,0,2:T(8,128)(2,1)S(1)}, u32[]{:S(2)}, u32[]{:S(2)}) collective-permute-start(bf16[8,16,2]{1,0,2:T(8,128)(2,1)S(1)} %dynamic-slice_bitcast_fusion.12), channel_id=1, source_target_pairs={{0,3},{4,7},{9,8},{13,12},{18,17},{22,21},{27,26},{31,30}} | collective-permute-start | bytes 1544 | tf_op jit(solution)/shard_map/ppermute | solution.py:245
  153.8 1.2 collective-permute-done.13
  155.1 0.6 collective-permute-start.23
  155.8 0.5 collective-permute-start.21
  156.5 0.6 select_reduce_fusion
  157.4 0.7 reshape.126.refs_1_
  158.1 3.5 %collective-permute-done.23.refs_15_ = bf16[32,128,128]{2,1,0:T(8,128)(2,1)S(1)} collective-permute-done((bf16[32,128,128]{2,1,0:T(8,128)(2,1)S(1)}, bf16[32,128,128]{2,1,0:T(8,128)(2,1)S(1)}, u32[]{:S(2)}, u32[]{:S(2)}) %collective-permute-start.23) | collective-permute-done | bytes 1048608 | tf_op jit(solution)/shard_map/ppermute | solution.py:245
  161.6 4.8 %collective-permute-start.25 = (bf16[20,128,128]{2,1,0:T(8,128)(2,1)}, bf16[20,128,128]{2,1,0:T(8,128)(2,1)S(1)}, u32[]{:S(2)}, u32[]{:S(2)}) collective-permute-start(bf16[20,128,128]{2,1,0:T(8,128)(2,1)} %get-tuple-element.88), channel_id=1, source_target_pairs={{0,8},{2,10},{3,11},{4,12},{6,14},{7,15},{9,1},{10,2},{11,3},{13,5... | collective-permute-start | bytes 1966088 | tf_op jit(solution)/shard_map/ppermute | solution.py:245
  166.5 1.3 collective-permute-start.26
  167.8 3.3 %collective-permute-start.27 = (bf16[20,128,128]{2,1,0:T(8,128)(2,1)}, bf16[20,128,128]{2,1,0:T(8,128)(2,1)S(1)}, u32[]{:S(2)}, u32[]{:S(2)}) collective-permute-start(bf16[20,128,128]{2,1,0:T(8,128)(2,1)} %get-tuple-element.90), channel_id=1, source_target_pairs={{0,24},{1,25},{2,26},{4,28},{5,29},{6,30},{8,16},{9,17},{11,19},{1... | collective-permute-start | bytes 1966088 | tf_op jit(solution)/shard_map/ppermute | solution.py:245
  171.4 0.7 reshape.122.refs_0_
  172.5 17.2 %shard_map.37.refs_24_ = f32[192,128,128]{2,1,0:T(8,128)} custom-call(s32[256]{0:T(256)S(1)} %reshape.118.plan_ref, s32[3]{0:T(128)S(1)} %pad_add_fusion.place_ref, bf16[4,32,128,128]{3,2,1,0:T(8,128)(2,1)} %bitcast.49, bf16[32,128,128]{2,1,0:T(8,128)(2,1)S(1)} %collective-permute-done.17.refs_1_, bf16[32,128,128]{2,1,0:T(8,128)(2,1)} %collective-permute-done.18.refs_2_, ...), custom_call_target="tpu_custom_call" | custom-call | flops 1073741824 | bytes 37748736 | tf_op jit(solution)/shard_map/pallas_call | solution.py:195
  189.7 7.3 %shard_map.38 = (s32[700]{0:T(1024)}, s32[508]{0:T(512)}) custom-call(s32[3]{0:T(128)} %copy-done, s32[160]{0:T(256)} %reshape.122.refs_0_, s32[96]{0:T(128)} %reshape.126.refs_1_), custom_call_target="tpu_custom_call" | custom-call | bytes 1024 | tf_op jit(solution)/shard_map/pallas_call | solution.py:65
  197.1 1.5 dynamic-slice_bitcast_fusion.8
  198.7 0.5 collective-permute-start.29
  199.3 1.9 collective-permute-start.32
  201.2 2.2 collective-permute-start.33
  203.4 3.1 %collective-permute-start.34 = (bf16[12,128,128]{2,1,0:T(8,128)(2,1)S(1)}, bf16[12,128,128]{2,1,0:T(8,128)(2,1)S(1)}, u32[]{:S(2)}, u32[]{:S(2)}) collective-permute-start(bf16[12,128,128]{2,1,0:T(8,128)(2,1)S(1)} %get-tuple-element.101), channel_id=1, source_target_pairs={{0,24},{1,25},{2,26},{4,28},{5,29},{6,30},{8,16},{9,17},{11,19},{1... | collective-permute-start | bytes 1179656 | tf_op jit(solution)/shard_map/ppermute | solution.py:245
  206.7 0.7 copy-done.19
  207.4 0.9 copy-done.20
  208.3 11.6 %shard_map.39.refs_24_ = f32[192,128,128]{2,1,0:T(8,128)} custom-call(s32[700]{0:T(1024)S(1)} %copy-done.2, s32[3]{0:T(128)S(1)} %copy-done.1, bf16[4,20,128,128]{3,2,1,0:T(8,128)(2,1)} %bitcast.51, bf16[20,128,128]{2,1,0:T(8,128)(2,1)S(1)} %collective-permute-done.25.refs_1_, ...), custom_call_target="tpu_custom_call", output_to_operand_aliasing={{}: (26, {})} | custom-call | flops 671088640 | bytes 33030144 | tf_op jit(solution)/shard_map/pallas_call | solution.py:195
  219.9 0.6 collective-permute-done.33.refs_2_
  220.6 0.5 collective-permute-start.36
  221.2 1.1 collective-permute-done.35.refs_5_
  222.3 0.6 collective-permute-done.36.refs_6_
  222.9 0.6 collective-permute-done.37.refs_7_
  223.6 0.7 copy-done.22
  224.4 8.2 %shard_map.40 = f32[192,128,128]{2,1,0:T(8,128)} custom-call(s32[508]{0:T(512)S(1)} %copy-done.3, s32[3]{0:T(128)S(1)} %copy-done.1, bf16[4,12,128,128]{3,2,1,0:T(8,128)(2,1)} %bitcast.53, bf16[12,128,128]{2,1,0:T(8,128)(2,1)S(1)} %collective-permute-done.32.refs_1_, ...), custom_call_target="tpu_custom_call", output_to_operand_aliasing={{}: (26, {})} | custom-call | flops 402653184 | bytes 29884416 | tf_op jit(solution)/shard_map/pallas_call | solution.py:195
  (130 shorter events, 3.6 us)
Async XLA Ops:
  6.5 2.5 %copy-start.17 = (bf16[16,2,2,128,128]{4,3,2,1,0:T(8,128)(2,1)S(1)}, bf16[16,2,2,128,128]{4,3,2,1,0:T(8,128)(2,1)}, u32[]{:S(2)}) copy-start(bf16[16,2,2,128,128]{4,3,2,1,0:T(8,128)(2,1)} %param.3) | copy-start | bytes 6291460
  6.5 86.1 %all-gather.7.cloned.1.call-start = ((), (), s32[]{:S(2)}) async-start(), calls=%async_computation | async-start | bytes 5242880 | tf_op jit(solution)/shard_map/all_gather | solution.py:260
  9.0 1.5 copy-start.4
  9.0 138.5 %all-gather.11.cloned.1.call-start = ((), (), s32[]{:S(2)}) async-start(), calls=%async_computation.2 | async-start | bytes 3276800 | tf_op jit(solution)/shard_map/all_gather | solution.py:262
  10.0 6.0 %copy-start.23 = (s32[16,2,2]{0,2,1:T(2,128)S(1)}, s32[16,2,2]{0,2,1:T(2,128)}, u32[]{:S(2)}) copy-start(s32[16,2,2]{0,2,1:T(2,128)} %param.4) | copy-start | bytes 772
  10.0 187.1 %all-gather.9.cloned.1.call-start = ((), (), s32[]{:S(2)}) async-start(), calls=%async_computation.1 | async-start | bytes 1966080 | tf_op jit(solution)/shard_map/all_gather | solution.py:262
  10.5 27.1 %collective-permute-start.3 = (bf16[32,128,128]{2,1,0:T(8,128)(2,1)S(1)}, bf16[32,128,128]{2,1,0:T(8,128)(2,1)}, u32[]{:S(2)}, u32[]{:S(2)}) collective-permute-start(bf16[32,128,128]{2,1,0:T(8,128)(2,1)S(1)} %bitcast.45), channel_id=1, source_target_pairs={{0,16},{1,17},{2,18},{3,19},{4,20},{5,21},{6,22},{7,23},{8,24},{9,... | collective-permute-start | bytes 3145736 | tf_op jit(solution)/shard_map/ppermute | solution.py:245
  13.4 26.2 %collective-permute-start.1 = (bf16[32,128,128]{2,1,0:T(8,128)(2,1)S(1)}, bf16[32,128,128]{2,1,0:T(8,128)(2,1)}, u32[]{:S(2)}, u32[]{:S(2)}) collective-permute-start(bf16[32,128,128]{2,1,0:T(8,128)(2,1)S(1)} %bitcast.46), channel_id=1, source_target_pairs={{0,8},{1,9},{2,10},{3,11},{4,12},{5,13},{6,14},{7,15},{8,0},{9,1},... | collective-permute-start | bytes 3145736 | tf_op jit(solution)/shard_map/ppermute | solution.py:245
  17.4 91.5 %copy-start.5 = (bf16[33,128,128]{2,1,0:T(8,128)(2,1)}, bf16[33,128,128]{2,1,0:T(8,128)(2,1)S(1)}, u32[]{:S(2)}) copy-start(bf16[33,128,128]{2,1,0:T(8,128)(2,1)S(1)} %pad_maximum_fusion.refs_16_) | copy-start | bytes 3244036
  17.4 42.3 %collective-permute-start.9 = (bf16[33,128,128]{2,1,0:T(8,128)(2,1)S(1)}, bf16[33,128,128]{2,1,0:T(8,128)(2,1)S(1)}, u32[]{:S(2)}, u32[]{:S(2)}) collective-permute-start(bf16[33,128,128]{2,1,0:T(8,128)(2,1)S(1)} %pad_maximum_fusion.refs_16_), channel_id=1, source_target_pairs={{0,16},{1,17},{2,18},{3,19},{4,20},{5,21},{6,22},{7,23},{8,24},{9,... | collective-permute-start | bytes 3244040 | tf_op jit(solution)/shard_map/ppermute | solution.py:245
  18.0 44.7 %collective-permute-start.7 = (bf16[33,128,128]{2,1,0:T(8,128)(2,1)S(1)}, bf16[33,128,128]{2,1,0:T(8,128)(2,1)S(1)}, u32[]{:S(2)}, u32[]{:S(2)}) collective-permute-start(bf16[33,128,128]{2,1,0:T(8,128)(2,1)S(1)} %pad_maximum_fusion.refs_16_), channel_id=1, source_target_pairs={{0,8},{1,9},{2,10},{3,11},{4,12},{5,13},{6,14},{7,15},{8,0},{9,1},... | collective-permute-start | bytes 3244040 | tf_op jit(solution)/shard_map/ppermute | solution.py:245
  18.1 44.7 %collective-permute-start.6 = (bf16[33,128,128]{2,1,0:T(8,128)(2,1)S(1)}, bf16[33,128,128]{2,1,0:T(8,128)(2,1)S(1)}, u32[]{:S(2)}, u32[]{:S(2)}) collective-permute-start(bf16[33,128,128]{2,1,0:T(8,128)(2,1)S(1)} %pad_maximum_fusion.refs_16_), channel_id=1, source_target_pairs={{0,4},{1,5},{2,6},{3,7},{4,0},{5,1},{6,2},{7,3},{8,12},{9,13},{10,... | collective-permute-start | bytes 3244040 | tf_op jit(solution)/shard_map/ppermute | solution.py:245
  37.5 25.2 %collective-permute-start = (bf16[32,128,128]{2,1,0:T(8,128)(2,1)S(1)}, bf16[32,128,128]{2,1,0:T(8,128)(2,1)S(1)}, u32[]{:S(2)}, u32[]{:S(2)}) collective-permute-start(bf16[32,128,128]{2,1,0:T(8,128)(2,1)S(1)} %bitcast.47), channel_id=1, source_target_pairs={{0,4},{1,5},{2,6},{3,7},{4,0},{5,1},{6,2},{7,3},{8,12},{9,13},{10,... | collective-permute-start | bytes 3145736 | tf_op jit(solution)/shard_map/ppermute | solution.py:245
  39.6 44.1 %collective-permute-start.5 = (bf16[32,128,128]{2,1,0:T(8,128)(2,1)}, bf16[32,128,128]{2,1,0:T(8,128)(2,1)S(1)}, u32[]{:S(2)}, u32[]{:S(2)}) collective-permute-start(bf16[32,128,128]{2,1,0:T(8,128)(2,1)} %collective-permute-done.3.refs_12_), channel_id=1, source_target_pairs={{0,8},{1,9},{2,10},{3,11},{4,12},{5,13},{6,14},{7,15},{8,0},{9,1},... | collective-permute-start | bytes 3145736 | tf_op jit(solution)/shard_map/ppermute | solution.py:245
  59.8 51.6 %copy-start.6 = (bf16[33,128,128]{2,1,0:T(8,128)(2,1)}, bf16[33,128,128]{2,1,0:T(8,128)(2,1)S(1)}, u32[]{:S(2)}) copy-start(bf16[33,128,128]{2,1,0:T(8,128)(2,1)S(1)} %collective-permute-done.9.refs_20_) | copy-start | bytes 3244036
  59.8 26.8 %collective-permute-start.10 = (bf16[33,128,128]{2,1,0:T(8,128)(2,1)S(1)}, bf16[33,128,128]{2,1,0:T(8,128)(2,1)S(1)}, u32[]{:S(2)}, u32[]{:S(2)}) collective-permute-start(bf16[33,128,128]{2,1,0:T(8,128)(2,1)S(1)} %collective-permute-done.9.refs_20_), channel_id=1, source_target_pairs={{0,4},{1,5},{2,6},{3,7},{4,0},{5,1},{6,2},{7,3},{8,12},{9,13},{10,... | collective-permute-start | bytes 3244040 | tf_op jit(solution)/shard_map/ppermute | solution.py:245
  62.7 23.9 %copy-start.7 = (bf16[33,128,128]{2,1,0:T(8,128)(2,1)}, bf16[33,128,128]{2,1,0:T(8,128)(2,1)S(1)}, u32[]{:S(2)}) copy-start(bf16[33,128,128]{2,1,0:T(8,128)(2,1)S(1)} %collective-permute-done.7.refs_18_) | copy-start | bytes 3244036
  62.7 23.9 %collective-permute-start.11 = (bf16[33,128,128]{2,1,0:T(8,128)(2,1)S(1)}, bf16[33,128,128]{2,1,0:T(8,128)(2,1)S(1)}, u32[]{:S(2)}, u32[]{:S(2)}) collective-permute-start(bf16[33,128,128]{2,1,0:T(8,128)(2,1)S(1)} %collective-permute-done.7.refs_18_), channel_id=1, source_target_pairs={{0,16},{1,17},{2,18},{3,19},{4,20},{5,21},{6,22},{7,23},{8,24},{9,... | collective-permute-start | bytes 3244040 | tf_op jit(solution)/shard_map/ppermute | solution.py:245
  62.7 23.9 %copy-start.11 = (bf16[32,128,128]{2,1,0:T(8,128)(2,1)}, bf16[32,128,128]{2,1,0:T(8,128)(2,1)S(1)}, u32[]{:S(2)}) copy-start(bf16[32,128,128]{2,1,0:T(8,128)(2,1)S(1)} %collective-permute-done.refs_9_) | copy-start | bytes 3145732
  62.7 26.2 %collective-permute-start.8 = (bf16[33,128,128]{2,1,0:T(8,128)(2,1)S(1)}, bf16[33,128,128]{2,1,0:T(8,128)(2,1)}, u32[]{:S(2)}, u32[]{:S(2)}) collective-permute-start(bf16[33,128,128]{2,1,0:T(8,128)(2,1)S(1)} %collective-permute-done.7.refs_18_), channel_id=1, source_target_pairs={{0,4},{1,5},{2,6},{3,7},{4,0},{5,1},{6,2},{7,3},{8,12},{9,13},{10,... | collective-permute-start | bytes 3244040 | tf_op jit(solution)/shard_map/ppermute | solution.py:245
  62.8 23.8 %copy-start.8 = (bf16[33,128,128]{2,1,0:T(8,128)(2,1)}, bf16[33,128,128]{2,1,0:T(8,128)(2,1)S(1)}, u32[]{:S(2)}) copy-start(bf16[33,128,128]{2,1,0:T(8,128)(2,1)S(1)} %collective-permute-done.6.refs_17_) | copy-start | bytes 3244036
  62.8 20.9 %collective-permute-start.4 = (bf16[32,128,128]{2,1,0:T(8,128)(2,1)}, bf16[32,128,128]{2,1,0:T(8,128)(2,1)S(1)}, u32[]{:S(2)}, u32[]{:S(2)}) collective-permute-start(bf16[32,128,128]{2,1,0:T(8,128)(2,1)} %collective-permute-done.3.refs_12_), channel_id=1, source_target_pairs={{0,4},{1,5},{2,6},{3,7},{4,0},{5,1},{6,2},{7,3},{8,12},{9,13},{10,... | collective-permute-start | bytes 3145736 | tf_op jit(solution)/shard_map/ppermute | solution.py:245
  83.7 2.9 %copy-start.12 = (bf16[32,128,128]{2,1,0:T(8,128)(2,1)}, bf16[32,128,128]{2,1,0:T(8,128)(2,1)S(1)}, u32[]{:S(2)}) copy-start(bf16[32,128,128]{2,1,0:T(8,128)(2,1)S(1)} %collective-permute-done.5.refs_14_) | copy-start | bytes 3145732
  83.7 2.9 %collective-permute-start.2 = (bf16[32,128,128]{2,1,0:T(8,128)(2,1)}, bf16[32,128,128]{2,1,0:T(8,128)(2,1)S(1)}, u32[]{:S(2)}, u32[]{:S(2)}) collective-permute-start(bf16[32,128,128]{2,1,0:T(8,128)(2,1)} %collective-permute-done.1.refs_10_), channel_id=1, source_target_pairs={{0,4},{1,5},{2,6},{3,7},{4,0},{5,1},{6,2},{7,3},{8,12},{9,13},{10,... | collective-permute-start | bytes 3145736 | tf_op jit(solution)/shard_map/ppermute | solution.py:245
  83.7 2.9 %copy-start.14 = (bf16[32,128,128]{2,1,0:T(8,128)(2,1)}, bf16[32,128,128]{2,1,0:T(8,128)(2,1)S(1)}, u32[]{:S(2)}) copy-start(bf16[32,128,128]{2,1,0:T(8,128)(2,1)S(1)} %collective-permute-done.4.refs_13_) | copy-start | bytes 3145732
  86.6 1.0 copy-start.15
  86.6 1.4 copy-start.9
  88.0 1.0 copy-start.10
  92.6 19.7 %collective-permute-start.12 = (bf16[33,128,128]{2,1,0:T(8,128)(2,1)}, bf16[33,128,128]{2,1,0:T(8,128)(2,1)}, u32[]{:S(2)}, u32[]{:S(2)}) collective-permute-start(bf16[33,128,128]{2,1,0:T(8,128)(2,1)} %copy-done.10), channel_id=1, source_target_pairs={{0,4},{1,5},{2,6},{3,7},{4,0},{5,1},{6,2},{7,3},{8,12},{9,13},{10,... | collective-permute-start | bytes 3244040 | tf_op jit(solution)/shard_map/ppermute | solution.py:245
  98.9 56.1 %collective-permute-start.19 = (bf16[32,128,128]{2,1,0:T(8,128)(2,1)}, bf16[32,128,128]{2,1,0:T(8,128)(2,1)}, u32[]{:S(2)}, u32[]{:S(2)}) collective-permute-start(bf16[32,128,128]{2,1,0:T(8,128)(2,1)} %get-tuple-element.107), channel_id=1, source_target_pairs={{0,24},{1,25},{2,26},{4,28},{5,29},{6,30},{8,16},{9,17},{11,19},{1... | collective-permute-start | bytes 3145736 | tf_op jit(solution)/shard_map/ppermute | solution.py:245
  104.2 51.4 %collective-permute-start.18 = (bf16[32,128,128]{2,1,0:T(8,128)(2,1)}, bf16[32,128,128]{2,1,0:T(8,128)(2,1)}, u32[]{:S(2)}, u32[]{:S(2)}) collective-permute-start(bf16[32,128,128]{2,1,0:T(8,128)(2,1)} %get-tuple-element.108), channel_id=1, source_target_pairs={{0,16},{1,17},{3,19},{4,20},{5,21},{7,23},{8,24},{9,25},{10,26},{1... | collective-permute-start | bytes 3145736 | tf_op jit(solution)/shard_map/ppermute | solution.py:245
  106.7 49.0 %collective-permute-start.17 = (bf16[32,128,128]{2,1,0:T(8,128)(2,1)}, bf16[32,128,128]{2,1,0:T(8,128)(2,1)S(1)}, u32[]{:S(2)}, u32[]{:S(2)}) collective-permute-start(bf16[32,128,128]{2,1,0:T(8,128)(2,1)} %get-tuple-element.109), channel_id=1, source_target_pairs={{0,8},{2,10},{3,11},{4,12},{6,14},{7,15},{9,1},{10,2},{11,3},{13,5... | collective-permute-start | bytes 3145736 | tf_op jit(solution)/shard_map/ppermute | solution.py:245
  108.0 47.6 %collective-permute-start.16 = (bf16[32,128,128]{2,1,0:T(8,128)(2,1)}, bf16[32,128,128]{2,1,0:T(8,128)(2,1)}, u32[]{:S(2)}, u32[]{:S(2)}) collective-permute-start(bf16[32,128,128]{2,1,0:T(8,128)(2,1)} %get-tuple-element.110), channel_id=1, source_target_pairs={{0,4},{1,5},{2,6},{3,7},{4,0},{5,1},{6,2},{7,3},{8,12},{9,13},{10,... | collective-permute-start | bytes 3145736 | tf_op jit(solution)/shard_map/ppermute | solution.py:245
  108.2 64.3 %copy-start = (s32[3]{0:T(128)}, s32[3]{0:T(128)S(1)}, u32[]{:S(2)}) copy-start(s32[3]{0:T(128)S(1)} %pad_add_fusion.place_ref) | copy-start | bytes 40
  113.2 2.6 %collective-permute-start.15 = (bf16[8,16,2]{1,0,2:T(8,128)(2,1)S(1)}, bf16[8,16,2]{1,0,2:T(8,128)(2,1)S(1)}, u32[]{:S(2)}, u32[]{:S(2)}) collective-permute-start(bf16[8,16,2]{1,0,2:T(8,128)(2,1)S(1)} %dynamic-slice_bitcast_fusion.12), channel_id=1, source_target_pairs={{0,1},{4,5},{9,10},{13,14},{18,19},{22,23},{27,24},{31,28}} | collective-permute-start | bytes 1544 | tf_op jit(solution)/shard_map/ppermute | solution.py:245
  115.8 35.1 %collective-permute-start.14 = (bf16[8,16,2]{1,0,2:T(8,128)(2,1)S(1)}, bf16[8,16,2]{1,0,2:T(8,128)(2,1)S(1)}, u32[]{:S(2)}, u32[]{:S(2)}) collective-permute-start(bf16[8,16,2]{1,0,2:T(8,128)(2,1)S(1)} %dynamic-slice_bitcast_fusion.12), channel_id=1, source_target_pairs={{0,2},{4,6},{9,11},{13,15},{18,16},{22,20},{27,25},{31,29}} | collective-permute-start | bytes 1544 | tf_op jit(solution)/shard_map/ppermute | solution.py:245
  147.6 7.5 %copy-start.13 = (bf16[32,128,128]{2,1,0:T(8,128)(2,1)S(1)}, bf16[32,128,128]{2,1,0:T(8,128)(2,1)}, u32[]{:S(2)}) copy-start(bf16[32,128,128]{2,1,0:T(8,128)(2,1)} %copy-done.12) | copy-start | bytes 3145732
  147.6 8.9 %copy-start.24 = (s32[96,2]{0,1:T(2,128)S(1)}, s32[96,2]{0,1:T(2,128)}, u32[]{:S(2)}) copy-start(s32[96,2]{0,1:T(2,128)} %param.5) | copy-start | bytes 2308
  150.9 4.1 %collective-permute-start.13 = (bf16[8,16,2]{1,0,2:T(8,128)(2,1)S(1)}, bf16[8,16,2]{1,0,2:T(8,128)(2,1)S(1)}, u32[]{:S(2)}, u32[]{:S(2)}) collective-permute-start(bf16[8,16,2]{1,0,2:T(8,128)(2,1)S(1)} %dynamic-slice_bitcast_fusion.12), channel_id=1, source_target_pairs={{0,3},{4,7},{9,8},{13,12},{18,17},{22,21},{27,26},{31,30}} | collective-permute-start | bytes 1544 | tf_op jit(solution)/shard_map/ppermute | solution.py:245
  155.0 43.6 %collective-permute-start.24 = (bf16[20,128,128]{2,1,0:T(8,128)(2,1)}, bf16[20,128,128]{2,1,0:T(8,128)(2,1)}, u32[]{:S(2)}, u32[]{:S(2)}) collective-permute-start(bf16[20,128,128]{2,1,0:T(8,128)(2,1)} %get-tuple-element.114), channel_id=1, source_target_pairs={{0,4},{1,5},{2,6},{3,7},{4,0},{5,1},{6,2},{7,3},{8,12},{9,13},{10,... | collective-permute-start | bytes 1966088 | tf_op jit(solution)/shard_map/ppermute | solution.py:245
  155.1 6.6 %collective-permute-start.23 = (bf16[32,128,128]{2,1,0:T(8,128)(2,1)S(1)}, bf16[32,128,128]{2,1,0:T(8,128)(2,1)S(1)}, u32[]{:S(2)}, u32[]{:S(2)}) collective-permute-start(bf16[32,128,128]{2,1,0:T(8,128)(2,1)S(1)} %copy-done.13), channel_id=1, source_target_pairs={{0,4},{1,5},{2,6},{3,7},{4,0},{5,1},{6,2},{7,3},{8,12},{9,13},{10,... | collective-permute-start | bytes 3145736 | tf_op jit(solution)/shard_map/ppermute | solution.py:245
  155.7 10.8 %collective-permute-start.20 = (bf16[32,128,128]{2,1,0:T(8,128)(2,1)S(1)}, bf16[32,128,128]{2,1,0:T(8,128)(2,1)}, u32[]{:S(2)}, u32[]{:S(2)}) collective-permute-start(bf16[32,128,128]{2,1,0:T(8,128)(2,1)S(1)} %collective-permute-done.17.refs_1_), channel_id=1, source_target_pairs={{0,4},{1,5},{2,6},{3,7},{4,0},{5,1},{6,2},{7,3},{8,12},{9,13},{10,... | collective-permute-start | bytes 3145736 | tf_op jit(solution)/shard_map/ppermute | solution.py:245
  155.8 12.0 %collective-permute-start.21 = (bf16[32,128,128]{2,1,0:T(8,128)(2,1)}, bf16[32,128,128]{2,1,0:T(8,128)(2,1)}, u32[]{:S(2)}, u32[]{:S(2)}) collective-permute-start(bf16[32,128,128]{2,1,0:T(8,128)(2,1)} %collective-permute-done.18.refs_2_), channel_id=1, source_target_pairs={{0,4},{1,5},{2,6},{3,7},{4,0},{5,1},{6,2},{7,3},{8,12},{9,13},{10,... | collective-permute-start | bytes 3145736 | tf_op jit(solution)/shard_map/ppermute | solution.py:245
  156.2 16.2 %collective-permute-start.22 = (bf16[32,128,128]{2,1,0:T(8,128)(2,1)}, bf16[32,128,128]{2,1,0:T(8,128)(2,1)}, u32[]{:S(2)}, u32[]{:S(2)}) collective-permute-start(bf16[32,128,128]{2,1,0:T(8,128)(2,1)} %collective-permute-done.19.refs_3_), channel_id=1, source_target_pairs={{0,4},{1,5},{2,6},{3,7},{4,0},{5,1},{6,2},{7,3},{8,12},{9,13},{10,... | collective-permute-start | bytes 3145736 | tf_op jit(solution)/shard_map/ppermute | solution.py:245
  161.6 4.8 %copy-start.16 = (bf16[32,128,128]{2,1,0:T(8,128)(2,1)}, bf16[32,128,128]{2,1,0:T(8,128)(2,1)S(1)}, u32[]{:S(2)}) copy-start(bf16[32,128,128]{2,1,0:T(8,128)(2,1)S(1)} %collective-permute-done.23.refs_15_) | copy-start | bytes 3145732
  161.6 37.0 %collective-permute-start.25 = (bf16[20,128,128]{2,1,0:T(8,128)(2,1)}, bf16[20,128,128]{2,1,0:T(8,128)(2,1)S(1)}, u32[]{:S(2)}, u32[]{:S(2)}) collective-permute-start(bf16[20,128,128]{2,1,0:T(8,128)(2,1)} %get-tuple-element.88), channel_id=1, source_target_pairs={{0,8},{2,10},{3,11},{4,12},{6,14},{7,15},{9,1},{10,2},{11,3},{13,5... | collective-permute-start | bytes 1966088 | tf_op jit(solution)/shard_map/ppermute | solution.py:245
  166.5 32.2 %collective-permute-start.26 = (bf16[20,128,128]{2,1,0:T(8,128)(2,1)}, bf16[20,128,128]{2,1,0:T(8,128)(2,1)S(1)}, u32[]{:S(2)}, u32[]{:S(2)}) collective-permute-start(bf16[20,128,128]{2,1,0:T(8,128)(2,1)} %get-tuple-element.89), channel_id=1, source_target_pairs={{0,16},{1,17},{3,19},{4,20},{5,21},{7,23},{8,24},{9,25},{10,26},{1... | collective-permute-start | bytes 1966088 | tf_op jit(solution)/shard_map/ppermute | solution.py:245
  167.8 30.8 %collective-permute-start.27 = (bf16[20,128,128]{2,1,0:T(8,128)(2,1)}, bf16[20,128,128]{2,1,0:T(8,128)(2,1)S(1)}, u32[]{:S(2)}, u32[]{:S(2)}) collective-permute-start(bf16[20,128,128]{2,1,0:T(8,128)(2,1)} %get-tuple-element.90), channel_id=1, source_target_pairs={{0,24},{1,25},{2,26},{4,28},{5,29},{6,30},{8,16},{9,17},{11,19},{1... | collective-permute-start | bytes 1966088 | tf_op jit(solution)/shard_map/ppermute | solution.py:245
  197.1 11.2 %copy-start.1 = (s32[3]{0:T(128)S(1)}, s32[3]{0:T(128)}, u32[]{:S(2)}) copy-start(s32[3]{0:T(128)} %copy-done) | copy-start | bytes 40
  197.1 11.2 %copy-start.2 = (s32[700]{0:T(1024)S(1)}, s32[700]{0:T(1024)}, u32[]{:S(2)}) copy-start(s32[700]{0:T(1024)} %get-tuple-element.86.plan_ref) | copy-start | bytes 8404
  198.6 4.8 %collective-permute-start.28 = (bf16[20,128,128]{2,1,0:T(8,128)(2,1)S(1)}, bf16[20,128,128]{2,1,0:T(8,128)(2,1)S(1)}, u32[]{:S(2)}, u32[]{:S(2)}) collective-permute-start(bf16[20,128,128]{2,1,0:T(8,128)(2,1)S(1)} %collective-permute-done.25.refs_1_), channel_id=1, source_target_pairs={{0,4},{1,5},{2,6},{3,7},{4,0},{5,1},{6,2},{7,3},{8,12},{9,13},{10,... | collective-permute-start | bytes 1966088 | tf_op jit(solution)/shard_map/ppermute | solution.py:245
  198.7 7.8 %collective-permute-start.29 = (bf16[20,128,128]{2,1,0:T(8,128)(2,1)S(1)}, bf16[20,128,128]{2,1,0:T(8,128)(2,1)S(1)}, u32[]{:S(2)}, u32[]{:S(2)}) collective-permute-start(bf16[20,128,128]{2,1,0:T(8,128)(2,1)S(1)} %collective-permute-done.26.refs_2_), channel_id=1, source_target_pairs={{0,4},{1,5},{2,6},{3,7},{4,0},{5,1},{6,2},{7,3},{8,12},{9,13},{10,... | collective-permute-start | bytes 1966088 | tf_op jit(solution)/shard_map/ppermute | solution.py:245
  199.2 7.4 %collective-permute-start.30 = (bf16[20,128,128]{2,1,0:T(8,128)(2,1)S(1)}, bf16[20,128,128]{2,1,0:T(8,128)(2,1)S(1)}, u32[]{:S(2)}, u32[]{:S(2)}) collective-permute-start(bf16[20,128,128]{2,1,0:T(8,128)(2,1)S(1)} %collective-permute-done.27.refs_3_), channel_id=1, source_target_pairs={{0,4},{1,5},{2,6},{3,7},{4,0},{5,1},{6,2},{7,3},{8,12},{9,13},{10,... | collective-permute-start | bytes 1966088 | tf_op jit(solution)/shard_map/ppermute | solution.py:245
  199.3 20.6 %collective-permute-start.32 = (bf16[12,128,128]{2,1,0:T(8,128)(2,1)S(1)}, bf16[12,128,128]{2,1,0:T(8,128)(2,1)S(1)}, u32[]{:S(2)}, u32[]{:S(2)}) collective-permute-start(bf16[12,128,128]{2,1,0:T(8,128)(2,1)S(1)} %get-tuple-element.99), channel_id=1, source_target_pairs={{0,8},{2,10},{3,11},{4,12},{6,14},{7,15},{9,1},{10,2},{11,3},{13,5... | collective-permute-start | bytes 1179656 | tf_op jit(solution)/shard_map/ppermute | solution.py:245
  201.2 19.4 %collective-permute-start.33 = (bf16[12,128,128]{2,1,0:T(8,128)(2,1)S(1)}, bf16[12,128,128]{2,1,0:T(8,128)(2,1)S(1)}, u32[]{:S(2)}, u32[]{:S(2)}) collective-permute-start(bf16[12,128,128]{2,1,0:T(8,128)(2,1)S(1)} %get-tuple-element.100), channel_id=1, source_target_pairs={{0,16},{1,17},{3,19},{4,20},{5,21},{7,23},{8,24},{9,25},{10,26},{1... | collective-permute-start | bytes 1179656 | tf_op jit(solution)/shard_map/ppermute | solution.py:245
  203.4 3.3 %copy-start.18 = (bf16[20,128,128]{2,1,0:T(8,128)(2,1)}, bf16[20,128,128]{2,1,0:T(8,128)(2,1)S(1)}, u32[]{:S(2)}) copy-start(bf16[20,128,128]{2,1,0:T(8,128)(2,1)S(1)} %collective-permute-done.28.refs_5_) | copy-start | bytes 1966084
  203.4 17.2 %collective-permute-start.34 = (bf16[12,128,128]{2,1,0:T(8,128)(2,1)S(1)}, bf16[12,128,128]{2,1,0:T(8,128)(2,1)S(1)}, u32[]{:S(2)}, u32[]{:S(2)}) collective-permute-start(bf16[12,128,128]{2,1,0:T(8,128)(2,1)S(1)} %get-tuple-element.101), channel_id=1, source_target_pairs={{0,24},{1,25},{2,26},{4,28},{5,29},{6,30},{8,16},{9,17},{11,19},{1... | collective-permute-start | bytes 1179656 | tf_op jit(solution)/shard_map/ppermute | solution.py:245
  206.6 0.9 copy-start.19
  206.6 17.8 %copy-start.3 = (s32[508]{0:T(512)S(1)}, s32[508]{0:T(512)}, u32[]{:S(2)}) copy-start(s32[508]{0:T(512)} %get-tuple-element.84.plan_ref) | copy-start | bytes 6100
  206.6 14.0 %collective-permute-start.31 = (bf16[12,128,128]{2,1,0:T(8,128)(2,1)S(1)}, bf16[12,128,128]{2,1,0:T(8,128)(2,1)S(1)}, u32[]{:S(2)}, u32[]{:S(2)}) collective-permute-start(bf16[12,128,128]{2,1,0:T(8,128)(2,1)S(1)} %get-tuple-element.115), channel_id=1, source_target_pairs={{0,4},{1,5},{2,6},{3,7},{4,0},{5,1},{6,2},{7,3},{8,12},{9,13},{10,... | collective-permute-start | bytes 1179656 | tf_op jit(solution)/shard_map/ppermute | solution.py:245
  207.4 0.9 copy-start.20
  220.6 1.7 collective-permute-start.35
  220.6 2.3 collective-permute-start.36
  221.1 2.3 collective-permute-start.37
  (2 other events, 1.5 us)
Sparse Core Ops, SparseCore 0:
  9.1 83.4 all-gather.6
  94.2 53.3 all-gather.10
  149.1 35.9 all-gather.8

commit v3 on v2

--- a/solution.py
+++ b/solution.py
@@ -320,7 +320,7 @@
     for hop in range(1, n_col):
         pairs = [((r, r // group_count), (r, (r // group_count + hop) % n_col)) for r in range(n_row)]
         a_cols = jnp.where((col - panel) % n_col == hop, send(group_columns, pairs), a_cols)
-    a_cols, *arrived = after(a_cols, *own_swapped, *held)
+    a_cols, gathered[1], *arrived = after(a_cols, gathered[1], *own_swapped, *held)
     own_swapped, held = arrived[: group_count - 1], arrived[group_count - 1 :]
     a_cols, b_cols = a_cols.astype(jnp.int32), columns.astype(jnp.int32)
     b_cols = b_cols + width_g * lax.broadcasted_iota(jnp.int32, columns.shape, 2)

time: 241 us -> 236 us (0.979)
  waiting for transfers between devices: 109 us -> 105 us
    all_gather x2, waiting for transfers between devices: 30.5 us -> 26.7 us  [on_device(): lax.all_gather(x_rest[i * panel_slots:j * panel_slots], 'col')]
    unnamed x50 -> x46, local copies, waits for them, and re-layouts: 5.31 us -> 5.3 us
  transfers between devices with their start and end apart: 41 -> 41, of which waited for: 15 -> 16; matrix products, arithmetic and copies ran while one was open for 9% -> 10% of each run, Pallas kernels for 15% -> 16%
where the time goes in v3:
time: 236 us; the launch traced here: 235 us
  waiting for transfers between devices  105 us (44%)
  Pallas kernels  45.4 us (19%)
  starting transfers between devices  41.1 us (17%)
  local copies, waits for them, and re-layouts  27.9 us (12%)
  between operations  13.7 us (6%)
  other arithmetic  2.44 us (1%)
    ppermute x38, waiting for transfers between devices, send(): return lax.ppermute(value, ('row', 'col'), places)  74.1 us
    ppermute x38, starting transfers between devices, send(): return lax.ppermute(value, ('row', 'col'), places)  41 us
    pallas_call x3, Pallas kernels, add_products(): pl.pallas_call(functools.partial(product_kernel, cuts=cuts, pairs=pairs,...  38.1 us
    all_gather x2, waiting for transfers between devices, on_device(): lax.all_gather(x_rest[i * panel_slots:j * panel_slots], 'col')  26.7 us
    squeeze x2, local copies, waits for them, and re-layouts, pieces(): lax.dynamic_index_in_dim(gathered[q], panel ^ offset // group_count, 0, F...  7.66 us
    pallas_call x1, Pallas kernels, make_plans(): pl.pallas_call(functools.partial(plan_kernel, slot_count=slot_count, grou...  7.33 us
    unnamed x46, local copies, waits for them, and re-layouts  5.3 us
    slice x16, local copies, waits for them, and re-layouts, on_device(): tag_parts = [part[-1, :rows_here, :panel_slots] for part in b_parts[1]]  4.89 us
  transfers between devices with their start and end apart: 41, of which 16 were waited for; matrix products, arithmetic and copies ran while one was open for 10% of the time, Pallas kernels for 16%

profile of v3, /device:TPU:0, one launch (start us, length us, event | category | flops | bytes accessed | tf_op | source)
XLA Modules:
  0.0 235.1 jit_solution(14704929047796673900)
XLA Ops:
  6.5 2.5 %slice.60 = bf16[8,2,2,128,128]{4,3,2,1,0:T(8,128)(2,1)} slice(bf16[16,2,2,128,128]{4,3,2,1,0:T(8,128)(2,1)} %param.3), slice={[0:8], [0:2], [0:2], [0:128], [0:128]} | slice | bytes 2097152 | tf_op jit(solution)/shard_map/slice | solution.py:258
  9.1 0.9 slice.71
  10.1 0.4 copy-done.4
  10.5 3.0 %collective-permute-start.3 = (bf16[32,128,128]{2,1,0:T(8,128)(2,1)S(1)}, bf16[32,128,128]{2,1,0:T(8,128)(2,1)}, u32[]{:S(2)}, u32[]{:S(2)}) collective-permute-start(bf16[32,128,128]{2,1,0:T(8,128)(2,1)S(1)} %bitcast.45), channel_id=1, source_target_pairs={{0,16},{1,17},{2,18},{3,19},{4,20},{5,21},{6,22},{7,23},{8,24},{9,... | collective-permute-start | bytes 3145736 | tf_op jit(solution)/shard_map/ppermute | solution.py:245
  13.5 1.5 collective-permute-start.1
  14.9 1.0 slice.62
  16.1 1.3 pad_maximum_fusion.refs_16_
  17.4 0.6 collective-permute-start.9
  18.1 19.4 %collective-permute-done.3.refs_12_ = bf16[32,128,128]{2,1,0:T(8,128)(2,1)} collective-permute-done((bf16[32,128,128]{2,1,0:T(8,128)(2,1)S(1)}, bf16[32,128,128]{2,1,0:T(8,128)(2,1)}, u32[]{:S(2)}, u32[]{:S(2)}) %collective-permute-start.3) | collective-permute-done | bytes 1048608 | tf_op jit(solution)/shard_map/ppermute | solution.py:245
  37.5 2.1 collective-permute-done.1.refs_10_
  39.6 1.5 collective-permute-start.5
  41.1 18.6 %collective-permute-done.9.refs_20_ = bf16[33,128,128]{2,1,0:T(8,128)(2,1)S(1)} collective-permute-done((bf16[33,128,128]{2,1,0:T(8,128)(2,1)S(1)}, bf16[33,128,128]{2,1,0:T(8,128)(2,1)S(1)}, u32[]{:S(2)}, u32[]{:S(2)}) %collective-permute-start.9) | collective-permute-done | bytes 1081376 | tf_op jit(solution)/shard_map/ppermute | solution.py:245
  59.8 2.9 %collective-permute-done.7.refs_18_ = bf16[33,128,128]{2,1,0:T(8,128)(2,1)S(1)} collective-permute-done((bf16[33,128,128]{2,1,0:T(8,128)(2,1)S(1)}, bf16[33,128,128]{2,1,0:T(8,128)(2,1)S(1)}, u32[]{:S(2)}, u32[]{:S(2)}) %collective-permute-start.7) | collective-permute-done | bytes 1081376 | tf_op jit(solution)/shard_map/ppermute | solution.py:245
  62.8 0.5 collective-permute-start.4
  63.3 20.4 %collective-permute-done.5.refs_14_ = bf16[32,128,128]{2,1,0:T(8,128)(2,1)S(1)} collective-permute-done((bf16[32,128,128]{2,1,0:T(8,128)(2,1)}, bf16[32,128,128]{2,1,0:T(8,128)(2,1)S(1)}, u32[]{:S(2)}, u32[]{:S(2)}) %collective-permute-start.5) | collective-permute-done | bytes 1048608 | tf_op jit(solution)/shard_map/ppermute | solution.py:245
  83.7 2.9 %collective-permute-done.2.refs_11_ = bf16[32,128,128]{2,1,0:T(8,128)(2,1)S(1)} collective-permute-done((bf16[32,128,128]{2,1,0:T(8,128)(2,1)}, bf16[32,128,128]{2,1,0:T(8,128)(2,1)S(1)}, u32[]{:S(2)}, u32[]{:S(2)}) %collective-permute-start.2) | collective-permute-done | bytes 1048608 | tf_op jit(solution)/shard_map/ppermute | solution.py:245
  86.7 0.9 copy-done.14
  87.6 0.4 copy-done.9
  88.0 1.0 copy-done.10
  89.0 3.7 %all-gather.7.cloned.1.call-done = bf16[128,128,128]{2,1,0:T(8,128)(2,1)} async-done(((bf16[32,128,128]{2,1,0:T(8,128)(2,1)}), bf16[128,128,128]{2,1,0:T(8,128)(2,1)}) %all-gather.7.cloned.1.call-update) | async-done | bytes 4194320 | tf_op jit(solution)/shard_map/all_gather | solution.py:260
  92.6 1.8 slice.78
  94.5 4.4 %dynamic-slice_bitcast_fusion = (bf16[32,128,128]{2,1,0:T(8,128)(2,1)}, bf16[32,128,128]{2,1,0:T(8,128)(2,1)}, bf16[32,128,128]{2,1,0:T(8,128)(2,1)}, bf16[32,128,128]{2,1,0:T(8,128)(2,1)}) fusion(bf16[4,32,128,128]{3,2,1,0:T(8,128)(2,1)} %bitcast.48, s32[]{:T(128)S(6)} %select_n.99, s32[]{:T(128)S(6)} %select_n.98, s32[]{:T(128)S(6)} %select_n.97, ...), kind=kLoop, calls=%fused_computation.1 | loop fusion | bytes 8388624 | tf_op jit(solution)/shard_map/jit(dynamic_index_in_dim)/squeeze | solution.py:297
  98.9 5.3 %collective-permute-start.19 = (bf16[32,128,128]{2,1,0:T(8,128)(2,1)}, bf16[32,128,128]{2,1,0:T(8,128)(2,1)}, u32[]{:S(2)}, u32[]{:S(2)}) collective-permute-start(bf16[32,128,128]{2,1,0:T(8,128)(2,1)} %get-tuple-element.109), channel_id=1, source_target_pairs={{0,24},{1,25},{2,26},{4,28},{5,29},{6,30},{8,16},{9,17},{11,19},{1... | collective-permute-start | bytes 3145736 | tf_op jit(solution)/shard_map/ppermute | solution.py:245
  104.2 2.5 %collective-permute-start.18 = (bf16[32,128,128]{2,1,0:T(8,128)(2,1)}, bf16[32,128,128]{2,1,0:T(8,128)(2,1)}, u32[]{:S(2)}, u32[]{:S(2)}) collective-permute-start(bf16[32,128,128]{2,1,0:T(8,128)(2,1)} %get-tuple-element.110), channel_id=1, source_target_pairs={{0,16},{1,17},{3,19},{4,20},{5,21},{7,23},{8,24},{9,25},{10,26},{1... | collective-permute-start | bytes 3145736 | tf_op jit(solution)/shard_map/ppermute | solution.py:245
  106.7 1.3 collective-permute-start.17
  108.2 0.7 slice.69
  109.0 0.7 slice.64
  109.7 0.7 slice.65
  110.5 0.7 slice.66
  111.4 0.7 slice.68
  112.3 0.7 slice.79
  113.1 1.3 collective-permute-start.15
  114.5 1.2 collective-permute-done.15
  115.7 1.3 collective-permute-start.14
  117.2 1.1 collective-permute-done.14
  118.3 1.3 collective-permute-start.13
  119.7 1.2 collective-permute-done.13
  121.0 26.6 %all-gather.9.cloned.1.call-done = bf16[80,128,128]{2,1,0:T(8,128)(2,1)} async-done(((bf16[20,128,128]{2,1,0:T(8,128)(2,1)}), bf16[80,128,128]{2,1,0:T(8,128)(2,1)}) %all-gather.9.cloned.1.call-update) | async-done | bytes 2621456 | tf_op jit(solution)/shard_map/all_gather | solution.py:262
  147.6 1.5 collective-permute-done.18.refs_2_
  149.2 0.5 collective-permute-start.21
  149.8 0.6 select_reduce_fusion
  150.9 0.7 reshape.126.refs_1_
  151.6 3.3 %dynamic-slice_bitcast_fusion.4 = (bf16[20,128,128]{2,1,0:T(8,128)(2,1)}, bf16[20,128,128]{2,1,0:T(8,128)(2,1)}, bf16[20,128,128]{2,1,0:T(8,128)(2,1)}, bf16[20,128,128]{2,1,0:T(8,128)(2,1)}) fusion(bf16[4,20,128,128]{3,2,1,0:T(8,128)(2,1)} %bitcast.50, s32[]{:T(128)S(6)} %select_n.99, s32[]{:T(128)S(6)} %select_n.98, s32[]{:T(128)S(6)} %select_n.97, ...), kind=kLoop, calls=%fused_computation.5 | loop fusion | bytes 5242896 | tf_op jit(solution)/shard_map/jit(dynamic_index_in_dim)/squeeze | solution.py:297
  154.9 4.4 %collective-permute-start.25 = (bf16[20,128,128]{2,1,0:T(8,128)(2,1)}, bf16[20,128,128]{2,1,0:T(8,128)(2,1)S(1)}, u32[]{:S(2)}, u32[]{:S(2)}) collective-permute-start(bf16[20,128,128]{2,1,0:T(8,128)(2,1)} %get-tuple-element.90), channel_id=1, source_target_pairs={{0,8},{2,10},{3,11},{4,12},{6,14},{7,15},{9,1},{10,2},{11,3},{13,5... | collective-permute-start | bytes 1966088 | tf_op jit(solution)/shard_map/ppermute | solution.py:245
  159.3 3.4 %collective-permute-start.26 = (bf16[20,128,128]{2,1,0:T(8,128)(2,1)}, bf16[20,128,128]{2,1,0:T(8,128)(2,1)S(1)}, u32[]{:S(2)}, u32[]{:S(2)}) collective-permute-start(bf16[20,128,128]{2,1,0:T(8,128)(2,1)} %get-tuple-element.91), channel_id=1, source_target_pairs={{0,16},{1,17},{3,19},{4,20},{5,21},{7,23},{8,24},{9,25},{10,26},{1... | collective-permute-start | bytes 1966088 | tf_op jit(solution)/shard_map/ppermute | solution.py:245
  162.7 1.9 collective-permute-start.27
  164.9 0.7 reshape.122.refs_0_
  166.0 17.8 %shard_map.37.refs_24_ = f32[192,128,128]{2,1,0:T(8,128)} custom-call(s32[256]{0:T(256)S(1)} %reshape.118.plan_ref, s32[3]{0:T(128)S(1)} %pad_add_fusion.place_ref, bf16[4,32,128,128]{3,2,1,0:T(8,128)(2,1)} %bitcast.49, bf16[32,128,128]{2,1,0:T(8,128)(2,1)S(1)} %collective-permute-done.17.refs_1_, bf16[32,128,128]{2,1,0:T(8,128)(2,1)} %collective-permute-done.18.refs_2_, ...), custom_call_target="tpu_custom_call" | custom-call | flops 1073741824 | bytes 37748736 | tf_op jit(solution)/shard_map/pallas_call | solution.py:195
  183.8 7.3 %shard_map.38 = (s32[700]{0:T(1024)}, s32[508]{0:T(512)}) custom-call(s32[3]{0:T(128)} %copy-done, s32[160]{0:T(256)} %reshape.122.refs_0_, s32[96]{0:T(128)} %reshape.126.refs_1_), custom_call_target="tpu_custom_call" | custom-call | bytes 1024 | tf_op jit(solution)/shard_map/pallas_call | solution.py:65
  191.2 1.5 dynamic-slice_bitcast_fusion.8
  192.9 0.3 collective-permute-start.29
  193.5 2.4 %collective-permute-start.32 = (bf16[12,128,128]{2,1,0:T(8,128)(2,1)S(1)}, bf16[12,128,128]{2,1,0:T(8,128)(2,1)S(1)}, u32[]{:S(2)}, u32[]{:S(2)}) collective-permute-start(bf16[12,128,128]{2,1,0:T(8,128)(2,1)S(1)} %get-tuple-element.101), channel_id=1, source_target_pairs={{0,8},{2,10},{3,11},{4,12},{6,14},{7,15},{9,1},{10,2},{11,3},{13,5... | collective-permute-start | bytes 1179656 | tf_op jit(solution)/shard_map/ppermute | solution.py:245
  195.9 3.1 %collective-permute-start.33 = (bf16[12,128,128]{2,1,0:T(8,128)(2,1)S(1)}, bf16[12,128,128]{2,1,0:T(8,128)(2,1)S(1)}, u32[]{:S(2)}, u32[]{:S(2)}) collective-permute-start(bf16[12,128,128]{2,1,0:T(8,128)(2,1)S(1)} %get-tuple-element.102), channel_id=1, source_target_pairs={{0,16},{1,17},{3,19},{4,20},{5,21},{7,23},{8,24},{9,25},{10,26},{1... | collective-permute-start | bytes 1179656 | tf_op jit(solution)/shard_map/ppermute | solution.py:245
  199.0 3.4 %collective-permute-start.34 = (bf16[12,128,128]{2,1,0:T(8,128)(2,1)S(1)}, bf16[12,128,128]{2,1,0:T(8,128)(2,1)S(1)}, u32[]{:S(2)}, u32[]{:S(2)}) collective-permute-start(bf16[12,128,128]{2,1,0:T(8,128)(2,1)S(1)} %get-tuple-element.103), channel_id=1, source_target_pairs={{0,24},{1,25},{2,26},{4,28},{5,29},{6,30},{8,16},{9,17},{11,19},{1... | collective-permute-start | bytes 1179656 | tf_op jit(solution)/shard_map/ppermute | solution.py:245
  202.5 0.7 copy-done.17
  203.2 0.8 copy-done.18
  204.1 11.5 %shard_map.39.refs_24_ = f32[192,128,128]{2,1,0:T(8,128)} custom-call(s32[700]{0:T(1024)S(1)} %copy-done.2, s32[3]{0:T(128)S(1)} %copy-done.1, bf16[4,20,128,128]{3,2,1,0:T(8,128)(2,1)} %bitcast.51, bf16[20,128,128]{2,1,0:T(8,128)(2,1)S(1)} %collective-permute-done.25.refs_1_, ...), custom_call_target="tpu_custom_call", output_to_operand_aliasing={{}: (26, {})} | custom-call | flops 671088640 | bytes 33030144 | tf_op jit(solution)/shard_map/pallas_call | solution.py:195
  215.6 0.3 collective-permute-done.33.refs_2_
  216.0 0.5 collective-permute-start.36
  216.6 1.1 collective-permute-done.35.refs_5_
  217.7 0.6 collective-permute-done.36.refs_6_
  218.3 0.6 collective-permute-done.37.refs_7_
  219.0 0.7 copy-done.20
  219.8 8.8 %shard_map.40 = f32[192,128,128]{2,1,0:T(8,128)} custom-call(s32[508]{0:T(512)S(1)} %copy-done.3, s32[3]{0:T(128)S(1)} %copy-done.1, bf16[4,12,128,128]{3,2,1,0:T(8,128)(2,1)} %bitcast.53, bf16[12,128,128]{2,1,0:T(8,128)(2,1)S(1)} %collective-permute-done.32.refs_1_, ...), custom_call_target="tpu_custom_call", output_to_operand_aliasing={{}: (26, {})} | custom-call | flops 402653184 | bytes 29884416 | tf_op jit(solution)/shard_map/pallas_call | solution.py:195
  (126 shorter events, 4.1 us)
Async XLA Ops:
  6.5 2.6 %copy-start.15 = (bf16[16,2,2,128,128]{4,3,2,1,0:T(8,128)(2,1)S(1)}, bf16[16,2,2,128,128]{4,3,2,1,0:T(8,128)(2,1)}, u32[]{:S(2)}) copy-start(bf16[16,2,2,128,128]{4,3,2,1,0:T(8,128)(2,1)} %param.3) | copy-start | bytes 6291460
  6.5 86.1 %all-gather.7.cloned.1.call-start = ((), (), s32[]{:S(2)}) async-start(), calls=%async_computation | async-start | bytes 5242880 | tf_op jit(solution)/shard_map/all_gather | solution.py:260
  9.0 1.5 copy-start.4
  9.0 138.5 %all-gather.9.cloned.1.call-start = ((), (), s32[]{:S(2)}) async-start(), calls=%async_computation.1 | async-start | bytes 3276800 | tf_op jit(solution)/shard_map/all_gather | solution.py:262
  10.0 6.0 %copy-start.21 = (s32[16,2,2]{0,2,1:T(2,128)S(1)}, s32[16,2,2]{0,2,1:T(2,128)}, u32[]{:S(2)}) copy-start(s32[16,2,2]{0,2,1:T(2,128)} %param.4) | copy-start | bytes 772
  10.1 181.1 %all-gather.11.cloned.1.call-start = ((), (), s32[]{:S(2)}) async-start(), calls=%async_computation.2 | async-start | bytes 1966080 | tf_op jit(solution)/shard_map/all_gather | solution.py:262
  10.5 27.1 %collective-permute-start.3 = (bf16[32,128,128]{2,1,0:T(8,128)(2,1)S(1)}, bf16[32,128,128]{2,1,0:T(8,128)(2,1)}, u32[]{:S(2)}, u32[]{:S(2)}) collective-permute-start(bf16[32,128,128]{2,1,0:T(8,128)(2,1)S(1)} %bitcast.45), channel_id=1, source_target_pairs={{0,16},{1,17},{2,18},{3,19},{4,20},{5,21},{6,22},{7,23},{8,24},{9,... | collective-permute-start | bytes 3145736 | tf_op jit(solution)/shard_map/ppermute | solution.py:245
  13.5 26.2 %collective-permute-start.1 = (bf16[32,128,128]{2,1,0:T(8,128)(2,1)S(1)}, bf16[32,128,128]{2,1,0:T(8,128)(2,1)}, u32[]{:S(2)}, u32[]{:S(2)}) collective-permute-start(bf16[32,128,128]{2,1,0:T(8,128)(2,1)S(1)} %bitcast.46), channel_id=1, source_target_pairs={{0,8},{1,9},{2,10},{3,11},{4,12},{5,13},{6,14},{7,15},{8,0},{9,1},... | collective-permute-start | bytes 3145736 | tf_op jit(solution)/shard_map/ppermute | solution.py:245
  17.4 91.4 %copy-start.5 = (bf16[33,128,128]{2,1,0:T(8,128)(2,1)}, bf16[33,128,128]{2,1,0:T(8,128)(2,1)S(1)}, u32[]{:S(2)}) copy-start(bf16[33,128,128]{2,1,0:T(8,128)(2,1)S(1)} %pad_maximum_fusion.refs_16_) | copy-start | bytes 3244036
  17.4 42.3 %collective-permute-start.9 = (bf16[33,128,128]{2,1,0:T(8,128)(2,1)S(1)}, bf16[33,128,128]{2,1,0:T(8,128)(2,1)S(1)}, u32[]{:S(2)}, u32[]{:S(2)}) collective-permute-start(bf16[33,128,128]{2,1,0:T(8,128)(2,1)S(1)} %pad_maximum_fusion.refs_16_), channel_id=1, source_target_pairs={{0,16},{1,17},{2,18},{3,19},{4,20},{5,21},{6,22},{7,23},{8,24},{9,... | collective-permute-start | bytes 3244040 | tf_op jit(solution)/shard_map/ppermute | solution.py:245
  18.0 44.7 %collective-permute-start.7 = (bf16[33,128,128]{2,1,0:T(8,128)(2,1)S(1)}, bf16[33,128,128]{2,1,0:T(8,128)(2,1)S(1)}, u32[]{:S(2)}, u32[]{:S(2)}) collective-permute-start(bf16[33,128,128]{2,1,0:T(8,128)(2,1)S(1)} %pad_maximum_fusion.refs_16_), channel_id=1, source_target_pairs={{0,8},{1,9},{2,10},{3,11},{4,12},{5,13},{6,14},{7,15},{8,0},{9,1},... | collective-permute-start | bytes 3244040 | tf_op jit(solution)/shard_map/ppermute | solution.py:245
  18.1 44.7 %collective-permute-start.6 = (bf16[33,128,128]{2,1,0:T(8,128)(2,1)S(1)}, bf16[33,128,128]{2,1,0:T(8,128)(2,1)S(1)}, u32[]{:S(2)}, u32[]{:S(2)}) collective-permute-start(bf16[33,128,128]{2,1,0:T(8,128)(2,1)S(1)} %pad_maximum_fusion.refs_16_), channel_id=1, source_target_pairs={{0,4},{1,5},{2,6},{3,7},{4,0},{5,1},{6,2},{7,3},{8,12},{9,13},{10,... | collective-permute-start | bytes 3244040 | tf_op jit(solution)/shard_map/ppermute | solution.py:245
  37.5 25.2 %collective-permute-start = (bf16[32,128,128]{2,1,0:T(8,128)(2,1)S(1)}, bf16[32,128,128]{2,1,0:T(8,128)(2,1)S(1)}, u32[]{:S(2)}, u32[]{:S(2)}) collective-permute-start(bf16[32,128,128]{2,1,0:T(8,128)(2,1)S(1)} %bitcast.47), channel_id=1, source_target_pairs={{0,4},{1,5},{2,6},{3,7},{4,0},{5,1},{6,2},{7,3},{8,12},{9,13},{10,... | collective-permute-start | bytes 3145736 | tf_op jit(solution)/shard_map/ppermute | solution.py:245
  39.6 44.1 %collective-permute-start.5 = (bf16[32,128,128]{2,1,0:T(8,128)(2,1)}, bf16[32,128,128]{2,1,0:T(8,128)(2,1)S(1)}, u32[]{:S(2)}, u32[]{:S(2)}) collective-permute-start(bf16[32,128,128]{2,1,0:T(8,128)(2,1)} %collective-permute-done.3.refs_12_), channel_id=1, source_target_pairs={{0,8},{1,9},{2,10},{3,11},{4,12},{5,13},{6,14},{7,15},{8,0},{9,1},... | collective-permute-start | bytes 3145736 | tf_op jit(solution)/shard_map/ppermute | solution.py:245
  59.8 51.5 %copy-start.6 = (bf16[33,128,128]{2,1,0:T(8,128)(2,1)}, bf16[33,128,128]{2,1,0:T(8,128)(2,1)S(1)}, u32[]{:S(2)}) copy-start(bf16[33,128,128]{2,1,0:T(8,128)(2,1)S(1)} %collective-permute-done.9.refs_20_) | copy-start | bytes 3244036
  59.8 26.8 %collective-permute-start.10 = (bf16[33,128,128]{2,1,0:T(8,128)(2,1)S(1)}, bf16[33,128,128]{2,1,0:T(8,128)(2,1)S(1)}, u32[]{:S(2)}, u32[]{:S(2)}) collective-permute-start(bf16[33,128,128]{2,1,0:T(8,128)(2,1)S(1)} %collective-permute-done.9.refs_20_), channel_id=1, source_target_pairs={{0,4},{1,5},{2,6},{3,7},{4,0},{5,1},{6,2},{7,3},{8,12},{9,13},{10,... | collective-permute-start | bytes 3244040 | tf_op jit(solution)/shard_map/ppermute | solution.py:245
  62.7 23.9 %copy-start.7 = (bf16[33,128,128]{2,1,0:T(8,128)(2,1)}, bf16[33,128,128]{2,1,0:T(8,128)(2,1)S(1)}, u32[]{:S(2)}) copy-start(bf16[33,128,128]{2,1,0:T(8,128)(2,1)S(1)} %collective-permute-done.7.refs_18_) | copy-start | bytes 3244036
  62.7 23.9 %collective-permute-start.11 = (bf16[33,128,128]{2,1,0:T(8,128)(2,1)S(1)}, bf16[33,128,128]{2,1,0:T(8,128)(2,1)S(1)}, u32[]{:S(2)}, u32[]{:S(2)}) collective-permute-start(bf16[33,128,128]{2,1,0:T(8,128)(2,1)S(1)} %collective-permute-done.7.refs_18_), channel_id=1, source_target_pairs={{0,16},{1,17},{2,18},{3,19},{4,20},{5,21},{6,22},{7,23},{8,24},{9,... | collective-permute-start | bytes 3244040 | tf_op jit(solution)/shard_map/ppermute | solution.py:245
  62.7 23.9 %copy-start.11 = (bf16[32,128,128]{2,1,0:T(8,128)(2,1)}, bf16[32,128,128]{2,1,0:T(8,128)(2,1)S(1)}, u32[]{:S(2)}) copy-start(bf16[32,128,128]{2,1,0:T(8,128)(2,1)S(1)} %collective-permute-done.refs_9_) | copy-start | bytes 3145732
  62.7 26.2 %collective-permute-start.8 = (bf16[33,128,128]{2,1,0:T(8,128)(2,1)S(1)}, bf16[33,128,128]{2,1,0:T(8,128)(2,1)}, u32[]{:S(2)}, u32[]{:S(2)}) collective-permute-start(bf16[33,128,128]{2,1,0:T(8,128)(2,1)S(1)} %collective-permute-done.7.refs_18_), channel_id=1, source_target_pairs={{0,4},{1,5},{2,6},{3,7},{4,0},{5,1},{6,2},{7,3},{8,12},{9,13},{10,... | collective-permute-start | bytes 3244040 | tf_op jit(solution)/shard_map/ppermute | solution.py:245
  62.8 23.8 %copy-start.8 = (bf16[33,128,128]{2,1,0:T(8,128)(2,1)}, bf16[33,128,128]{2,1,0:T(8,128)(2,1)S(1)}, u32[]{:S(2)}) copy-start(bf16[33,128,128]{2,1,0:T(8,128)(2,1)S(1)} %collective-permute-done.6.refs_17_) | copy-start | bytes 3244036
  62.8 20.9 %collective-permute-start.4 = (bf16[32,128,128]{2,1,0:T(8,128)(2,1)}, bf16[32,128,128]{2,1,0:T(8,128)(2,1)S(1)}, u32[]{:S(2)}, u32[]{:S(2)}) collective-permute-start(bf16[32,128,128]{2,1,0:T(8,128)(2,1)} %collective-permute-done.3.refs_12_), channel_id=1, source_target_pairs={{0,4},{1,5},{2,6},{3,7},{4,0},{5,1},{6,2},{7,3},{8,12},{9,13},{10,... | collective-permute-start | bytes 3145736 | tf_op jit(solution)/shard_map/ppermute | solution.py:245
  83.7 2.9 %copy-start.12 = (bf16[32,128,128]{2,1,0:T(8,128)(2,1)}, bf16[32,128,128]{2,1,0:T(8,128)(2,1)S(1)}, u32[]{:S(2)}) copy-start(bf16[32,128,128]{2,1,0:T(8,128)(2,1)S(1)} %collective-permute-done.5.refs_14_) | copy-start | bytes 3145732
  83.7 2.9 %collective-permute-start.2 = (bf16[32,128,128]{2,1,0:T(8,128)(2,1)}, bf16[32,128,128]{2,1,0:T(8,128)(2,1)S(1)}, u32[]{:S(2)}, u32[]{:S(2)}) collective-permute-start(bf16[32,128,128]{2,1,0:T(8,128)(2,1)} %collective-permute-done.1.refs_10_), channel_id=1, source_target_pairs={{0,4},{1,5},{2,6},{3,7},{4,0},{5,1},{6,2},{7,3},{8,12},{9,13},{10,... | collective-permute-start | bytes 3145736 | tf_op jit(solution)/shard_map/ppermute | solution.py:245
  83.7 2.9 %copy-start.13 = (bf16[32,128,128]{2,1,0:T(8,128)(2,1)}, bf16[32,128,128]{2,1,0:T(8,128)(2,1)S(1)}, u32[]{:S(2)}) copy-start(bf16[32,128,128]{2,1,0:T(8,128)(2,1)S(1)} %collective-permute-done.4.refs_13_) | copy-start | bytes 3145732
  86.6 1.0 copy-start.14
  86.6 1.4 copy-start.9
  88.0 1.0 copy-start.10
  92.6 19.7 %collective-permute-start.12 = (bf16[33,128,128]{2,1,0:T(8,128)(2,1)}, bf16[33,128,128]{2,1,0:T(8,128)(2,1)}, u32[]{:S(2)}, u32[]{:S(2)}) collective-permute-start(bf16[33,128,128]{2,1,0:T(8,128)(2,1)} %copy-done.10), channel_id=1, source_target_pairs={{0,4},{1,5},{2,6},{3,7},{4,0},{5,1},{6,2},{7,3},{8,12},{9,13},{10,... | collective-permute-start | bytes 3244040 | tf_op jit(solution)/shard_map/ppermute | solution.py:245
  94.5 55.3 %copy-start.22 = (s32[96,2]{0,1:T(2,128)S(1)}, s32[96,2]{0,1:T(2,128)}, u32[]{:S(2)}) copy-start(s32[96,2]{0,1:T(2,128)} %param.5) | copy-start | bytes 2308
  98.9 48.7 %collective-permute-start.19 = (bf16[32,128,128]{2,1,0:T(8,128)(2,1)}, bf16[32,128,128]{2,1,0:T(8,128)(2,1)}, u32[]{:S(2)}, u32[]{:S(2)}) collective-permute-start(bf16[32,128,128]{2,1,0:T(8,128)(2,1)} %get-tuple-element.109), channel_id=1, source_target_pairs={{0,24},{1,25},{2,26},{4,28},{5,29},{6,30},{8,16},{9,17},{11,19},{1... | collective-permute-start | bytes 3145736 | tf_op jit(solution)/shard_map/ppermute | solution.py:245
  104.2 44.9 %collective-permute-start.18 = (bf16[32,128,128]{2,1,0:T(8,128)(2,1)}, bf16[32,128,128]{2,1,0:T(8,128)(2,1)}, u32[]{:S(2)}, u32[]{:S(2)}) collective-permute-start(bf16[32,128,128]{2,1,0:T(8,128)(2,1)} %get-tuple-element.110), channel_id=1, source_target_pairs={{0,16},{1,17},{3,19},{4,20},{5,21},{7,23},{8,24},{9,25},{10,26},{1... | collective-permute-start | bytes 3145736 | tf_op jit(solution)/shard_map/ppermute | solution.py:245
  106.7 42.4 %collective-permute-start.17 = (bf16[32,128,128]{2,1,0:T(8,128)(2,1)}, bf16[32,128,128]{2,1,0:T(8,128)(2,1)S(1)}, u32[]{:S(2)}, u32[]{:S(2)}) collective-permute-start(bf16[32,128,128]{2,1,0:T(8,128)(2,1)} %get-tuple-element.111), channel_id=1, source_target_pairs={{0,8},{2,10},{3,11},{4,12},{6,14},{7,15},{9,1},{10,2},{11,3},{13,5... | collective-permute-start | bytes 3145736 | tf_op jit(solution)/shard_map/ppermute | solution.py:245
  108.0 41.1 %collective-permute-start.16 = (bf16[32,128,128]{2,1,0:T(8,128)(2,1)}, bf16[32,128,128]{2,1,0:T(8,128)(2,1)}, u32[]{:S(2)}, u32[]{:S(2)}) collective-permute-start(bf16[32,128,128]{2,1,0:T(8,128)(2,1)} %get-tuple-element.112), channel_id=1, source_target_pairs={{0,4},{1,5},{2,6},{3,7},{4,0},{5,1},{6,2},{7,3},{8,12},{9,13},{10,... | collective-permute-start | bytes 3145736 | tf_op jit(solution)/shard_map/ppermute | solution.py:245
  113.1 2.6 %collective-permute-start.15 = (bf16[8,16,2]{1,0,2:T(8,128)(2,1)S(1)}, bf16[8,16,2]{1,0,2:T(8,128)(2,1)S(1)}, u32[]{:S(2)}, u32[]{:S(2)}) collective-permute-start(bf16[8,16,2]{1,0,2:T(8,128)(2,1)S(1)} %dynamic-slice_bitcast_fusion.12), channel_id=1, source_target_pairs={{0,1},{4,5},{9,10},{13,14},{18,19},{22,23},{27,24},{31,28}} | collective-permute-start | bytes 1544 | tf_op jit(solution)/shard_map/ppermute | solution.py:245
  114.5 51.5 %copy-start = (s32[3]{0:T(128)}, s32[3]{0:T(128)S(1)}, u32[]{:S(2)}) copy-start(s32[3]{0:T(128)S(1)} %pad_add_fusion.place_ref) | copy-start | bytes 40
  115.7 2.6 %collective-permute-start.14 = (bf16[8,16,2]{1,0,2:T(8,128)(2,1)S(1)}, bf16[8,16,2]{1,0,2:T(8,128)(2,1)S(1)}, u32[]{:S(2)}, u32[]{:S(2)}) collective-permute-start(bf16[8,16,2]{1,0,2:T(8,128)(2,1)S(1)} %dynamic-slice_bitcast_fusion.12), channel_id=1, source_target_pairs={{0,2},{4,6},{9,11},{13,15},{18,16},{22,20},{27,25},{31,29}} | collective-permute-start | bytes 1544 | tf_op jit(solution)/shard_map/ppermute | solution.py:245
  118.3 2.6 %collective-permute-start.13 = (bf16[8,16,2]{1,0,2:T(8,128)(2,1)S(1)}, bf16[8,16,2]{1,0,2:T(8,128)(2,1)S(1)}, u32[]{:S(2)}, u32[]{:S(2)}) collective-permute-start(bf16[8,16,2]{1,0,2:T(8,128)(2,1)S(1)} %dynamic-slice_bitcast_fusion.12), channel_id=1, source_target_pairs={{0,3},{4,7},{9,8},{13,12},{18,17},{22,21},{27,26},{31,30}} | collective-permute-start | bytes 1544 | tf_op jit(solution)/shard_map/ppermute | solution.py:245
  120.9 38.3 %collective-permute-start.23 = (bf16[32,128,128]{2,1,0:T(8,128)(2,1)}, bf16[32,128,128]{2,1,0:T(8,128)(2,1)}, u32[]{:S(2)}, u32[]{:S(2)}) collective-permute-start(bf16[32,128,128]{2,1,0:T(8,128)(2,1)} %copy-done.12), channel_id=1, source_target_pairs={{0,4},{1,5},{2,6},{3,7},{4,0},{5,1},{6,2},{7,3},{8,12},{9,13},{10,... | collective-permute-start | bytes 3145736 | tf_op jit(solution)/shard_map/ppermute | solution.py:245
  149.1 13.5 %collective-permute-start.20 = (bf16[32,128,128]{2,1,0:T(8,128)(2,1)S(1)}, bf16[32,128,128]{2,1,0:T(8,128)(2,1)}, u32[]{:S(2)}, u32[]{:S(2)}) collective-permute-start(bf16[32,128,128]{2,1,0:T(8,128)(2,1)S(1)} %collective-permute-done.17.refs_1_), channel_id=1, source_target_pairs={{0,4},{1,5},{2,6},{3,7},{4,0},{5,1},{6,2},{7,3},{8,12},{9,13},{10,... | collective-permute-start | bytes 3145736 | tf_op jit(solution)/shard_map/ppermute | solution.py:245
  149.2 15.4 %collective-permute-start.21 = (bf16[32,128,128]{2,1,0:T(8,128)(2,1)}, bf16[32,128,128]{2,1,0:T(8,128)(2,1)}, u32[]{:S(2)}, u32[]{:S(2)}) collective-permute-start(bf16[32,128,128]{2,1,0:T(8,128)(2,1)} %collective-permute-done.18.refs_2_), channel_id=1, source_target_pairs={{0,4},{1,5},{2,6},{3,7},{4,0},{5,1},{6,2},{7,3},{8,12},{9,13},{10,... | collective-permute-start | bytes 3145736 | tf_op jit(solution)/shard_map/ppermute | solution.py:245
  150.5 15.5 %collective-permute-start.22 = (bf16[32,128,128]{2,1,0:T(8,128)(2,1)}, bf16[32,128,128]{2,1,0:T(8,128)(2,1)}, u32[]{:S(2)}, u32[]{:S(2)}) collective-permute-start(bf16[32,128,128]{2,1,0:T(8,128)(2,1)} %collective-permute-done.19.refs_3_), channel_id=1, source_target_pairs={{0,4},{1,5},{2,6},{3,7},{4,0},{5,1},{6,2},{7,3},{8,12},{9,13},{10,... | collective-permute-start | bytes 3145736 | tf_op jit(solution)/shard_map/ppermute | solution.py:245
  154.9 37.8 %collective-permute-start.25 = (bf16[20,128,128]{2,1,0:T(8,128)(2,1)}, bf16[20,128,128]{2,1,0:T(8,128)(2,1)S(1)}, u32[]{:S(2)}, u32[]{:S(2)}) collective-permute-start(bf16[20,128,128]{2,1,0:T(8,128)(2,1)} %get-tuple-element.90), channel_id=1, source_target_pairs={{0,8},{2,10},{3,11},{4,12},{6,14},{7,15},{9,1},{10,2},{11,3},{13,5... | collective-permute-start | bytes 1966088 | tf_op jit(solution)/shard_map/ppermute | solution.py:245
  159.3 33.4 %collective-permute-start.26 = (bf16[20,128,128]{2,1,0:T(8,128)(2,1)}, bf16[20,128,128]{2,1,0:T(8,128)(2,1)S(1)}, u32[]{:S(2)}, u32[]{:S(2)}) collective-permute-start(bf16[20,128,128]{2,1,0:T(8,128)(2,1)} %get-tuple-element.91), channel_id=1, source_target_pairs={{0,16},{1,17},{3,19},{4,20},{5,21},{7,23},{8,24},{9,25},{10,26},{1... | collective-permute-start | bytes 1966088 | tf_op jit(solution)/shard_map/ppermute | solution.py:245
  162.7 30.0 %collective-permute-start.27 = (bf16[20,128,128]{2,1,0:T(8,128)(2,1)}, bf16[20,128,128]{2,1,0:T(8,128)(2,1)S(1)}, u32[]{:S(2)}, u32[]{:S(2)}) collective-permute-start(bf16[20,128,128]{2,1,0:T(8,128)(2,1)} %get-tuple-element.92), channel_id=1, source_target_pairs={{0,24},{1,25},{2,26},{4,28},{5,29},{6,30},{8,16},{9,17},{11,19},{1... | collective-permute-start | bytes 1966088 | tf_op jit(solution)/shard_map/ppermute | solution.py:245
  164.6 28.1 %collective-permute-start.24 = (bf16[20,128,128]{2,1,0:T(8,128)(2,1)}, bf16[20,128,128]{2,1,0:T(8,128)(2,1)}, u32[]{:S(2)}, u32[]{:S(2)}) collective-permute-start(bf16[20,128,128]{2,1,0:T(8,128)(2,1)} %get-tuple-element.116), channel_id=1, source_target_pairs={{0,4},{1,5},{2,6},{3,7},{4,0},{5,1},{6,2},{7,3},{8,12},{9,13},{10,... | collective-permute-start | bytes 1966088 | tf_op jit(solution)/shard_map/ppermute | solution.py:245
  191.1 12.9 %copy-start.1 = (s32[3]{0:T(128)S(1)}, s32[3]{0:T(128)}, u32[]{:S(2)}) copy-start(s32[3]{0:T(128)} %copy-done) | copy-start | bytes 40
  191.2 12.9 %copy-start.2 = (s32[700]{0:T(1024)S(1)}, s32[700]{0:T(1024)}, u32[]{:S(2)}) copy-start(s32[700]{0:T(1024)} %get-tuple-element.87.plan_ref) | copy-start | bytes 8404
  192.7 6.3 %collective-permute-start.28 = (bf16[20,128,128]{2,1,0:T(8,128)(2,1)S(1)}, bf16[20,128,128]{2,1,0:T(8,128)(2,1)S(1)}, u32[]{:S(2)}, u32[]{:S(2)}) collective-permute-start(bf16[20,128,128]{2,1,0:T(8,128)(2,1)S(1)} %collective-permute-done.25.refs_1_), channel_id=1, source_target_pairs={{0,4},{1,5},{2,6},{3,7},{4,0},{5,1},{6,2},{7,3},{8,12},{9,13},{10,... | collective-permute-start | bytes 1966088 | tf_op jit(solution)/shard_map/ppermute | solution.py:245
  192.9 9.4 %collective-permute-start.29 = (bf16[20,128,128]{2,1,0:T(8,128)(2,1)S(1)}, bf16[20,128,128]{2,1,0:T(8,128)(2,1)S(1)}, u32[]{:S(2)}, u32[]{:S(2)}) collective-permute-start(bf16[20,128,128]{2,1,0:T(8,128)(2,1)S(1)} %collective-permute-done.26.refs_2_), channel_id=1, source_target_pairs={{0,4},{1,5},{2,6},{3,7},{4,0},{5,1},{6,2},{7,3},{8,12},{9,13},{10,... | collective-permute-start | bytes 1966088 | tf_op jit(solution)/shard_map/ppermute | solution.py:245
  193.3 9.2 %collective-permute-start.30 = (bf16[20,128,128]{2,1,0:T(8,128)(2,1)S(1)}, bf16[20,128,128]{2,1,0:T(8,128)(2,1)S(1)}, u32[]{:S(2)}, u32[]{:S(2)}) collective-permute-start(bf16[20,128,128]{2,1,0:T(8,128)(2,1)S(1)} %collective-permute-done.27.refs_3_), channel_id=1, source_target_pairs={{0,4},{1,5},{2,6},{3,7},{4,0},{5,1},{6,2},{7,3},{8,12},{9,13},{10,... | collective-permute-start | bytes 1966088 | tf_op jit(solution)/shard_map/ppermute | solution.py:245
  193.5 22.2 %collective-permute-start.32 = (bf16[12,128,128]{2,1,0:T(8,128)(2,1)S(1)}, bf16[12,128,128]{2,1,0:T(8,128)(2,1)S(1)}, u32[]{:S(2)}, u32[]{:S(2)}) collective-permute-start(bf16[12,128,128]{2,1,0:T(8,128)(2,1)S(1)} %get-tuple-element.101), channel_id=1, source_target_pairs={{0,8},{2,10},{3,11},{4,12},{6,14},{7,15},{9,1},{10,2},{11,3},{13,5... | collective-permute-start | bytes 1179656 | tf_op jit(solution)/shard_map/ppermute | solution.py:245
  195.9 20.1 %collective-permute-start.33 = (bf16[12,128,128]{2,1,0:T(8,128)(2,1)S(1)}, bf16[12,128,128]{2,1,0:T(8,128)(2,1)S(1)}, u32[]{:S(2)}, u32[]{:S(2)}) collective-permute-start(bf16[12,128,128]{2,1,0:T(8,128)(2,1)S(1)} %get-tuple-element.102), channel_id=1, source_target_pairs={{0,16},{1,17},{3,19},{4,20},{5,21},{7,23},{8,24},{9,25},{10,26},{1... | collective-permute-start | bytes 1179656 | tf_op jit(solution)/shard_map/ppermute | solution.py:245
  199.0 3.5 %copy-start.16 = (bf16[20,128,128]{2,1,0:T(8,128)(2,1)}, bf16[20,128,128]{2,1,0:T(8,128)(2,1)S(1)}, u32[]{:S(2)}) copy-start(bf16[20,128,128]{2,1,0:T(8,128)(2,1)S(1)} %collective-permute-done.28.refs_5_) | copy-start | bytes 1966084
  199.0 17.0 %collective-permute-start.34 = (bf16[12,128,128]{2,1,0:T(8,128)(2,1)S(1)}, bf16[12,128,128]{2,1,0:T(8,128)(2,1)S(1)}, u32[]{:S(2)}, u32[]{:S(2)}) collective-permute-start(bf16[12,128,128]{2,1,0:T(8,128)(2,1)S(1)} %get-tuple-element.103), channel_id=1, source_target_pairs={{0,24},{1,25},{2,26},{4,28},{5,29},{6,30},{8,16},{9,17},{11,19},{1... | collective-permute-start | bytes 1179656 | tf_op jit(solution)/shard_map/ppermute | solution.py:245
  202.4 0.9 copy-start.17
  202.4 17.4 %copy-start.3 = (s32[508]{0:T(512)S(1)}, s32[508]{0:T(512)}, u32[]{:S(2)}) copy-start(s32[508]{0:T(512)} %get-tuple-element.85.plan_ref) | copy-start | bytes 6100
  202.4 13.6 %collective-permute-start.31 = (bf16[12,128,128]{2,1,0:T(8,128)(2,1)S(1)}, bf16[12,128,128]{2,1,0:T(8,128)(2,1)S(1)}, u32[]{:S(2)}, u32[]{:S(2)}) collective-permute-start(bf16[12,128,128]{2,1,0:T(8,128)(2,1)S(1)} %get-tuple-element.117), channel_id=1, source_target_pairs={{0,4},{1,5},{2,6},{3,7},{4,0},{5,1},{6,2},{7,3},{8,12},{9,13},{10,... | collective-permute-start | bytes 1179656 | tf_op jit(solution)/shard_map/ppermute | solution.py:245
  203.2 0.8 copy-start.18
  216.0 1.7 collective-permute-start.35
  216.0 2.3 collective-permute-start.36
  216.5 2.3 collective-permute-start.37
  218.3 0.8 copy-start.19
  219.0 0.7 copy-start.20
Sparse Core Ops, SparseCore 0:
  9.1 83.4 all-gather.6
  94.2 53.3 all-gather.8
  149.2 36.0 all-gather.10

commit v4 on v3

--- a/solution.py
+++ b/solution.py
@@ -11,7 +11,9 @@
 UNROLL = 8
 
 
-def fill_plan(code_ref, plan_ref, seen, own, group, slot_count, group_count, keep_count, block_total):
+def fill_plan(
+    code_ref, plan_ref, seen, own, group, slot_count, group_count, keep_count, block_total, with_touched=True
+):
     panel_slots = group_count * slot_count
     pairs = code_ref.shape[0]
     size = pairs + UNROLL
@@ -21,7 +23,8 @@
         seen[block] = 0
         return carry
 
-    lax.fori_loop(0, block_total, clear, 0)
+    if with_touched:
+        lax.fori_loop(0, block_total, clear, 0)
 
     def note(at, counts):
         count, touched_count = counts
@@ -30,15 +33,16 @@
         for keep in range(keep_count):
             code = code_ref[at * keep_count + keep]
             block = lax.bitwise_and(code, (1 << SHIFT) - 1)
-            known = jnp.minimum(block, block_total - 1)
             plan_ref[2 + count] = a_at
             plan_ref[2 + size + count] = lax.shift_right_logical(code, SHIFT) + b_base
             plan_ref[2 + 2 * size + count] = block
             count = count + (code >= 0).astype(jnp.int32)
-            fresh = jnp.logical_and(code >= 0, seen[known] == 0)
-            plan_ref[2 + 3 * size + touched_count] = known
-            seen[known] = jnp.where(code >= 0, 1, seen[known])
-            touched_count = touched_count + fresh.astype(jnp.int32)
+            if with_touched:
+                known = jnp.minimum(block, block_total - 1)
+                fresh = jnp.logical_and(code >= 0, seen[known] == 0)
+                plan_ref[2 + 3 * size + touched_count] = known
+                seen[known] = jnp.where(code >= 0, 1, seen[known])
+                touched_count = touched_count + fresh.astype(jnp.int32)
         return count, touched_count
 
     count, touched_count = lax.fori_loop(0, b_base, note, (jnp.int32(0), jnp.int32(0)))
@@ -78,7 +82,7 @@
     )(place, *codes)
 
 
-def product_kernel(plan_ref, place_ref, *refs, cuts, pairs, source_count, slot_count, group_count, first):
+def product_kernel(plan_ref, place_ref, *refs, cuts, pairs, source_count, slot_count, group_count, first, planned):
     chip_count, panel_slots = source_count // group_count, group_count * slot_count
     row0, row_count, pieces = cuts[0], cuts[-1] - cuts[0], list(zip(cuts, cuts[1:]))
     a_refs = []
@@ -90,7 +94,7 @@
         before_ref, refs = refs[0], refs[1:]
     own, group, panel = place_ref[0], place_ref[1], place_ref[2]
     size = pairs + UNROLL
-    if first:
+    if not planned:
         code_ref, plan_ref, seen, refs = plan_ref, refs[-2], refs[-1], refs[:-2]
     out_ref, blocks, total, a_sem, b_sem, out_sem = refs
     a_size, b_size = row_count * slot_count, row_count * panel_slots
@@ -147,9 +151,12 @@
 
     if first:
         total[...] = jnp.zeros_like(total)
+    if not planned:
         keep_count = pairs // (source_count * row_count * slot_count)
-        fill_plan(code_ref, plan_ref, seen, own, group, slot_count, group_count, keep_count, out_ref.shape[0])
-    else:
+        fill_plan(
+            code_ref, plan_ref, seen, own, group, slot_count, group_count, keep_count, out_ref.shape[0], not first
+        )
+    if not first:
         each_touched(lambda block: load(block).start())
 
     for source in range(source_count):
@@ -185,7 +192,7 @@
         each_touched(lambda block: store(block).wait())
 
 
-def add_products(cuts, pairs, plan, place, a_parts, b_parts, before, out_blocks, group_count, slot_count):
+def add_products(cuts, pairs, plan, place, a_parts, b_parts, before, out_blocks, group_count, slot_count, planned):
     source_count, block_size, row_count = len(b_parts) // 2, b_parts[0].shape[-1], cuts[-1] - cuts[0]
     first = before is None
     anywhere = pl.BlockSpec(memory_space=pl.ANY)
@@ -201,6 +208,7 @@
             slot_count=slot_count,
             group_count=group_count,
             first=first,
+            planned=planned,
         ),
         out_shape=jax.ShapeDtypeStruct((out_blocks, block_size, block_size), jnp.float32),
         in_specs=[scalars, scalars] + [anywhere] * (len(operands) - 2),
@@ -212,7 +220,7 @@
             pltpu.SemaphoreType.DMA((2, source_count)),
             pltpu.SemaphoreType.DMA((out_blocks,)),
         ]
-        + first
+        + (not planned)
         * [pltpu.SMEM((plan_size(pairs, out_blocks),), jnp.int32), pltpu.SMEM((out_blocks,), jnp.int32)],
         input_output_aliases={} if first else {len(operands) - 1: 0},
         compiler_params=pltpu.CompilerParams(vmem_limit_bytes=52 << 20),
@@ -258,8 +266,8 @@
     first_part = x_flat[: cuts[1] * panel_slots]
     x_rest, first_part = after(x_flat, first_part)
     gathered = [lax.all_gather(first_part, "col")]
-    for i, j in zip(cuts[1:], cuts[2:]):
-        gathered.append(lax.all_gather(x_rest[i * panel_slots : j * panel_slots], "col"))
+    operands = after(*(x_rest[i * panel_slots : j * panel_slots] for i, j in zip(cuts[1:], cuts[2:])))
+    gathered += [lax.all_gather(operand, "col") for operand in operands]
     tags = x_columns.reshape(rows_here, panel_slots).astype(jnp.bfloat16)
     tags = jnp.pad(tags, ((0, block_size - rows_here), (0, block_size - panel_slots)))
     half = rows_here * panel_slots // 2
@@ -337,7 +345,7 @@
         code = (rows_q * panel_slots + hit[:, i:j]) * (1 << SHIFT) + result[:, i:j]
         codes.append(jnp.where(hit[:, i:j] >= 0, code, -1).reshape(-1))
 
-    out, parts, plans = None, pieces(1), codes[:1]
+    out, parts, plans = None, pieces(1), codes[:-1]
     for q in range(len(gathered)):
         a_parts = cores(held, own_swapped)
         if q + 1 < len(gathered):
@@ -346,13 +354,13 @@
             coming = in_plane(q + 1, arrived[: len(chips)])
             own_swapped = own_swaps(q + 1)
         out = add_products(
-            cuts[q : q + 2], codes[q].shape[0], plans[q], place, a_parts, [*b_parts[0], *b_parts[1]], out, out_blocks, group_count, slot_count
+            cuts[q : q + 2], codes[q].shape[0], plans[q], place, a_parts, [*b_parts[0], *b_parts[1]], out, out_blocks, group_count, slot_count, q + 1 == len(gathered)
         )
         parts = []
         if q + 2 < len(gathered):
             if q == 0:
-                out, *later = after(out, *codes[1:])
-                plans += make_plans(later, place, out_blocks, group_count, slot_count, keep_count)
+                out, later = after(out, codes[-1])
+                plans += make_plans([later], place, out_blocks, group_count, slot_count, keep_count)
             out, gathered[q + 2], *plans = after(out, gathered[q + 2], *plans)
             parts = pieces(q + 2)
         if q + 1 < len(gathered):

time: 236 us -> 235 us (level)
  Pallas kernels: 45.4 us -> 41.6 us
  waiting for transfers between devices: 105 us -> 108 us
    all_gather x2, waiting for transfers between devices: 26.7 us -> 30.1 us  [on_device(): gathered += [lax.all_gather(operand, 'col') for operand in operands]]
    pallas_call x1, Pallas kernels: 7.33 us -> 3.92 us  [make_plans(): pl.pallas_call(functools.partial(plan_kernel, slot_count=slot_count, grou...]
    unnamed x46 -> x44, local copies, waits for them, and re-layouts: 5.3 us -> 5.34 us
  transfers between devices with their start and end apart: 41 -> 41, of which waited for: 16 -> 16; matrix products, arithmetic and copies ran while one was open for 10% -> 9% of each run, Pallas kernels for 16% -> 14%
where the time goes in v4:
time: 235 us; the launch traced here: 234 us
  waiting for transfers between devices  108 us (46%)
  Pallas kernels  41.6 us (18%)
  starting transfers between devices  41.4 us (18%)
  local copies, waits for them, and re-layouts  26.4 us (11%)
  between operations  13.8 us (6%)
  other arithmetic  2.45 us (1%)
    ppermute x38, waiting for transfers between devices, send(): return lax.ppermute(value, ('row', 'col'), places)  75 us
    ppermute x38, starting transfers between devices, send(): return lax.ppermute(value, ('row', 'col'), places)  41.3 us
    pallas_call x3, Pallas kernels, add_products(): pl.pallas_call(functools.partial(product_kernel, cuts=cuts, pairs=pairs,...  37.7 us
    all_gather x2, waiting for transfers between devices, on_device(): gathered += [lax.all_gather(operand, 'col') for operand in operands]  30.1 us
    squeeze x2, local copies, waits for them, and re-layouts, pieces(): lax.dynamic_index_in_dim(gathered[q], panel ^ offset // group_count, 0, F...  7.64 us
    unnamed x44, local copies, waits for them, and re-layouts  5.34 us
    slice x16, local copies, waits for them, and re-layouts, on_device(): tag_parts = [part[-1, :rows_here, :panel_slots] for part in b_parts[1]]  4.9 us
  transfers between devices with their start and end apart: 41, of which 16 were waited for; matrix products, arithmetic and copies ran while one was open for 9% of the time, Pallas kernels for 14%

profile of v4, /device:TPU:0, one launch (start us, length us, event | category | flops | bytes accessed | tf_op | source)
XLA Modules:
  0.0 233.5 jit_solution(4652374842067545172)
XLA Ops:
  6.5 2.5 %slice.60 = bf16[8,2,2,128,128]{4,3,2,1,0:T(8,128)(2,1)} slice(bf16[16,2,2,128,128]{4,3,2,1,0:T(8,128)(2,1)} %param.3), slice={[0:8], [0:2], [0:2], [0:128], [0:128]} | slice | bytes 2097152 | tf_op jit(solution)/shard_map/slice | solution.py:266
  9.1 0.8 slice.72
  9.9 0.9 slice.71
  10.9 0.4 copy-done.3
  11.4 3.0 %collective-permute-start.3 = (bf16[32,128,128]{2,1,0:T(8,128)(2,1)S(1)}, bf16[32,128,128]{2,1,0:T(8,128)(2,1)}, u32[]{:S(2)}, u32[]{:S(2)}) collective-permute-start(bf16[32,128,128]{2,1,0:T(8,128)(2,1)S(1)} %bitcast.45), channel_id=1, source_target_pairs={{0,16},{1,17},{2,18},{3,19},{4,20},{5,21},{6,22},{7,23},{8,24},{9,... | collective-permute-start | bytes 3145736 | tf_op jit(solution)/shard_map/ppermute | solution.py:253
  14.3 1.5 collective-permute-start.1
  15.8 1.0 slice.62
  17.0 1.3 pad_maximum_fusion.refs_16_
  18.3 0.6 collective-permute-start.9
  19.0 19.4 %collective-permute-done.3.refs_12_ = bf16[32,128,128]{2,1,0:T(8,128)(2,1)} collective-permute-done((bf16[32,128,128]{2,1,0:T(8,128)(2,1)S(1)}, bf16[32,128,128]{2,1,0:T(8,128)(2,1)}, u32[]{:S(2)}, u32[]{:S(2)}) %collective-permute-start.3) | collective-permute-done | bytes 1048608 | tf_op jit(solution)/shard_map/ppermute | solution.py:253
  38.4 2.1 collective-permute-done.1.refs_10_
  40.5 1.5 collective-permute-start.5
  42.0 18.6 %collective-permute-done.9.refs_20_ = bf16[33,128,128]{2,1,0:T(8,128)(2,1)S(1)} collective-permute-done((bf16[33,128,128]{2,1,0:T(8,128)(2,1)S(1)}, bf16[33,128,128]{2,1,0:T(8,128)(2,1)S(1)}, u32[]{:S(2)}, u32[]{:S(2)}) %collective-permute-start.9) | collective-permute-done | bytes 1081376 | tf_op jit(solution)/shard_map/ppermute | solution.py:253
  60.7 2.9 %collective-permute-done.7.refs_18_ = bf16[33,128,128]{2,1,0:T(8,128)(2,1)S(1)} collective-permute-done((bf16[33,128,128]{2,1,0:T(8,128)(2,1)S(1)}, bf16[33,128,128]{2,1,0:T(8,128)(2,1)S(1)}, u32[]{:S(2)}, u32[]{:S(2)}) %collective-permute-start.7) | collective-permute-done | bytes 1081376 | tf_op jit(solution)/shard_map/ppermute | solution.py:253
  63.7 0.5 collective-permute-start.4
  64.2 20.4 %collective-permute-done.5.refs_14_ = bf16[32,128,128]{2,1,0:T(8,128)(2,1)S(1)} collective-permute-done((bf16[32,128,128]{2,1,0:T(8,128)(2,1)}, bf16[32,128,128]{2,1,0:T(8,128)(2,1)S(1)}, u32[]{:S(2)}, u32[]{:S(2)}) %collective-permute-start.5) | collective-permute-done | bytes 1048608 | tf_op jit(solution)/shard_map/ppermute | solution.py:253
  84.6 2.9 %collective-permute-done.2.refs_11_ = bf16[32,128,128]{2,1,0:T(8,128)(2,1)S(1)} collective-permute-done((bf16[32,128,128]{2,1,0:T(8,128)(2,1)}, bf16[32,128,128]{2,1,0:T(8,128)(2,1)S(1)}, u32[]{:S(2)}, u32[]{:S(2)}) %collective-permute-start.2) | collective-permute-done | bytes 1048608 | tf_op jit(solution)/shard_map/ppermute | solution.py:253
  87.5 0.9 copy-done.13
  88.4 0.4 copy-done.8
  88.9 1.0 copy-done.9
  89.8 2.8 %all-gather.7.cloned.1.call-done = bf16[128,128,128]{2,1,0:T(8,128)(2,1)} async-done(((bf16[32,128,128]{2,1,0:T(8,128)(2,1)}), bf16[128,128,128]{2,1,0:T(8,128)(2,1)}) %all-gather.7.cloned.1.call-update) | async-done | bytes 4194320 | tf_op jit(solution)/shard_map/all_gather | solution.py:268
  92.8 4.4 %dynamic-slice_bitcast_fusion = (bf16[32,128,128]{2,1,0:T(8,128)(2,1)}, bf16[32,128,128]{2,1,0:T(8,128)(2,1)}, bf16[32,128,128]{2,1,0:T(8,128)(2,1)}, bf16[32,128,128]{2,1,0:T(8,128)(2,1)}) fusion(bf16[4,32,128,128]{3,2,1,0:T(8,128)(2,1)} %bitcast.48, s32[]{:T(128)S(6)} %select_n.99, s32[]{:T(128)S(6)} %select_n.98, s32[]{:T(128)S(6)} %select_n.97, ...), kind=kLoop, calls=%fused_computation.1 | loop fusion | bytes 8388624 | tf_op jit(solution)/shard_map/jit(dynamic_index_in_dim)/squeeze | solution.py:305
  97.1 5.3 %collective-permute-start.19 = (bf16[32,128,128]{2,1,0:T(8,128)(2,1)}, bf16[32,128,128]{2,1,0:T(8,128)(2,1)}, u32[]{:S(2)}, u32[]{:S(2)}) collective-permute-start(bf16[32,128,128]{2,1,0:T(8,128)(2,1)} %get-tuple-element.107), channel_id=1, source_target_pairs={{0,24},{1,25},{2,26},{4,28},{5,29},{6,30},{8,16},{9,17},{11,19},{1... | collective-permute-start | bytes 3145736 | tf_op jit(solution)/shard_map/ppermute | solution.py:253
  102.4 2.5 %collective-permute-start.18 = (bf16[32,128,128]{2,1,0:T(8,128)(2,1)}, bf16[32,128,128]{2,1,0:T(8,128)(2,1)}, u32[]{:S(2)}, u32[]{:S(2)}) collective-permute-start(bf16[32,128,128]{2,1,0:T(8,128)(2,1)} %get-tuple-element.108), channel_id=1, source_target_pairs={{0,16},{1,17},{3,19},{4,20},{5,21},{7,23},{8,24},{9,25},{10,26},{1... | collective-permute-start | bytes 3145736 | tf_op jit(solution)/shard_map/ppermute | solution.py:253
  104.9 1.3 collective-permute-start.17
  106.4 0.7 slice.69
  107.2 0.7 slice.64
  108.0 0.7 slice.65
  108.8 0.7 slice.66
  109.6 0.7 slice.68
  110.5 0.7 slice.79
  111.4 1.3 collective-permute-start.15
  112.8 1.2 collective-permute-done.15
  114.0 1.3 collective-permute-start.14
  115.4 1.1 collective-permute-done.14
  116.6 1.3 collective-permute-start.13
  118.0 1.2 collective-permute-done.13
  119.2 28.4 %all-gather.9.cloned.1.call-done = bf16[80,128,128]{2,1,0:T(8,128)(2,1)} async-done(((bf16[20,128,128]{2,1,0:T(8,128)(2,1)}), bf16[80,128,128]{2,1,0:T(8,128)(2,1)}) %all-gather.9.cloned.1.call-update) | async-done | bytes 2621456 | tf_op jit(solution)/shard_map/all_gather | solution.py:270
  147.7 0.5 collective-permute-start.21
  148.3 0.6 select_reduce_fusion
  149.5 0.6 reshape.122.refs_0_
  150.1 3.3 %dynamic-slice_bitcast_fusion.4 = (bf16[20,128,128]{2,1,0:T(8,128)(2,1)}, bf16[20,128,128]{2,1,0:T(8,128)(2,1)}, bf16[20,128,128]{2,1,0:T(8,128)(2,1)}, bf16[20,128,128]{2,1,0:T(8,128)(2,1)}) fusion(bf16[4,20,128,128]{3,2,1,0:T(8,128)(2,1)} %bitcast.50, s32[]{:T(128)S(6)} %select_n.99, s32[]{:T(128)S(6)} %select_n.98, s32[]{:T(128)S(6)} %select_n.97, ...), kind=kLoop, calls=%fused_computation.5 | loop fusion | bytes 5242896 | tf_op jit(solution)/shard_map/jit(dynamic_index_in_dim)/squeeze | solution.py:305
  153.4 4.1 %collective-permute-start.25 = (bf16[20,128,128]{2,1,0:T(8,128)(2,1)}, bf16[20,128,128]{2,1,0:T(8,128)(2,1)S(1)}, u32[]{:S(2)}, u32[]{:S(2)}) collective-permute-start(bf16[20,128,128]{2,1,0:T(8,128)(2,1)} %get-tuple-element.88), channel_id=1, source_target_pairs={{0,8},{2,10},{3,11},{4,12},{6,14},{7,15},{9,1},{10,2},{11,3},{13,5... | collective-permute-start | bytes 1966088 | tf_op jit(solution)/shard_map/ppermute | solution.py:253
  157.5 3.4 %collective-permute-start.26 = (bf16[20,128,128]{2,1,0:T(8,128)(2,1)}, bf16[20,128,128]{2,1,0:T(8,128)(2,1)S(1)}, u32[]{:S(2)}, u32[]{:S(2)}) collective-permute-start(bf16[20,128,128]{2,1,0:T(8,128)(2,1)} %get-tuple-element.89), channel_id=1, source_target_pairs={{0,16},{1,17},{3,19},{4,20},{5,21},{7,23},{8,24},{9,25},{10,26},{1... | collective-permute-start | bytes 1966088 | tf_op jit(solution)/shard_map/ppermute | solution.py:253
  160.9 1.9 collective-permute-start.27
  163.0 0.2 copy.39
  163.7 16.0 %shard_map.37.refs_24_ = f32[192,128,128]{2,1,0:T(8,128)} custom-call(s32[256]{0:T(256)S(1)} %reshape.118.plan_ref, s32[3]{0:T(128)S(1)} %pad_add_fusion.place_ref, bf16[4,32,128,128]{3,2,1,0:T(8,128)(2,1)} %bitcast.49, bf16[32,128,128]{2,1,0:T(8,128)(2,1)S(1)} %collective-permute-done.17.refs_1_, bf16[32,128,128]{2,1,0:T(8,128)(2,1)} %collective-permute-done.18.refs_2_, ...), custom_call_target="tpu_custom_call" | custom-call | flops 1073741824 | bytes 37748736 | tf_op jit(solution)/shard_map/pallas_call | solution.py:202
  179.7 3.9 %shard_map.38.plan_ref = s32[508]{0:T(512)} custom-call(s32[3]{0:T(128)} %copy-done, s32[96]{0:T(128)} %reshape.122.refs_0_), custom_call_target="tpu_custom_call" | custom-call | bytes 1024 | tf_op jit(solution)/shard_map/pallas_call | solution.py:69
  183.6 1.7 all-gather.11.cloned.1.call-done
  185.3 1.5 dynamic-slice_bitcast_fusion.8
  186.8 2.7 %collective-permute-done.26.refs_2_ = bf16[20,128,128]{2,1,0:T(8,128)(2,1)S(1)} collective-permute-done((bf16[20,128,128]{2,1,0:T(8,128)(2,1)}, bf16[20,128,128]{2,1,0:T(8,128)(2,1)S(1)}, u32[]{:S(2)}, u32[]{:S(2)}) %collective-permute-start.26) | collective-permute-done | bytes 655392 | tf_op jit(solution)/shard_map/ppermute | solution.py:253
  189.5 0.5 collective-permute-start.29
  190.1 3.1 %collective-permute-start.32 = (bf16[12,128,128]{2,1,0:T(8,128)(2,1)S(1)}, bf16[12,128,128]{2,1,0:T(8,128)(2,1)S(1)}, u32[]{:S(2)}, u32[]{:S(2)}) collective-permute-start(bf16[12,128,128]{2,1,0:T(8,128)(2,1)S(1)} %get-tuple-element.99), channel_id=1, source_target_pairs={{0,8},{2,10},{3,11},{4,12},{6,14},{7,15},{9,1},{10,2},{11,3},{13,5... | collective-permute-start | bytes 1179656 | tf_op jit(solution)/shard_map/ppermute | solution.py:253
  193.2 3.6 %collective-permute-start.33 = (bf16[12,128,128]{2,1,0:T(8,128)(2,1)S(1)}, bf16[12,128,128]{2,1,0:T(8,128)(2,1)S(1)}, u32[]{:S(2)}, u32[]{:S(2)}) collective-permute-start(bf16[12,128,128]{2,1,0:T(8,128)(2,1)S(1)} %get-tuple-element.100), channel_id=1, source_target_pairs={{0,16},{1,17},{3,19},{4,20},{5,21},{7,23},{8,24},{9,25},{10,26},{1... | collective-permute-start | bytes 1179656 | tf_op jit(solution)/shard_map/ppermute | solution.py:253
  196.9 2.8 %collective-permute-start.34 = (bf16[12,128,128]{2,1,0:T(8,128)(2,1)S(1)}, bf16[12,128,128]{2,1,0:T(8,128)(2,1)S(1)}, u32[]{:S(2)}, u32[]{:S(2)}) collective-permute-start(bf16[12,128,128]{2,1,0:T(8,128)(2,1)S(1)} %get-tuple-element.101), channel_id=1, source_target_pairs={{0,24},{1,25},{2,26},{4,28},{5,29},{6,30},{8,16},{9,17},{11,19},{1... | collective-permute-start | bytes 1179656 | tf_op jit(solution)/shard_map/ppermute | solution.py:253
  199.8 0.7 copy-done.16
  200.6 0.8 copy-done.17
  201.4 13.5 %shard_map.39.refs_24_ = f32[192,128,128]{2,1,0:T(8,128)} custom-call(s32[160]{0:T(256)S(1)} %reshape.126.plan_ref, s32[3]{0:T(128)S(1)} %copy-done.1, bf16[4,20,128,128]{3,2,1,0:T(8,128)(2,1)} %bitcast.51, bf16[20,128,128]{2,1,0:T(8,128)(2,1)S(1)} %collective-permute-done.25.refs_1_, ...), custom_call_target="tpu_custom_call", output_to_operand_aliasing={{}: (26, {})} | custom-call | flops 671088640 | bytes 33030144 | tf_op jit(solution)/shard_map/pallas_call | solution.py:202
  215.1 0.5 collective-permute-start.36
  215.6 1.1 collective-permute-done.35.refs_5_
  216.8 0.6 collective-permute-done.36.refs_6_
  217.3 0.6 collective-permute-done.37.refs_7_
  218.1 0.7 copy-done.19
  218.9 8.1 %shard_map.40 = f32[192,128,128]{2,1,0:T(8,128)} custom-call(s32[508]{0:T(512)S(1)} %copy-done.2, s32[3]{0:T(128)S(1)} %copy-done.1, bf16[4,12,128,128]{3,2,1,0:T(8,128)(2,1)} %bitcast.53, bf16[12,128,128]{2,1,0:T(8,128)(2,1)S(1)} %collective-permute-done.32.refs_1_, ...), custom_call_target="tpu_custom_call", output_to_operand_aliasing={{}: (26, {})} | custom-call | flops 402653184 | bytes 29884416 | tf_op jit(solution)/shard_map/pallas_call | solution.py:202
  (124 shorter events, 3.6 us)
Async XLA Ops:
  6.5 2.6 %copy-start.14 = (bf16[16,2,2,128,128]{4,3,2,1,0:T(8,128)(2,1)S(1)}, bf16[16,2,2,128,128]{4,3,2,1,0:T(8,128)(2,1)}, u32[]{:S(2)}) copy-start(bf16[16,2,2,128,128]{4,3,2,1,0:T(8,128)(2,1)} %param.3) | copy-start | bytes 6291460
  6.5 86.1 %all-gather.7.cloned.1.call-start = ((), (), s32[]{:S(2)}) async-start(), calls=%async_computation | async-start | bytes 5242880 | tf_op jit(solution)/shard_map/all_gather | solution.py:268
  9.1 138.6 %all-gather.9.cloned.1.call-start = ((), (), s32[]{:S(2)}) async-start(), calls=%async_computation.1 | async-start | bytes 3276800 | tf_op jit(solution)/shard_map/all_gather | solution.py:270
  9.9 1.5 copy-start.3
  10.8 6.0 %copy-start.20 = (s32[16,2,2]{0,2,1:T(2,128)S(1)}, s32[16,2,2]{0,2,1:T(2,128)}, u32[]{:S(2)}) copy-start(s32[16,2,2]{0,2,1:T(2,128)} %param.4) | copy-start | bytes 772
  10.9 174.4 %all-gather.11.cloned.1.call-start = ((), (), s32[]{:S(2)}) async-start(), calls=%async_computation.2 | async-start | bytes 1966080 | tf_op jit(solution)/shard_map/all_gather | solution.py:270
  11.4 27.1 %collective-permute-start.3 = (bf16[32,128,128]{2,1,0:T(8,128)(2,1)S(1)}, bf16[32,128,128]{2,1,0:T(8,128)(2,1)}, u32[]{:S(2)}, u32[]{:S(2)}) collective-permute-start(bf16[32,128,128]{2,1,0:T(8,128)(2,1)S(1)} %bitcast.45), channel_id=1, source_target_pairs={{0,16},{1,17},{2,18},{3,19},{4,20},{5,21},{6,22},{7,23},{8,24},{9,... | collective-permute-start | bytes 3145736 | tf_op jit(solution)/shard_map/ppermute | solution.py:253
  14.3 26.2 %collective-permute-start.1 = (bf16[32,128,128]{2,1,0:T(8,128)(2,1)S(1)}, bf16[32,128,128]{2,1,0:T(8,128)(2,1)}, u32[]{:S(2)}, u32[]{:S(2)}) collective-permute-start(bf16[32,128,128]{2,1,0:T(8,128)(2,1)S(1)} %bitcast.46), channel_id=1, source_target_pairs={{0,8},{1,9},{2,10},{3,11},{4,12},{5,13},{6,14},{7,15},{8,0},{9,1},... | collective-permute-start | bytes 3145736 | tf_op jit(solution)/shard_map/ppermute | solution.py:253
  18.3 88.8 %copy-start.4 = (bf16[33,128,128]{2,1,0:T(8,128)(2,1)}, bf16[33,128,128]{2,1,0:T(8,128)(2,1)S(1)}, u32[]{:S(2)}) copy-start(bf16[33,128,128]{2,1,0:T(8,128)(2,1)S(1)} %pad_maximum_fusion.refs_16_) | copy-start | bytes 3244036
  18.3 42.3 %collective-permute-start.9 = (bf16[33,128,128]{2,1,0:T(8,128)(2,1)S(1)}, bf16[33,128,128]{2,1,0:T(8,128)(2,1)S(1)}, u32[]{:S(2)}, u32[]{:S(2)}) collective-permute-start(bf16[33,128,128]{2,1,0:T(8,128)(2,1)S(1)} %pad_maximum_fusion.refs_16_), channel_id=1, source_target_pairs={{0,16},{1,17},{2,18},{3,19},{4,20},{5,21},{6,22},{7,23},{8,24},{9,... | collective-permute-start | bytes 3244040 | tf_op jit(solution)/shard_map/ppermute | solution.py:253
  18.9 44.7 %collective-permute-start.7 = (bf16[33,128,128]{2,1,0:T(8,128)(2,1)S(1)}, bf16[33,128,128]{2,1,0:T(8,128)(2,1)S(1)}, u32[]{:S(2)}, u32[]{:S(2)}) collective-permute-start(bf16[33,128,128]{2,1,0:T(8,128)(2,1)S(1)} %pad_maximum_fusion.refs_16_), channel_id=1, source_target_pairs={{0,8},{1,9},{2,10},{3,11},{4,12},{5,13},{6,14},{7,15},{8,0},{9,1},... | collective-permute-start | bytes 3244040 | tf_op jit(solution)/shard_map/ppermute | solution.py:253
  19.0 44.7 %collective-permute-start.6 = (bf16[33,128,128]{2,1,0:T(8,128)(2,1)S(1)}, bf16[33,128,128]{2,1,0:T(8,128)(2,1)S(1)}, u32[]{:S(2)}, u32[]{:S(2)}) collective-permute-start(bf16[33,128,128]{2,1,0:T(8,128)(2,1)S(1)} %pad_maximum_fusion.refs_16_), channel_id=1, source_target_pairs={{0,4},{1,5},{2,6},{3,7},{4,0},{5,1},{6,2},{7,3},{8,12},{9,13},{10,... | collective-permute-start | bytes 3244040 | tf_op jit(solution)/shard_map/ppermute | solution.py:253
  38.4 25.2 %collective-permute-start = (bf16[32,128,128]{2,1,0:T(8,128)(2,1)S(1)}, bf16[32,128,128]{2,1,0:T(8,128)(2,1)S(1)}, u32[]{:S(2)}, u32[]{:S(2)}) collective-permute-start(bf16[32,128,128]{2,1,0:T(8,128)(2,1)S(1)} %bitcast.47), channel_id=1, source_target_pairs={{0,4},{1,5},{2,6},{3,7},{4,0},{5,1},{6,2},{7,3},{8,12},{9,13},{10,... | collective-permute-start | bytes 3145736 | tf_op jit(solution)/shard_map/ppermute | solution.py:253
  40.5 44.1 %collective-permute-start.5 = (bf16[32,128,128]{2,1,0:T(8,128)(2,1)}, bf16[32,128,128]{2,1,0:T(8,128)(2,1)S(1)}, u32[]{:S(2)}, u32[]{:S(2)}) collective-permute-start(bf16[32,128,128]{2,1,0:T(8,128)(2,1)} %collective-permute-done.3.refs_12_), channel_id=1, source_target_pairs={{0,8},{1,9},{2,10},{3,11},{4,12},{5,13},{6,14},{7,15},{8,0},{9,1},... | collective-permute-start | bytes 3145736 | tf_op jit(solution)/shard_map/ppermute | solution.py:253
  60.6 48.9 %copy-start.5 = (bf16[33,128,128]{2,1,0:T(8,128)(2,1)}, bf16[33,128,128]{2,1,0:T(8,128)(2,1)S(1)}, u32[]{:S(2)}) copy-start(bf16[33,128,128]{2,1,0:T(8,128)(2,1)S(1)} %collective-permute-done.9.refs_20_) | copy-start | bytes 3244036
  60.6 26.8 %collective-permute-start.10 = (bf16[33,128,128]{2,1,0:T(8,128)(2,1)S(1)}, bf16[33,128,128]{2,1,0:T(8,128)(2,1)S(1)}, u32[]{:S(2)}, u32[]{:S(2)}) collective-permute-start(bf16[33,128,128]{2,1,0:T(8,128)(2,1)S(1)} %collective-permute-done.9.refs_20_), channel_id=1, source_target_pairs={{0,4},{1,5},{2,6},{3,7},{4,0},{5,1},{6,2},{7,3},{8,12},{9,13},{10,... | collective-permute-start | bytes 3244040 | tf_op jit(solution)/shard_map/ppermute | solution.py:253
  63.6 23.9 %copy-start.6 = (bf16[33,128,128]{2,1,0:T(8,128)(2,1)}, bf16[33,128,128]{2,1,0:T(8,128)(2,1)S(1)}, u32[]{:S(2)}) copy-start(bf16[33,128,128]{2,1,0:T(8,128)(2,1)S(1)} %collective-permute-done.7.refs_18_) | copy-start | bytes 3244036
  63.6 23.9 %collective-permute-start.11 = (bf16[33,128,128]{2,1,0:T(8,128)(2,1)S(1)}, bf16[33,128,128]{2,1,0:T(8,128)(2,1)S(1)}, u32[]{:S(2)}, u32[]{:S(2)}) collective-permute-start(bf16[33,128,128]{2,1,0:T(8,128)(2,1)S(1)} %collective-permute-done.7.refs_18_), channel_id=1, source_target_pairs={{0,16},{1,17},{2,18},{3,19},{4,20},{5,21},{6,22},{7,23},{8,24},{9,... | collective-permute-start | bytes 3244040 | tf_op jit(solution)/shard_map/ppermute | solution.py:253
  63.6 23.9 %copy-start.10 = (bf16[32,128,128]{2,1,0:T(8,128)(2,1)}, bf16[32,128,128]{2,1,0:T(8,128)(2,1)S(1)}, u32[]{:S(2)}) copy-start(bf16[32,128,128]{2,1,0:T(8,128)(2,1)S(1)} %collective-permute-done.refs_9_) | copy-start | bytes 3145732
  63.6 26.2 %collective-permute-start.8 = (bf16[33,128,128]{2,1,0:T(8,128)(2,1)S(1)}, bf16[33,128,128]{2,1,0:T(8,128)(2,1)}, u32[]{:S(2)}, u32[]{:S(2)}) collective-permute-start(bf16[33,128,128]{2,1,0:T(8,128)(2,1)S(1)} %collective-permute-done.7.refs_18_), channel_id=1, source_target_pairs={{0,4},{1,5},{2,6},{3,7},{4,0},{5,1},{6,2},{7,3},{8,12},{9,13},{10,... | collective-permute-start | bytes 3244040 | tf_op jit(solution)/shard_map/ppermute | solution.py:253
  63.7 23.8 %copy-start.7 = (bf16[33,128,128]{2,1,0:T(8,128)(2,1)}, bf16[33,128,128]{2,1,0:T(8,128)(2,1)S(1)}, u32[]{:S(2)}) copy-start(bf16[33,128,128]{2,1,0:T(8,128)(2,1)S(1)} %collective-permute-done.6.refs_17_) | copy-start | bytes 3244036
  63.7 20.9 %collective-permute-start.4 = (bf16[32,128,128]{2,1,0:T(8,128)(2,1)}, bf16[32,128,128]{2,1,0:T(8,128)(2,1)S(1)}, u32[]{:S(2)}, u32[]{:S(2)}) collective-permute-start(bf16[32,128,128]{2,1,0:T(8,128)(2,1)} %collective-permute-done.3.refs_12_), channel_id=1, source_target_pairs={{0,4},{1,5},{2,6},{3,7},{4,0},{5,1},{6,2},{7,3},{8,12},{9,13},{10,... | collective-permute-start | bytes 3145736 | tf_op jit(solution)/shard_map/ppermute | solution.py:253
  84.6 2.9 %copy-start.11 = (bf16[32,128,128]{2,1,0:T(8,128)(2,1)}, bf16[32,128,128]{2,1,0:T(8,128)(2,1)S(1)}, u32[]{:S(2)}) copy-start(bf16[32,128,128]{2,1,0:T(8,128)(2,1)S(1)} %collective-permute-done.5.refs_14_) | copy-start | bytes 3145732
  84.6 2.9 %collective-permute-start.2 = (bf16[32,128,128]{2,1,0:T(8,128)(2,1)}, bf16[32,128,128]{2,1,0:T(8,128)(2,1)S(1)}, u32[]{:S(2)}, u32[]{:S(2)}) collective-permute-start(bf16[32,128,128]{2,1,0:T(8,128)(2,1)} %collective-permute-done.1.refs_10_), channel_id=1, source_target_pairs={{0,4},{1,5},{2,6},{3,7},{4,0},{5,1},{6,2},{7,3},{8,12},{9,13},{10,... | collective-permute-start | bytes 3145736 | tf_op jit(solution)/shard_map/ppermute | solution.py:253
  84.6 2.9 %copy-start.12 = (bf16[32,128,128]{2,1,0:T(8,128)(2,1)}, bf16[32,128,128]{2,1,0:T(8,128)(2,1)S(1)}, u32[]{:S(2)}) copy-start(bf16[32,128,128]{2,1,0:T(8,128)(2,1)S(1)} %collective-permute-done.4.refs_13_) | copy-start | bytes 3145732
  87.5 1.0 copy-start.13
  87.5 1.4 copy-start.8
  88.9 1.0 copy-start.9
  92.7 17.9 %collective-permute-start.12 = (bf16[33,128,128]{2,1,0:T(8,128)(2,1)}, bf16[33,128,128]{2,1,0:T(8,128)(2,1)}, u32[]{:S(2)}, u32[]{:S(2)}) collective-permute-start(bf16[33,128,128]{2,1,0:T(8,128)(2,1)} %copy-done.9), channel_id=1, source_target_pairs={{0,4},{1,5},{2,6},{3,7},{4,0},{5,1},{6,2},{7,3},{8,12},{9,13},{10,... | collective-permute-start | bytes 3244040 | tf_op jit(solution)/shard_map/ppermute | solution.py:253
  92.7 55.6 %copy-start.21 = (s32[96,2]{0,1:T(2,128)S(1)}, s32[96,2]{0,1:T(2,128)}, u32[]{:S(2)}) copy-start(s32[96,2]{0,1:T(2,128)} %param.5) | copy-start | bytes 2308
  97.1 50.5 %collective-permute-start.19 = (bf16[32,128,128]{2,1,0:T(8,128)(2,1)}, bf16[32,128,128]{2,1,0:T(8,128)(2,1)}, u32[]{:S(2)}, u32[]{:S(2)}) collective-permute-start(bf16[32,128,128]{2,1,0:T(8,128)(2,1)} %get-tuple-element.107), channel_id=1, source_target_pairs={{0,24},{1,25},{2,26},{4,28},{5,29},{6,30},{8,16},{9,17},{11,19},{1... | collective-permute-start | bytes 3145736 | tf_op jit(solution)/shard_map/ppermute | solution.py:253
  102.4 45.2 %collective-permute-start.18 = (bf16[32,128,128]{2,1,0:T(8,128)(2,1)}, bf16[32,128,128]{2,1,0:T(8,128)(2,1)}, u32[]{:S(2)}, u32[]{:S(2)}) collective-permute-start(bf16[32,128,128]{2,1,0:T(8,128)(2,1)} %get-tuple-element.108), channel_id=1, source_target_pairs={{0,16},{1,17},{3,19},{4,20},{5,21},{7,23},{8,24},{9,25},{10,26},{1... | collective-permute-start | bytes 3145736 | tf_op jit(solution)/shard_map/ppermute | solution.py:253
  104.9 42.7 %collective-permute-start.17 = (bf16[32,128,128]{2,1,0:T(8,128)(2,1)}, bf16[32,128,128]{2,1,0:T(8,128)(2,1)S(1)}, u32[]{:S(2)}, u32[]{:S(2)}) collective-permute-start(bf16[32,128,128]{2,1,0:T(8,128)(2,1)} %get-tuple-element.109), channel_id=1, source_target_pairs={{0,8},{2,10},{3,11},{4,12},{6,14},{7,15},{9,1},{10,2},{11,3},{13,5... | collective-permute-start | bytes 3145736 | tf_op jit(solution)/shard_map/ppermute | solution.py:253
  106.3 41.4 %collective-permute-start.16 = (bf16[32,128,128]{2,1,0:T(8,128)(2,1)}, bf16[32,128,128]{2,1,0:T(8,128)(2,1)}, u32[]{:S(2)}, u32[]{:S(2)}) collective-permute-start(bf16[32,128,128]{2,1,0:T(8,128)(2,1)} %get-tuple-element.110), channel_id=1, source_target_pairs={{0,4},{1,5},{2,6},{3,7},{4,0},{5,1},{6,2},{7,3},{8,12},{9,13},{10,... | collective-permute-start | bytes 3145736 | tf_op jit(solution)/shard_map/ppermute | solution.py:253
  111.4 2.6 %collective-permute-start.15 = (bf16[8,16,2]{1,0,2:T(8,128)(2,1)S(1)}, bf16[8,16,2]{1,0,2:T(8,128)(2,1)S(1)}, u32[]{:S(2)}, u32[]{:S(2)}) collective-permute-start(bf16[8,16,2]{1,0,2:T(8,128)(2,1)S(1)} %dynamic-slice_bitcast_fusion.12), channel_id=1, source_target_pairs={{0,1},{4,5},{9,10},{13,14},{18,19},{22,23},{27,24},{31,28}} | collective-permute-start | bytes 1544 | tf_op jit(solution)/shard_map/ppermute | solution.py:253
  112.8 50.9 %copy-start = (s32[3]{0:T(128)}, s32[3]{0:T(128)S(1)}, u32[]{:S(2)}) copy-start(s32[3]{0:T(128)S(1)} %pad_add_fusion.place_ref) | copy-start | bytes 40
  114.0 2.6 %collective-permute-start.14 = (bf16[8,16,2]{1,0,2:T(8,128)(2,1)S(1)}, bf16[8,16,2]{1,0,2:T(8,128)(2,1)S(1)}, u32[]{:S(2)}, u32[]{:S(2)}) collective-permute-start(bf16[8,16,2]{1,0,2:T(8,128)(2,1)S(1)} %dynamic-slice_bitcast_fusion.12), channel_id=1, source_target_pairs={{0,2},{4,6},{9,11},{13,15},{18,16},{22,20},{27,25},{31,29}} | collective-permute-start | bytes 1544 | tf_op jit(solution)/shard_map/ppermute | solution.py:253
  116.6 2.6 %collective-permute-start.13 = (bf16[8,16,2]{1,0,2:T(8,128)(2,1)S(1)}, bf16[8,16,2]{1,0,2:T(8,128)(2,1)S(1)}, u32[]{:S(2)}, u32[]{:S(2)}) collective-permute-start(bf16[8,16,2]{1,0,2:T(8,128)(2,1)S(1)} %dynamic-slice_bitcast_fusion.12), channel_id=1, source_target_pairs={{0,3},{4,7},{9,8},{13,12},{18,17},{22,21},{27,26},{31,30}} | collective-permute-start | bytes 1544 | tf_op jit(solution)/shard_map/ppermute | solution.py:253
  119.2 38.3 %collective-permute-start.23 = (bf16[32,128,128]{2,1,0:T(8,128)(2,1)}, bf16[32,128,128]{2,1,0:T(8,128)(2,1)}, u32[]{:S(2)}, u32[]{:S(2)}) collective-permute-start(bf16[32,128,128]{2,1,0:T(8,128)(2,1)} %copy-done.11), channel_id=1, source_target_pairs={{0,4},{1,5},{2,6},{3,7},{4,0},{5,1},{6,2},{7,3},{8,12},{9,13},{10,... | collective-permute-start | bytes 3145736 | tf_op jit(solution)/shard_map/ppermute | solution.py:253
  147.7 13.2 %collective-permute-start.20 = (bf16[32,128,128]{2,1,0:T(8,128)(2,1)S(1)}, bf16[32,128,128]{2,1,0:T(8,128)(2,1)}, u32[]{:S(2)}, u32[]{:S(2)}) collective-permute-start(bf16[32,128,128]{2,1,0:T(8,128)(2,1)S(1)} %collective-permute-done.17.refs_1_), channel_id=1, source_target_pairs={{0,4},{1,5},{2,6},{3,7},{4,0},{5,1},{6,2},{7,3},{8,12},{9,13},{10,... | collective-permute-start | bytes 3145736 | tf_op jit(solution)/shard_map/ppermute | solution.py:253
  147.7 15.1 %collective-permute-start.21 = (bf16[32,128,128]{2,1,0:T(8,128)(2,1)}, bf16[32,128,128]{2,1,0:T(8,128)(2,1)}, u32[]{:S(2)}, u32[]{:S(2)}) collective-permute-start(bf16[32,128,128]{2,1,0:T(8,128)(2,1)} %collective-permute-done.18.refs_2_), channel_id=1, source_target_pairs={{0,4},{1,5},{2,6},{3,7},{4,0},{5,1},{6,2},{7,3},{8,12},{9,13},{10,... | collective-permute-start | bytes 3145736 | tf_op jit(solution)/shard_map/ppermute | solution.py:253
  149.0 14.7 %collective-permute-start.22 = (bf16[32,128,128]{2,1,0:T(8,128)(2,1)}, bf16[32,128,128]{2,1,0:T(8,128)(2,1)}, u32[]{:S(2)}, u32[]{:S(2)}) collective-permute-start(bf16[32,128,128]{2,1,0:T(8,128)(2,1)} %collective-permute-done.19.refs_3_), channel_id=1, source_target_pairs={{0,4},{1,5},{2,6},{3,7},{4,0},{5,1},{6,2},{7,3},{8,12},{9,13},{10,... | collective-permute-start | bytes 3145736 | tf_op jit(solution)/shard_map/ppermute | solution.py:253
  153.4 33.4 %collective-permute-start.25 = (bf16[20,128,128]{2,1,0:T(8,128)(2,1)}, bf16[20,128,128]{2,1,0:T(8,128)(2,1)S(1)}, u32[]{:S(2)}, u32[]{:S(2)}) collective-permute-start(bf16[20,128,128]{2,1,0:T(8,128)(2,1)} %get-tuple-element.88), channel_id=1, source_target_pairs={{0,8},{2,10},{3,11},{4,12},{6,14},{7,15},{9,1},{10,2},{11,3},{13,5... | collective-permute-start | bytes 1966088 | tf_op jit(solution)/shard_map/ppermute | solution.py:253
  157.5 32.0 %collective-permute-start.26 = (bf16[20,128,128]{2,1,0:T(8,128)(2,1)}, bf16[20,128,128]{2,1,0:T(8,128)(2,1)S(1)}, u32[]{:S(2)}, u32[]{:S(2)}) collective-permute-start(bf16[20,128,128]{2,1,0:T(8,128)(2,1)} %get-tuple-element.89), channel_id=1, source_target_pairs={{0,16},{1,17},{3,19},{4,20},{5,21},{7,23},{8,24},{9,25},{10,26},{1... | collective-permute-start | bytes 1966088 | tf_op jit(solution)/shard_map/ppermute | solution.py:253
  160.9 28.6 %collective-permute-start.27 = (bf16[20,128,128]{2,1,0:T(8,128)(2,1)}, bf16[20,128,128]{2,1,0:T(8,128)(2,1)S(1)}, u32[]{:S(2)}, u32[]{:S(2)}) collective-permute-start(bf16[20,128,128]{2,1,0:T(8,128)(2,1)} %get-tuple-element.90), channel_id=1, source_target_pairs={{0,24},{1,25},{2,26},{4,28},{5,29},{6,30},{8,16},{9,17},{11,19},{1... | collective-permute-start | bytes 1966088 | tf_op jit(solution)/shard_map/ppermute | solution.py:253
  162.8 26.7 %collective-permute-start.24 = (bf16[20,128,128]{2,1,0:T(8,128)(2,1)}, bf16[20,128,128]{2,1,0:T(8,128)(2,1)}, u32[]{:S(2)}, u32[]{:S(2)}) collective-permute-start(bf16[20,128,128]{2,1,0:T(8,128)(2,1)} %get-tuple-element.114), channel_id=1, source_target_pairs={{0,4},{1,5},{2,6},{3,7},{4,0},{5,1},{6,2},{7,3},{8,12},{9,13},{10,... | collective-permute-start | bytes 1966088 | tf_op jit(solution)/shard_map/ppermute | solution.py:253
  185.3 16.1 %copy-start.1 = (s32[3]{0:T(128)S(1)}, s32[3]{0:T(128)}, u32[]{:S(2)}) copy-start(s32[3]{0:T(128)} %copy-done) | copy-start | bytes 40
  189.5 7.4 %collective-permute-start.28 = (bf16[20,128,128]{2,1,0:T(8,128)(2,1)S(1)}, bf16[20,128,128]{2,1,0:T(8,128)(2,1)S(1)}, u32[]{:S(2)}, u32[]{:S(2)}) collective-permute-start(bf16[20,128,128]{2,1,0:T(8,128)(2,1)S(1)} %collective-permute-done.25.refs_1_), channel_id=1, source_target_pairs={{0,4},{1,5},{2,6},{3,7},{4,0},{5,1},{6,2},{7,3},{8,12},{9,13},{10,... | collective-permute-start | bytes 1966088 | tf_op jit(solution)/shard_map/ppermute | solution.py:253
  189.5 10.2 %collective-permute-start.29 = (bf16[20,128,128]{2,1,0:T(8,128)(2,1)S(1)}, bf16[20,128,128]{2,1,0:T(8,128)(2,1)S(1)}, u32[]{:S(2)}, u32[]{:S(2)}) collective-permute-start(bf16[20,128,128]{2,1,0:T(8,128)(2,1)S(1)} %collective-permute-done.26.refs_2_), channel_id=1, source_target_pairs={{0,4},{1,5},{2,6},{3,7},{4,0},{5,1},{6,2},{7,3},{8,12},{9,13},{10,... | collective-permute-start | bytes 1966088 | tf_op jit(solution)/shard_map/ppermute | solution.py:253
  190.0 9.8 %collective-permute-start.30 = (bf16[20,128,128]{2,1,0:T(8,128)(2,1)S(1)}, bf16[20,128,128]{2,1,0:T(8,128)(2,1)S(1)}, u32[]{:S(2)}, u32[]{:S(2)}) collective-permute-start(bf16[20,128,128]{2,1,0:T(8,128)(2,1)S(1)} %collective-permute-done.27.refs_3_), channel_id=1, source_target_pairs={{0,4},{1,5},{2,6},{3,7},{4,0},{5,1},{6,2},{7,3},{8,12},{9,13},{10,... | collective-permute-start | bytes 1966088 | tf_op jit(solution)/shard_map/ppermute | solution.py:253
  190.1 24.9 %collective-permute-start.32 = (bf16[12,128,128]{2,1,0:T(8,128)(2,1)S(1)}, bf16[12,128,128]{2,1,0:T(8,128)(2,1)S(1)}, u32[]{:S(2)}, u32[]{:S(2)}) collective-permute-start(bf16[12,128,128]{2,1,0:T(8,128)(2,1)S(1)} %get-tuple-element.99), channel_id=1, source_target_pairs={{0,8},{2,10},{3,11},{4,12},{6,14},{7,15},{9,1},{10,2},{11,3},{13,5... | collective-permute-start | bytes 1179656 | tf_op jit(solution)/shard_map/ppermute | solution.py:253
  193.2 21.8 %collective-permute-start.33 = (bf16[12,128,128]{2,1,0:T(8,128)(2,1)S(1)}, bf16[12,128,128]{2,1,0:T(8,128)(2,1)S(1)}, u32[]{:S(2)}, u32[]{:S(2)}) collective-permute-start(bf16[12,128,128]{2,1,0:T(8,128)(2,1)S(1)} %get-tuple-element.100), channel_id=1, source_target_pairs={{0,16},{1,17},{3,19},{4,20},{5,21},{7,23},{8,24},{9,25},{10,26},{1... | collective-permute-start | bytes 1179656 | tf_op jit(solution)/shard_map/ppermute | solution.py:253
  196.9 3.0 %copy-start.15 = (bf16[20,128,128]{2,1,0:T(8,128)(2,1)}, bf16[20,128,128]{2,1,0:T(8,128)(2,1)S(1)}, u32[]{:S(2)}) copy-start(bf16[20,128,128]{2,1,0:T(8,128)(2,1)S(1)} %collective-permute-done.28.refs_5_) | copy-start | bytes 1966084
  196.9 18.1 %collective-permute-start.34 = (bf16[12,128,128]{2,1,0:T(8,128)(2,1)S(1)}, bf16[12,128,128]{2,1,0:T(8,128)(2,1)S(1)}, u32[]{:S(2)}, u32[]{:S(2)}) collective-permute-start(bf16[12,128,128]{2,1,0:T(8,128)(2,1)S(1)} %get-tuple-element.101), channel_id=1, source_target_pairs={{0,24},{1,25},{2,26},{4,28},{5,29},{6,30},{8,16},{9,17},{11,19},{1... | collective-permute-start | bytes 1179656 | tf_op jit(solution)/shard_map/ppermute | solution.py:253
  199.7 0.9 copy-start.16
  199.7 19.1 %copy-start.2 = (s32[508]{0:T(512)S(1)}, s32[508]{0:T(512)}, u32[]{:S(2)}) copy-start(s32[508]{0:T(512)} %shard_map.38.plan_ref) | copy-start | bytes 6100
  199.7 15.2 %collective-permute-start.31 = (bf16[12,128,128]{2,1,0:T(8,128)(2,1)S(1)}, bf16[12,128,128]{2,1,0:T(8,128)(2,1)S(1)}, u32[]{:S(2)}, u32[]{:S(2)}) collective-permute-start(bf16[12,128,128]{2,1,0:T(8,128)(2,1)S(1)} %get-tuple-element.115), channel_id=1, source_target_pairs={{0,4},{1,5},{2,6},{3,7},{4,0},{5,1},{6,2},{7,3},{8,12},{9,13},{10,... | collective-permute-start | bytes 1179656 | tf_op jit(solution)/shard_map/ppermute | solution.py:253
  200.6 0.8 copy-start.17
  215.0 1.8 collective-permute-start.35
  215.1 2.3 collective-permute-start.36
  215.6 2.3 %collective-permute-start.37 = (bf16[12,128,128]{2,1,0:T(8,128)(2,1)S(1)}, bf16[12,128,128]{2,1,0:T(8,128)(2,1)S(1)}, u32[]{:S(2)}, u32[]{:S(2)}) collective-permute-start(bf16[12,128,128]{2,1,0:T(8,128)(2,1)S(1)} %collective-permute-done.34.refs_3_), channel_id=1, source_target_pairs={{0,4},{1,5},{2,6},{3,7},{4,0},{5,1},{6,2},{7,3},{8,12},{9,13},{10,... | collective-permute-start | bytes 1179656 | tf_op jit(solution)/shard_map/ppermute | solution.py:253
  217.3 0.8 copy-start.18
  218.1 0.7 copy-start.19
Sparse Core Ops, SparseCore 0:
  9.2 83.4 all-gather.6
  94.2 53.3 all-gather.8
  149.2 36.0 all-gather.10
